TPU v7x, 32 devices: a whole 2x2x4 slice. The times are simulated.
32 devices in a mesh: grp: 4 (over y, x), shard: 8 (over z, core).
Axes of the slice: x: 2, y: 2, z: 4, core: 2. Of those that a mesh axis runs over, the one named last changes fastest.
Arguments:
- points: bfloat16 [4, 12288, 1024], P('grp', 'shard'), may hold values from -6 to 6
- centroids: bfloat16 [4, 1024, 1024], P('grp', 'shard'), may hold values from -1.5 to 1.5
- tile_counts: int32 [4], replicated, may hold values from 49 to 96, as said below
Outputs:
- new_centroids: float32 [4, 1024, 1024], P('grp', 'shard')
- posterior_rows: bfloat16 [4, 12288, 1024], P('grp', 'shard')
Inputs may be any that keep to these rules, and one draw needn't show every extreme that they name: `tile_counts`: every coarse cluster has more than half of its 96 tile slots live, and some cluster has all 96.
All inputs are finite; a program needn't handle non-finite values.
Results may differ from a plain program's by a relative error of at most 0.0076.
Values may be sent and summed in bfloat16 or wider, within the bound.
No kernel may reach another device: no remote copies, remote signals or barrier semaphores. Data moves between devices by JAX's collectives and lax.ppermute only.
A program may use at most 64 MiB of HBM per device.

v0:
```python
import jax
import jax.numpy as jnp
from jax import lax
from jax.sharding import PartitionSpec as P

TILE = 128
ITERS = 2


sharpness_factor = 48.0
epsilon = 1e-06


def rms_unit(values):
    return values * lax.rsqrt(jnp.mean(values * values, axis=-1, keepdims=True) + epsilon)


def pick_entry(lookup_table, wanted):
    positions = jnp.arange(lookup_table.shape[0], dtype=jnp.int32)
    return jnp.sum(jnp.where(positions == wanted, lookup_table, 0))


def held_tiles(tile_total, shard_place, shard_count, slot_count):
    return jnp.clip((tile_total - shard_place + shard_count - 1) // shard_count, 0, slot_count)


def tile_weights(rows_per_tile, centroid_table):
    affinity_scores = lax.dot_general(
        rows_per_tile, centroid_table, (((1,), (1,)), ((), ())), preferred_element_type=jnp.float32
    ) * (sharpness_factor / rows_per_tile.shape[-1])
    exponent_terms = jnp.exp(affinity_scores)
    return (exponent_terms / jnp.sum(exponent_terms, axis=-1, keepdims=True)).astype(jnp.bfloat16)


def sweep(tile_stack, tile_limit, centroid_table, with_rows):
    centroid_count = centroid_table.shape[0]
    zero_sums = jnp.zeros((centroid_count, tile_stack.shape[2]), jnp.float32)
    zero_rows = jnp.zeros(tile_stack.shape, jnp.bfloat16)

    def visit(position, state_pair):
        running_sums, mean_rows = state_pair
        rows_per_tile = lax.dynamic_index_in_dim(tile_stack, position, 0, keepdims=False)
        weights = tile_weights(rows_per_tile, centroid_table)
        running_sums = running_sums + lax.dot_general(
            weights, rows_per_tile, (((0,), (0,)), ((), ())), preferred_element_type=jnp.float32
        )
        if with_rows:
            blended = jnp.dot(weights, centroid_table, preferred_element_type=jnp.float32).astype(
                jnp.bfloat16
            )
            mean_rows = lax.dynamic_update_index_in_dim(mean_rows, blended, position, 0)
        return (running_sums, mean_rows)

    return lax.fori_loop(0, tile_limit, visit, (zero_sums, zero_rows))


def body(points, centroids, tile_counts):
    slot_count = points.shape[1] // TILE
    feature_width = points.shape[2]
    shard_count = lax.axis_size("shard")
    shard_place = lax.axis_index("shard")
    group_index = lax.axis_index("grp")
    unit_embeddings = rms_unit(points[0].astype(jnp.float32)).astype(jnp.bfloat16)
    tile_stack = unit_embeddings.reshape(slot_count, TILE, feature_width)
    own_held = held_tiles(
        pick_entry(tile_counts, group_index), shard_place, shard_count, slot_count
    )
    current_shard = centroids[0]
    updated = None
    out_rows = None
    for iteration in range(ITERS):
        is_last = iteration == ITERS - 1
        centroid_table = lax.all_gather(current_shard, "shard", axis=0, tiled=True)
        own_total, out_rows = sweep(tile_stack, own_held, centroid_table, is_last)
        own_reduced = lax.psum_scatter(own_total, "shard", scatter_dimension=0, tiled=True)
        updated = rms_unit(own_reduced)
        current_shard = updated.astype(jnp.bfloat16)
    return (updated[None], out_rows.reshape(1, slot_count * TILE, feature_width))


def solution(mesh):
    return jax.shard_map(
        body,
        mesh=mesh,
        in_specs=(P("grp", "shard", None), P("grp", "shard", None), P()),
        out_specs=(P("grp", "shard", None), P("grp", "shard", None)),
        check_vma=False,
    )
```

profile of v0, /device:TPU:0, one launch (start us, length us, event | category | flops | bytes accessed | tf_op | source)
XLA Modules:
  0.0 355.1 jit_solution(12290640170524231585)
XLA Ops:
  8.0 1.4 fusion.17
  10.1 2.6 multiply_reduce_fusion
  12.7 2.3 multiply_convert_fusion
  14.9 26.5 %all-gather.6.cloned.1.call-done = bf16[1,1024,1024]{2,1,0:T(8,128)(2,1)} async-done(((bf16[1,128,1024]{2,1,0:T(8,128)(2,1)}), bf16[1,1024,1024]{2,1,0:T(8,128)(2,1)}) %all-gather.6.cloned.1.call-update) | async-done | bytes 2097168 | tf_op jit(solution)/shard_map/all_gather | solution.py:73
  41.4 2.5 broadcast.57.clone
  43.9 62.1 %while.22 = (s32[]{:T(128)}, f32[1024,1024]{1,0:T(8,128)}, s32[]{:T(128)}, bf16[12,128,1024]{2,1,0:T(8,128)(2,1)}, bf16[1024,1024]{1,0:T(8,128)(2,1)S(1)}, /*index=5*/s32[]{:T(128)}, s32[]{:T(128)}, s32[]{:T(128)}) while((s32[]{:T(128)}, f32[1024,1024]{1,0:T(8,128)}, s32[]{:T(128)}, bf16[12,128,1024]{2,1,0:T(8,128)(2,1)}, ...), condition=%wide.region_4.5_spmd, body=%wide.region_2.4_spmd.sunk | while | flops 538443648 | bytes 12059783 | solution.py:54
  43.9 1.9 fusion.33
  45.8 5.0 %convolution_add_fusion.4 = f32[1024,1024]{1,0:T(8,128)} fusion(f32[1024,1024]{1,0:T(8,128)} %get-tuple-element.180, f32[128,1024]{1,0:T(8,128)S(1)} %get-tuple-element.161, f32[128]{0:T(128)S(1)} %get-tuple-element.162, bf16[12,128,1024]{2,1,0:T(8,128)(2,1)} %get-tuple-element.190, s32[]{:T(128)S(6)} %select_n.25), kind=kOutput, calls=%fused_computation.clone.1 | convolution fusion | flops 269746176 | bytes 9175556 | tf_op jit(solution)/shard_map/while/body/dot_general | solution.py:44
  50.8 1.9 fusion.33
  52.7 5.0 %convolution_add_fusion.4 = f32[1024,1024]{1,0:T(8,128)} fusion(f32[1024,1024]{1,0:T(8,128)} %get-tuple-element.180, f32[128,1024]{1,0:T(8,128)S(1)} %get-tuple-element.161, f32[128]{0:T(128)S(1)} %get-tuple-element.162, bf16[12,128,1024]{2,1,0:T(8,128)(2,1)} %get-tuple-element.190, s32[]{:T(128)S(6)} %select_n.25), kind=kOutput, calls=%fused_computation.clone.1 | convolution fusion | flops 269746176 | bytes 9175556 | tf_op jit(solution)/shard_map/while/body/dot_general | solution.py:44
  57.7 1.9 fusion.33
  59.6 5.0 %convolution_add_fusion.4 = f32[1024,1024]{1,0:T(8,128)} fusion(f32[1024,1024]{1,0:T(8,128)} %get-tuple-element.180, f32[128,1024]{1,0:T(8,128)S(1)} %get-tuple-element.161, f32[128]{0:T(128)S(1)} %get-tuple-element.162, bf16[12,128,1024]{2,1,0:T(8,128)(2,1)} %get-tuple-element.190, s32[]{:T(128)S(6)} %select_n.25), kind=kOutput, calls=%fused_computation.clone.1 | convolution fusion | flops 269746176 | bytes 9175556 | tf_op jit(solution)/shard_map/while/body/dot_general | solution.py:44
  64.6 1.9 fusion.33
  66.5 5.0 %convolution_add_fusion.4 = f32[1024,1024]{1,0:T(8,128)} fusion(f32[1024,1024]{1,0:T(8,128)} %get-tuple-element.180, f32[128,1024]{1,0:T(8,128)S(1)} %get-tuple-element.161, f32[128]{0:T(128)S(1)} %get-tuple-element.162, bf16[12,128,1024]{2,1,0:T(8,128)(2,1)} %get-tuple-element.190, s32[]{:T(128)S(6)} %select_n.25), kind=kOutput, calls=%fused_computation.clone.1 | convolution fusion | flops 269746176 | bytes 9175556 | tf_op jit(solution)/shard_map/while/body/dot_general | solution.py:44
  71.5 1.9 fusion.33
  73.4 5.0 %convolution_add_fusion.4 = f32[1024,1024]{1,0:T(8,128)} fusion(f32[1024,1024]{1,0:T(8,128)} %get-tuple-element.180, f32[128,1024]{1,0:T(8,128)S(1)} %get-tuple-element.161, f32[128]{0:T(128)S(1)} %get-tuple-element.162, bf16[12,128,1024]{2,1,0:T(8,128)(2,1)} %get-tuple-element.190, s32[]{:T(128)S(6)} %select_n.25), kind=kOutput, calls=%fused_computation.clone.1 | convolution fusion | flops 269746176 | bytes 9175556 | tf_op jit(solution)/shard_map/while/body/dot_general | solution.py:44
  78.4 1.9 fusion.33
  80.3 5.0 %convolution_add_fusion.4 = f32[1024,1024]{1,0:T(8,128)} fusion(f32[1024,1024]{1,0:T(8,128)} %get-tuple-element.180, f32[128,1024]{1,0:T(8,128)S(1)} %get-tuple-element.161, f32[128]{0:T(128)S(1)} %get-tuple-element.162, bf16[12,128,1024]{2,1,0:T(8,128)(2,1)} %get-tuple-element.190, s32[]{:T(128)S(6)} %select_n.25), kind=kOutput, calls=%fused_computation.clone.1 | convolution fusion | flops 269746176 | bytes 9175556 | tf_op jit(solution)/shard_map/while/body/dot_general | solution.py:44
  85.3 1.9 fusion.33
  87.2 5.0 %convolution_add_fusion.4 = f32[1024,1024]{1,0:T(8,128)} fusion(f32[1024,1024]{1,0:T(8,128)} %get-tuple-element.180, f32[128,1024]{1,0:T(8,128)S(1)} %get-tuple-element.161, f32[128]{0:T(128)S(1)} %get-tuple-element.162, bf16[12,128,1024]{2,1,0:T(8,128)(2,1)} %get-tuple-element.190, s32[]{:T(128)S(6)} %select_n.25), kind=kOutput, calls=%fused_computation.clone.1 | convolution fusion | flops 269746176 | bytes 9175556 | tf_op jit(solution)/shard_map/while/body/dot_general | solution.py:44
  92.2 1.9 fusion.33
  94.1 5.0 %convolution_add_fusion.4 = f32[1024,1024]{1,0:T(8,128)} fusion(f32[1024,1024]{1,0:T(8,128)} %get-tuple-element.180, f32[128,1024]{1,0:T(8,128)S(1)} %get-tuple-element.161, f32[128]{0:T(128)S(1)} %get-tuple-element.162, bf16[12,128,1024]{2,1,0:T(8,128)(2,1)} %get-tuple-element.190, s32[]{:T(128)S(6)} %select_n.25), kind=kOutput, calls=%fused_computation.clone.1 | convolution fusion | flops 269746176 | bytes 9175556 | tf_op jit(solution)/shard_map/while/body/dot_general | solution.py:44
  99.1 1.9 fusion.33
  100.9 5.0 %convolution_add_fusion.4 = f32[1024,1024]{1,0:T(8,128)} fusion(f32[1024,1024]{1,0:T(8,128)} %get-tuple-element.180, f32[128,1024]{1,0:T(8,128)S(1)} %get-tuple-element.161, f32[128]{0:T(128)S(1)} %get-tuple-element.162, bf16[12,128,1024]{2,1,0:T(8,128)(2,1)} %get-tuple-element.190, s32[]{:T(128)S(6)} %select_n.25), kind=kOutput, calls=%fused_computation.clone.1 | convolution fusion | flops 269746176 | bytes 9175556 | tf_op jit(solution)/shard_map/while/body/dot_general | solution.py:44
  106.0 70.3 %reduce-scatter.3.cloned.1.call-done = f32[128,1024]{1,0:T(8,128)} async-done(((f32[1024,1024]{1,0:T(8,128)}), f32[128,1024]{1,0:T(8,128)}) %reduce-scatter.3.cloned.1.call-update) | async-done | bytes 524304 | tf_op jit(solution)/shard_map/reduce_scatter | solution.py:75
  177.5 1.8 multiply_convert_fusion.1
  179.4 27.4 %all-gather.4.cloned.1.call-done = bf16[1024,1024]{1,0:T(8,128)(2,1)} async-done(((bf16[128,1024]{1,0:T(8,128)(2,1)}), bf16[1024,1024]{1,0:T(8,128)(2,1)}) %all-gather.4.cloned.1.call-update) | async-done | bytes 2097168 | tf_op jit(solution)/shard_map/all_gather | solution.py:73
  206.8 2.1 broadcast_in_dim.19
  208.9 2.5 broadcast.57
  211.3 63.4 %while.23 = (s32[]{:T(128)}, f32[1024,1024]{1,0:T(8,128)}, bf16[12,128,1024]{2,1,0:T(8,128)(2,1)}, s32[]{:T(128)}, bf16[12,128,1024]{2,1,0:T(8,128)(2,1)}, /*ind...) while((s32[]{:T(128)}, f32[1024,1024]{1,0:T(8,128)}, bf16[12,128,1024]{2,1,0:T(8,128)(2,1)}, ...), condition=%wide.region_9.10_spmd, body=%wide.region_7.9_spmd.sunk | while | flops 807272320 | bytes 48498376 | solution.py:54
  211.3 2.0 fusion.37
  214.6 1.9 convolution_add_fusion.5
  216.4 1.9 copy-done.1
  218.4 2.0 fusion.37
  220.4 1.2 fusion.38
  221.6 1.9 convolution_add_fusion.5
  223.5 1.9 copy-done.1
  225.4 2.0 fusion.37
  227.4 1.2 fusion.38
  228.6 1.9 convolution_add_fusion.5
  230.5 1.9 copy-done.1
  232.4 2.0 fusion.37
  234.5 1.2 fusion.38
  235.7 1.9 convolution_add_fusion.5
  237.6 1.9 copy-done.1
  239.5 2.0 fusion.37
  241.5 1.2 fusion.38
  242.7 1.9 convolution_add_fusion.5
  244.6 1.9 copy-done.1
  246.5 2.0 fusion.37
  248.5 1.2 fusion.38
  249.8 1.9 convolution_add_fusion.5
  251.6 1.9 copy-done.1
  253.6 2.0 fusion.37
  256.8 1.9 convolution_add_fusion.5
  258.7 1.9 copy-done.1
  260.6 2.0 fusion.37
  263.8 1.9 convolution_add_fusion.5
  265.7 1.9 copy-done.1
  267.6 2.0 fusion.37
  270.9 1.9 convolution_add_fusion.5
  272.8 1.9 copy-done.1
  274.7 70.8 %reduce-scatter.5.cloned.1.call-done = f32[128,1024]{1,0:T(8,128)} async-done(((f32[1024,1024]{1,0:T(8,128)}), f32[128,1024]{1,0:T(8,128)}) %reduce-scatter.5.cloned.1.call-update) | async-done | bytes 524304 | tf_op jit(solution)/shard_map/reduce_scatter | solution.py:75
  346.6 1.9 multiply_bitcast_fusion
  (50 shorter events, 8.2 us)
Async XLA Ops:
  7.2 5.5 %copy-start.4 = (bf16[1,1536,1024]{2,1,0:T(8,128)(2,1)S(1)}, bf16[1,1536,1024]{2,1,0:T(8,128)(2,1)}, u32[]{:S(2)}) copy-start(bf16[1,1536,1024]{2,1,0:T(8,128)(2,1)} %param.7) | copy-start | bytes 9437188
  7.2 34.3 %all-gather.6.cloned.1.call-start = ((), (), s32[]{:S(2)}) async-start(), calls=%async_computation.5 | async-start | bytes 2359296 | tf_op jit(solution)/shard_map/all_gather | solution.py:73
  7.9 168.4 %reduce-scatter.3.cloned.1.call-start = ((), (), s32[]{:S(2)}) async-start(), calls=%async_computation.2 | async-start | bytes 4718592 | tf_op jit(solution)/shard_map/reduce_scatter | solution.py:75
  41.4 2.5 copy-start.2
  106.0 100.8 %all-gather.4.cloned.1.call-start = ((), (), s32[]{:S(2)}) async-start(), calls=%async_computation.3 | async-start | bytes 2359296 | tf_op jit(solution)/shard_map/all_gather | solution.py:73
  179.4 166.1 %reduce-scatter.5.cloned.1.call-start = ((), (), s32[]{:S(2)}) async-start(), calls=%async_computation.4 | async-start | bytes 4718592 | tf_op jit(solution)/shard_map/reduce_scatter | solution.py:75
  206.8 4.5 %copy-start.3 = (bf16[1024,1024]{1,0:T(8,128)(2,1)S(1)}, bf16[1024,1024]{1,0:T(8,128)(2,1)}, u32[]{:S(2)}) copy-start(bf16[1024,1024]{1,0:T(8,128)(2,1)} %all-gather.4.cloned.1.call-done) | copy-start | bytes 6291460
  211.3 3.2 copy-start
  216.4 1.9 copy-start.1
  218.4 3.2 copy-start
  223.5 1.9 copy-start.1
  225.4 3.2 copy-start
  230.5 1.9 copy-start.1
  232.4 3.2 copy-start
  237.6 1.9 copy-start.1
  239.5 3.2 copy-start
  244.6 1.9 copy-start.1
  246.5 3.2 copy-start
  251.6 1.9 copy-start.1
  253.6 3.2 copy-start
  258.7 1.9 copy-start.1
  260.6 3.2 copy-start
  265.7 1.9 copy-start.1
  267.6 3.2 copy-start
  272.8 1.9 copy-start.1
Sparse Core Ops, SparseCore 0:
  9.6 31.7 all-gather.5
  106.1 70.1 reduce-scatter.2
  179.5 27.2 all-gather.3
  274.8 70.6 reduce-scatter.4
where the time goes:
time: 356 us; the launch traced here: 355 us
  waiting for transfers between devices  196 us (55%)
  matrix products  108 us (30%)
  local copies, waits for them, and re-layouts  24.3 us (7%)
  between operations  14.5 us (4%)
  other arithmetic  12.4 us (3%)
    reduce_scatter x2, waiting for transfers between devices, body(): lax.psum_scatter(own_total, 'shard', scatter_dimension=0, tiled=True)  141 us
    dot_general x18, matrix products, visit(): lax.dot_general(weights, rows_per_tile, (((0,), (0,)), ((), ())), preferr...  62 us
    all_gather x2, waiting for transfers between devices, body(): centroid_table = lax.all_gather(current_shard, 'shard', axis=0, tiled=True)  53.9 us
    dot_general x18, matrix products, tile_weights(): lax.dot_general(rows_per_tile, centroid_table, (((1,), (1,)), ((), ())),...  35.1 us
    while x36, local copies, waits for them, and re-layouts  17.3 us
    dot_general x9, matrix products, visit(): jnp.dot(weights, centroid_table, preferred_element_type=jnp.float32)  10.9 us
  transfers between devices with their start and end apart: 4, of which 4 were waited for; matrix products, arithmetic and copies ran while one was open for 2% of the time, Pallas kernels for 0%

commit v1 on v0

v1 whole, which is shorter than its diff:
```python
import jax
import jax.numpy as jnp
from jax import lax
from jax.sharding import PartitionSpec as P

TILE = 128
ITERS = 2


sharpness_factor = 48.0
epsilon = 1e-06


def rms_unit(values):
    return values * lax.rsqrt(jnp.mean(values * values, axis=-1, keepdims=True) + epsilon)


def pick_entry(lookup_table, wanted):
    positions = jnp.arange(lookup_table.shape[0], dtype=jnp.int32)
    return jnp.sum(jnp.where(positions == wanted, lookup_table, 0))


def held_tiles(tile_total, shard_place, shard_count, slot_count):
    return jnp.clip((tile_total - shard_place + shard_count - 1) // shard_count, 0, slot_count)


def swap(values, offset):
    places = lax.axis_size("shard")
    return lax.ppermute(values, "shard", [(place, place ^ offset) for place in range(places)])


def low_bit(number):
    return number & -number


def gather_blocks(own, chips):
    held = {0: own}
    bits = [1 << b for b in range(chips.bit_length() - 1)]
    for bit in reversed(bits):
        for j in sorted(held):
            if j ^ bit not in held:
                held[j ^ bit] = swap(held[j], 2 * bit)
    return {j: (rows, swap(rows, 1)) for j, rows in held.items()}


def scatter_blocks(own_parts, other_parts, chips):
    totals = {}
    for j in sorted(own_parts, reverse=True):
        totals[j] = own_parts[j] + swap(other_parts[j].astype(jnp.bfloat16), 1).astype(jnp.float32)
    for j in sorted(totals, key=lambda j: (low_bit(j), -j)):
        if j:
            got = swap(totals[j].astype(jnp.bfloat16), 2 * low_bit(j))
            totals[j ^ low_bit(j)] = totals[j ^ low_bit(j)] + got.astype(jnp.float32)
    return totals[0]


def body(points, centroids, tile_counts):
    slot_count = points.shape[1] // TILE
    feature_width = points.shape[2]
    shard_count = lax.axis_size("shard")
    shard_place = lax.axis_index("shard")
    group_index = lax.axis_index("grp")
    chips = shard_count // 2
    unit = rms_unit(points[0].astype(jnp.float32)).astype(jnp.bfloat16)
    own_held = held_tiles(
        pick_entry(tile_counts, group_index), shard_place, shard_count, slot_count
    )
    live = (jnp.arange(slot_count * TILE) // TILE < own_held).astype(jnp.float32)
    current = centroids[0]
    count = current.shape[0]
    for iteration in range(ITERS):
        blocks = gather_blocks(current, chips)
        tables = {j: jnp.concatenate(blocks[j]) for j in blocks}
        terms = {}
        normal = 0.0
        for j in sorted(tables):
            scores = lax.dot_general(
                tables[j], unit, (((1,), (1,)), ((), ())), preferred_element_type=jnp.float32
            ) * (sharpness_factor / feature_width)
            terms[j] = jnp.exp(scores).astype(jnp.bfloat16)
            normal = normal + jnp.sum(terms[j].astype(jnp.float32), axis=0)
        factor = live / normal
        weights = {j: (terms[j].astype(jnp.float32) * factor).astype(jnp.bfloat16) for j in terms}
        sums = {j: jnp.dot(weights[j], unit, preferred_element_type=jnp.float32) for j in weights}
        reduced = scatter_blocks(
            {j: sums[j][:count] for j in sums}, {j: sums[j][count:] for j in sums}, chips
        )
        if iteration == ITERS - 1:
            out_rows = sum(
                lax.dot_general(
                    weights[j], tables[j], (((0,), (0,)), ((), ())), preferred_element_type=jnp.float32
                )
                for j in sorted(tables)
            ).astype(jnp.bfloat16)
        updated = rms_unit(reduced)
        current = updated.astype(jnp.bfloat16)
    return (updated[None], out_rows[None])


def solution(mesh):
    return jax.shard_map(
        body,
        mesh=mesh,
        in_specs=(P("grp", "shard", None), P("grp", "shard", None), P()),
        out_specs=(P("grp", "shard", None), P("grp", "shard", None)),
        check_vma=False,
    )
```

time: 356 us -> 115 us (0.32)
  waiting for transfers between devices: 196 us -> 46.4 us
  matrix products: 108 us -> 25.2 us
  starting transfers between devices: 0.16 us -> 34 us
  local copies, waits for them, and re-layouts: 24.3 us -> 1.22 us
  between operations: 14.5 us -> 1.84 us
  other arithmetic: 12.4 us -> 5.76 us
    reduce_scatter x2 -> x0, waiting for transfers between devices: 141 us -> none  [body(): lax.psum_scatter(own_total, 'shard', scatter_dimension=0, tiled=True)]
    dot_general x45 -> x20, matrix products: 108 us -> 25.2 us  [the longest x8 11.5 us: body(): lax.dot_general(tables[j], unit, (((1,), (1,)), ((), ())), preferred_elem...]
    all_gather x2 -> x0, waiting for transfers between devices: 53.9 us -> none  [body(): centroid_table = lax.all_gather(current_shard, 'shard', axis=0, tiled=True)]
    ppermute x0 -> x28, waiting for transfers between devices: none -> 46.4 us  [swap(): lax.ppermute(values, 'shard', [(place, place ^ offset) for place in range...]
    ppermute x0 -> x28, starting transfers between devices: none -> 34 us  [swap(): lax.ppermute(values, 'shard', [(place, place ^ offset) for place in range...]
    while x36 -> x0, local copies, waits for them, and re-layouts: 17.3 us -> none
    another operation x2 -> x0, local copies, waits for them, and re-layouts: 4.9 us -> none
  transfers between devices with their start and end apart: 4 -> 28, of which waited for: 4 -> 11; matrix products, arithmetic and copies ran while one was open for 2% -> 20% of each run, Pallas kernels for 0% -> 0%
where the time goes in v1:
time: 115 us; the launch traced here: 114 us
  waiting for transfers between devices  46.4 us (40%)
  starting transfers between devices  34 us (30%)
  matrix products  25.2 us (22%)
  other arithmetic  5.76 us (5%)
  between operations  1.84 us (2%)
  local copies, waits for them, and re-layouts  1.22 us (1%)
    ppermute x28, waiting for transfers between devices, swap(): lax.ppermute(values, 'shard', [(place, place ^ offset) for place in range...  46.4 us
    ppermute x28, starting transfers between devices, swap(): lax.ppermute(values, 'shard', [(place, place ^ offset) for place in range...  34 us
    dot_general x8, matrix products, body(): lax.dot_general(tables[j], unit, (((1,), (1,)), ((), ())), preferred_elem...  11.5 us
    dot_general x8, matrix products, body(): jnp.dot(weights[j], unit, preferred_element_type=jnp.float32)  7.88 us
    dot_general x4, matrix products, body(): lax.dot_general(weights[j], tables[j], (((0,), (0,)), ((), ())), preferre...  5.84 us
    reduce_sum x3, other arithmetic, rms_unit(): jnp.mean(values * values, axis=-1, keepdims=True) + epsilon  3.01 us
  transfers between devices with their start and end apart: 28, of which 11 were waited for; matrix products, arithmetic and copies ran while one was open for 20% of the time, Pallas kernels for 0%

profile of v1, /device:TPU:0, one launch (start us, length us, event | category | flops | bytes accessed | tf_op | source)
XLA Modules:
  0.0 114.4 jit_solution(4515507460830353677)
XLA Ops:
  0.6 4.1 %collective-permute-start.3 = (bf16[128,1024]{1,0:T(8,128)(2,1)}, bf16[128,1024]{1,0:T(8,128)(2,1)}, u32[]{:S(2)}, u32[]{:S(2)}) collective-permute-start(bf16[128,1024]{1,0:T(8,128)(2,1)} %bitcast.31), channel_id=1, source_target_pairs={{0,4},{1,5},{2,6},{3,7},{4,0},{5,1},{6,2},{7,3},{8,12},{9,13},{10,... | collective-permute-start | bytes 786440 | tf_op jit(solution)/shard_map/ppermute | solution.py:29
  4.7 1.6 %collective-permute-start.1 = (bf16[128,1024]{1,0:T(8,128)(2,1)}, bf16[128,1024]{1,0:T(8,128)(2,1)}, u32[]{:S(2)}, u32[]{:S(2)}) collective-permute-start(bf16[128,1024]{1,0:T(8,128)(2,1)} %bitcast.32), channel_id=1, source_target_pairs={{0,2},{1,3},{2,0},{3,1},{4,6},{5,7},{6,4},{7,5},{8,10},{9,11},{10,... | collective-permute-start | bytes 786440 | tf_op jit(solution)/shard_map/ppermute | solution.py:29
  6.3 2.6 %fusion = f32[1536]{0:T(1024)S(1)} fusion(bf16[1,1536,1024]{2,1,0:T(8,128)(2,1)} %param.3), kind=kLoop, calls=%fused_computation.2 | loop fusion | flops 4717056 | bytes 3151872 | tf_op jit(solution)/shard_map/reduce_sum | solution.py:15
  8.9 0.6 fusion.1
  9.6 0.6 fusion.70
  10.9 6.2 %collective-permute-done.3 = bf16[128,1024]{1,0:T(8,128)(2,1)} collective-permute-done((bf16[128,1024]{1,0:T(8,128)(2,1)}, bf16[128,1024]{1,0:T(8,128)(2,1)}, u32[]{:S(2)}, u32[]{:S(2)}) %collective-permute-start.3) | collective-permute-done | bytes 262176 | tf_op jit(solution)/shard_map/ppermute | solution.py:29
  17.1 0.6 collective-permute-start.5
  17.7 0.5 collective-permute-start.2
  18.2 2.0 %fusion.79 = (f32[1536]{0:T(1024)S(1)}, f32[256,1536]{1,0:T(8,128)S(1)}) fusion(bf16[1536,1024]{1,0:T(8,128)(2,1)S(1)} %fusion.1, bf16[128,1024]{1,0:T(8,128)(2,1)} %collective-permute-done, bf16[128,1024]{1,0:T(8,128)(2,1)S(1)} %bitcast.34), kind=kOutput, calls=%fused_computation.135 | convolution fusion | flops 807926272 | bytes 5249024 | tf_op jit(solution)/shard_map/dot_general | solution.py:77
  20.2 4.5 %collective-permute-done.5 = bf16[128,1024]{1,0:T(8,128)(2,1)S(1)} collective-permute-done((bf16[128,1024]{1,0:T(8,128)(2,1)}, bf16[128,1024]{1,0:T(8,128)(2,1)S(1)}, u32[]{:S(2)}, u32[]{:S(2)}) %collective-permute-start.5) | collective-permute-done | bytes 262176 | tf_op jit(solution)/shard_map/ppermute | solution.py:29
  24.7 2.0 %fusion.78 = (f32[1536]{0:T(1024)S(1)}, f32[256,1536]{1,0:T(8,128)S(1)}) fusion(bf16[1536,1024]{1,0:T(8,128)(2,1)S(1)} %fusion.1, bf16[128,1024]{1,0:T(8,128)(2,1)S(1)} %collective-permute-done.4, bf16[128,1024]{1,0:T(8,128)(2,1)} %collective-permute-done.3), kind=kOutput, calls=%fused_computation.134 | convolution fusion | flops 807926272 | bytes 5249024 | tf_op jit(solution)/shard_map/dot_general | solution.py:77
  26.8 2.0 %fusion.80 = (f32[1536]{0:T(1024)S(1)}, f32[256,1536]{1,0:T(8,128)S(1)}) fusion(bf16[1536,1024]{1,0:T(8,128)(2,1)S(1)} %fusion.1, bf16[128,1024]{1,0:T(8,128)(2,1)S(1)} %collective-permute-done.2, bf16[128,1024]{1,0:T(8,128)(2,1)} %collective-permute-done.1), kind=kOutput, calls=%fused_computation.136 | convolution fusion | flops 807926272 | bytes 5249024 | tf_op jit(solution)/shard_map/dot_general | solution.py:77
  28.8 1.1 fusion.77
  29.9 1.0 fusion.29
  30.9 1.0 fusion.30
  32.0 0.6 collective-permute-start.11
  32.5 1.0 fusion.28
  33.6 0.1 collective-permute-start.8
  33.7 0.5 collective-permute-start.10
  34.2 1.5 %collective-permute-start.12 = (bf16[128,1024]{1,0:T(8,128)(2,1)S(1)}, bf16[128,1024]{1,0:T(8,128)(2,1)S(1)}, u32[]{:S(2)}, u32[]{:S(2)}) collective-permute-start(bf16[128,1024]{1,0:T(8,128)(2,1)S(1)} %fusion.41), channel_id=1, source_target_pairs={{0,2},{1,3},{2,0},{3,1},{4,6},{5,7},{6,4},{7,5},{8,10},{9,11},{10,... | collective-permute-start | bytes 786440 | tf_op jit(solution)/shard_map/ppermute | solution.py:29
  35.7 1.0 fusion.27
  36.7 0.1 collective-permute-start.7
  36.8 0.1 fusion.44
  36.9 0.7 collective-permute-start.9
  37.6 5.9 %collective-permute-done.12 = bf16[128,1024]{1,0:T(8,128)(2,1)S(1)} collective-permute-done((bf16[128,1024]{1,0:T(8,128)(2,1)S(1)}, bf16[128,1024]{1,0:T(8,128)(2,1)S(1)}, u32[]{:S(2)}, u32[]{:S(2)}) %collective-permute-start.12) | collective-permute-done | bytes 262176 | tf_op jit(solution)/shard_map/ppermute | solution.py:29
  43.4 0.1 fusion.43
  43.5 3.1 %collective-permute-start.13 = (bf16[128,1024]{1,0:T(8,128)(2,1)S(1)}, bf16[128,1024]{1,0:T(8,128)(2,1)S(1)}, u32[]{:S(2)}, u32[]{:S(2)}) collective-permute-start(bf16[128,1024]{1,0:T(8,128)(2,1)S(1)} %fusion.43), channel_id=1, source_target_pairs={{0,4},{1,5},{2,6},{3,7},{4,0},{5,1},{6,2},{7,3},{8,12},{9,13},{10,... | collective-permute-start | bytes 786440 | tf_op jit(solution)/shard_map/ppermute | solution.py:29
  46.7 6.4 %collective-permute-done.9 = bf16[128,1024]{1,0:T(8,128)(2,1)S(1)} collective-permute-done((bf16[128,1024]{1,0:T(8,128)(2,1)S(1)}, bf16[128,1024]{1,0:T(8,128)(2,1)S(1)}, u32[]{:S(2)}, u32[]{:S(2)}) %collective-permute-start.9) | collective-permute-done | bytes 262176 | tf_op jit(solution)/shard_map/ppermute | solution.py:29
  53.0 4.5 %collective-permute-done.13 = bf16[128,1024]{1,0:T(8,128)(2,1)S(1)} collective-permute-done((bf16[128,1024]{1,0:T(8,128)(2,1)S(1)}, bf16[128,1024]{1,0:T(8,128)(2,1)S(1)}, u32[]{:S(2)}, u32[]{:S(2)}) %collective-permute-start.13) | collective-permute-done | bytes 262176 | tf_op jit(solution)/shard_map/ppermute | solution.py:29
  57.5 0.2 multiply_reduce_fusion.1
  57.8 0.1 multiply_convert_fusion.12
  57.9 0.1 collective-permute-start.17
  58.0 9.1 %collective-permute-start.15 = (bf16[128,1024]{1,0:T(8,128)(2,1)S(1)}, bf16[128,1024]{1,0:T(8,128)(2,1)S(1)}, u32[]{:S(2)}, u32[]{:S(2)}) collective-permute-start(bf16[128,1024]{1,0:T(8,128)(2,1)S(1)} %multiply_convert_fusion.12), channel_id=1, source_target_pairs={{0,2},{1,3},{2,0},{3,1},{4,6},{5,7},{6,4},{7,5},{8,10},{9,11},{10,... | collective-permute-start | bytes 786440 | tf_op jit(solution)/shard_map/ppermute | solution.py:29
  67.1 5.1 %collective-permute-start.19 = (bf16[128,1024]{1,0:T(8,128)(2,1)S(1)}, bf16[128,1024]{1,0:T(8,128)(2,1)S(1)}, u32[]{:S(2)}, u32[]{:S(2)}) collective-permute-start(bf16[128,1024]{1,0:T(8,128)(2,1)S(1)} %collective-permute-done.17), channel_id=1, source_target_pairs={{0,2},{1,3},{2,0},{3,1},{4,6},{5,7},{6,4},{7,5},{8,10},{9,11},{10,... | collective-permute-start | bytes 786440 | tf_op jit(solution)/shard_map/ppermute | solution.py:29
  72.2 1.4 %collective-permute-done.15 = bf16[128,1024]{1,0:T(8,128)(2,1)S(1)} collective-permute-done((bf16[128,1024]{1,0:T(8,128)(2,1)S(1)}, bf16[128,1024]{1,0:T(8,128)(2,1)S(1)}, u32[]{:S(2)}, u32[]{:S(2)}) %collective-permute-start.15) | collective-permute-done | bytes 262176 | tf_op jit(solution)/shard_map/ppermute | solution.py:29
  73.6 1.1 fusion.83
  74.7 2.3 %collective-permute-done.19 = bf16[128,1024]{1,0:T(8,128)(2,1)S(1)} collective-permute-done((bf16[128,1024]{1,0:T(8,128)(2,1)S(1)}, bf16[128,1024]{1,0:T(8,128)(2,1)S(1)}, u32[]{:S(2)}, u32[]{:S(2)}) %collective-permute-start.19) | collective-permute-done | bytes 262176 | tf_op jit(solution)/shard_map/ppermute | solution.py:29
  77.1 1.3 %fusion.82 = (f32[1536]{0:T(1024)S(1)}, f32[256,1536]{1,0:T(8,128)S(1)}) fusion(bf16[256,1024]{1,0:T(8,128)(2,1)S(1)} %constant_dynamic-update-slice_fusion.2, bf16[1536,1024]{1,0:T(8,128)(2,1)S(1)} %fusion.1), kind=kOutput, calls=%fused_computation.138 | convolution fusion | flops 806877696 | bytes 5249024 | tf_op jit(solution)/shard_map/dot_general | solution.py:77
  78.4 1.1 fusion.84
  79.5 1.1 fusion.81
  80.6 1.0 fusion.64
  81.6 1.0 fusion.63
  82.6 1.0 fusion.60
  83.6 0.8 slice.139
  84.4 0.5 collective-permute-start.21
  84.9 1.0 fusion.62
  86.0 0.1 collective-permute-start.22
  86.1 1.0 fusion.65
  87.1 0.6 collective-permute-start.24
  87.7 0.1 collective-permute-start.25
  87.8 1.0 fusion.61
  88.8 0.4 collective-permute-done.25
  89.3 1.9 %collective-permute-start.26 = (bf16[128,1024]{1,0:T(8,128)(2,1)S(1)}, bf16[128,1024]{1,0:T(8,128)(2,1)S(1)}, u32[]{:S(2)}, u32[]{:S(2)}) collective-permute-start(bf16[128,1024]{1,0:T(8,128)(2,1)S(1)} %fusion.35), channel_id=1, source_target_pairs={{0,2},{1,3},{2,0},{3,1},{4,6},{5,7},{6,4},{7,5},{8,10},{9,11},{10,... | collective-permute-start | bytes 786440 | tf_op jit(solution)/shard_map/ppermute | solution.py:29
  91.2 1.0 fusion.59
  92.3 0.1 fusion.38
  92.3 0.2 collective-permute-start.23
  92.6 5.9 %collective-permute-done.26 = bf16[128,1024]{1,0:T(8,128)(2,1)S(1)} collective-permute-done((bf16[128,1024]{1,0:T(8,128)(2,1)S(1)}, bf16[128,1024]{1,0:T(8,128)(2,1)S(1)}, u32[]{:S(2)}, u32[]{:S(2)}) %collective-permute-start.26) | collective-permute-done | bytes 262176 | tf_op jit(solution)/shard_map/ppermute | solution.py:29
  98.5 0.1 fusion.37
  98.6 3.0 %collective-permute-start.27 = (bf16[128,1024]{1,0:T(8,128)(2,1)S(1)}, bf16[128,1024]{1,0:T(8,128)(2,1)S(1)}, u32[]{:S(2)}, u32[]{:S(2)}) collective-permute-start(bf16[128,1024]{1,0:T(8,128)(2,1)S(1)} %fusion.37), channel_id=1, source_target_pairs={{0,4},{1,5},{2,6},{3,7},{4,0},{5,1},{6,2},{7,3},{8,12},{9,13},{10,... | collective-permute-start | bytes 786440 | tf_op jit(solution)/shard_map/ppermute | solution.py:29
  101.6 2.8 %fusion.2 = bf16[1,1536,1024]{2,1,0:T(8,128)(2,1)} fusion(bf16[256,1024]{1,0:T(8,128)(2,1)S(1)} %copy-done.6, f32[1536,1024]{1,0:T(8,128)S(1)} %fusion.63, f32[1536,1024]{1,0:T(8,128)S(1)} %fusion.59, f32[1536,1024]{1,0:T(8,128)S(1)} %fusion.61, f32[256,1536]{1,0:T(8,128)S(1)} %copy-done.2, f32[1536]{0:T(1024)S(1)} %convert_divide_fusion), kind=kOutput, calls=%fused_computation.5 | convolution fusion | flops 812384256 | bytes 24123392 | tf_op jit(solution)/shard_map/dot_general | solution.py:90
  104.4 3.5 %collective-permute-done.23 = bf16[128,1024]{1,0:T(8,128)(2,1)S(1)} collective-permute-done((bf16[128,1024]{1,0:T(8,128)(2,1)S(1)}, bf16[128,1024]{1,0:T(8,128)(2,1)S(1)}, u32[]{:S(2)}, u32[]{:S(2)}) %collective-permute-start.23) | collective-permute-done | bytes 262176 | tf_op jit(solution)/shard_map/ppermute | solution.py:29
  107.9 5.3 %collective-permute-done.27 = bf16[128,1024]{1,0:T(8,128)(2,1)S(1)} collective-permute-done((bf16[128,1024]{1,0:T(8,128)(2,1)S(1)}, bf16[128,1024]{1,0:T(8,128)(2,1)S(1)}, u32[]{:S(2)}, u32[]{:S(2)}) %collective-permute-start.27) | collective-permute-done | bytes 262176 | tf_op jit(solution)/shard_map/ppermute | solution.py:29
  113.2 0.2 multiply_reduce_fusion
  113.4 1.0 multiply_bitcast_fusion
  (62 shorter events, 0.6 us)
Async XLA Ops:
  0.6 8.3 %copy-start = (bf16[1,1536,1024]{2,1,0:T(8,128)(2,1)S(1)}, bf16[1,1536,1024]{2,1,0:T(8,128)(2,1)}, u32[]{:S(2)}) copy-start(bf16[1,1536,1024]{2,1,0:T(8,128)(2,1)} %param.3) | copy-start | bytes 9437188
  0.6 16.5 %collective-permute-start.3 = (bf16[128,1024]{1,0:T(8,128)(2,1)}, bf16[128,1024]{1,0:T(8,128)(2,1)}, u32[]{:S(2)}, u32[]{:S(2)}) collective-permute-start(bf16[128,1024]{1,0:T(8,128)(2,1)} %bitcast.31), channel_id=1, source_target_pairs={{0,4},{1,5},{2,6},{3,7},{4,0},{5,1},{6,2},{7,3},{8,12},{9,13},{10,... | collective-permute-start | bytes 786440 | tf_op jit(solution)/shard_map/ppermute | solution.py:29
  4.7 13.0 %collective-permute-start.1 = (bf16[128,1024]{1,0:T(8,128)(2,1)}, bf16[128,1024]{1,0:T(8,128)(2,1)}, u32[]{:S(2)}, u32[]{:S(2)}) collective-permute-start(bf16[128,1024]{1,0:T(8,128)(2,1)} %bitcast.32), channel_id=1, source_target_pairs={{0,2},{1,3},{2,0},{3,1},{4,6},{5,7},{6,4},{7,5},{8,10},{9,11},{10,... | collective-permute-start | bytes 786440 | tf_op jit(solution)/shard_map/ppermute | solution.py:29
  6.3 11.9 %collective-permute-start = (bf16[128,1024]{1,0:T(8,128)(2,1)}, bf16[128,1024]{1,0:T(8,128)(2,1)}, u32[]{:S(2)}, u32[]{:S(2)}) collective-permute-start(bf16[128,1024]{1,0:T(8,128)(2,1)} %bitcast.33), channel_id=1, source_target_pairs={{0,1},{1,0},{2,3},{3,2},{4,5},{5,4},{6,7},{7,6},{8,9},{9,8},{10,11... | collective-permute-start | bytes 786440 | tf_op jit(solution)/shard_map/ppermute | solution.py:29
  8.9 0.7 copy-start.8
  8.9 9.3 %copy-start.7 = (bf16[1,128,1024]{2,1,0:T(8,128)(2,1)S(1)}, bf16[1,128,1024]{2,1,0:T(8,128)(2,1)}, u32[]{:S(2)}) copy-start(bf16[1,128,1024]{2,1,0:T(8,128)(2,1)} %param.4) | copy-start | bytes 786436
  17.1 7.6 %collective-permute-start.5 = (bf16[128,1024]{1,0:T(8,128)(2,1)}, bf16[128,1024]{1,0:T(8,128)(2,1)S(1)}, u32[]{:S(2)}, u32[]{:S(2)}) collective-permute-start(bf16[128,1024]{1,0:T(8,128)(2,1)} %collective-permute-done.3), channel_id=1, source_target_pairs={{0,2},{1,3},{2,0},{3,1},{4,6},{5,7},{6,4},{7,5},{8,10},{9,11},{10,... | collective-permute-start | bytes 786440 | tf_op jit(solution)/shard_map/ppermute | solution.py:29
  17.7 7.0 %collective-permute-start.4 = (bf16[128,1024]{1,0:T(8,128)(2,1)}, bf16[128,1024]{1,0:T(8,128)(2,1)S(1)}, u32[]{:S(2)}, u32[]{:S(2)}) collective-permute-start(bf16[128,1024]{1,0:T(8,128)(2,1)} %collective-permute-done.3), channel_id=1, source_target_pairs={{0,1},{1,0},{2,3},{3,2},{4,5},{5,4},{6,7},{7,6},{8,9},{9,8},{10,11... | collective-permute-start | bytes 786440 | tf_op jit(solution)/shard_map/ppermute | solution.py:29
  17.7 9.0 %collective-permute-start.2 = (bf16[128,1024]{1,0:T(8,128)(2,1)}, bf16[128,1024]{1,0:T(8,128)(2,1)S(1)}, u32[]{:S(2)}, u32[]{:S(2)}) collective-permute-start(bf16[128,1024]{1,0:T(8,128)(2,1)} %collective-permute-done.1), channel_id=1, source_target_pairs={{0,1},{1,0},{2,3},{3,2},{4,5},{5,4},{6,7},{7,6},{8,9},{9,8},{10,11... | collective-permute-start | bytes 786440 | tf_op jit(solution)/shard_map/ppermute | solution.py:29
  24.7 4.0 %collective-permute-start.6 = (bf16[128,1024]{1,0:T(8,128)(2,1)S(1)}, bf16[128,1024]{1,0:T(8,128)(2,1)S(1)}, u32[]{:S(2)}, u32[]{:S(2)}) collective-permute-start(bf16[128,1024]{1,0:T(8,128)(2,1)S(1)} %collective-permute-done.5), channel_id=1, source_target_pairs={{0,1},{1,0},{2,3},{3,2},{4,5},{5,4},{6,7},{7,6},{8,9},{9,8},{10,11... | collective-permute-start | bytes 786440 | tf_op jit(solution)/shard_map/ppermute | solution.py:29
  32.0 2.2 %collective-permute-start.11 = (bf16[128,1024]{1,0:T(8,128)(2,1)S(1)}, bf16[128,1024]{1,0:T(8,128)(2,1)S(1)}, u32[]{:S(2)}, u32[]{:S(2)}) collective-permute-start(bf16[128,1024]{1,0:T(8,128)(2,1)S(1)} %slice.140), channel_id=1, source_target_pairs={{0,1},{1,0},{2,3},{3,2},{4,5},{5,4},{6,7},{7,6},{8,9},{9,8},{10,11... | collective-permute-start | bytes 786440 | tf_op jit(solution)/shard_map/ppermute | solution.py:29
  33.6 3.2 %collective-permute-start.8 = (bf16[128,1024]{1,0:T(8,128)(2,1)S(1)}, bf16[128,1024]{1,0:T(8,128)(2,1)S(1)}, u32[]{:S(2)}, u32[]{:S(2)}) collective-permute-start(bf16[128,1024]{1,0:T(8,128)(2,1)S(1)} %slice.142), channel_id=1, source_target_pairs={{0,1},{1,0},{2,3},{3,2},{4,5},{5,4},{6,7},{7,6},{8,9},{9,8},{10,11... | collective-permute-start | bytes 786440 | tf_op jit(solution)/shard_map/ppermute | solution.py:29
  33.7 3.9 %collective-permute-start.10 = (bf16[128,1024]{1,0:T(8,128)(2,1)S(1)}, bf16[128,1024]{1,0:T(8,128)(2,1)S(1)}, u32[]{:S(2)}, u32[]{:S(2)}) collective-permute-start(bf16[128,1024]{1,0:T(8,128)(2,1)S(1)} %slice.141), channel_id=1, source_target_pairs={{0,1},{1,0},{2,3},{3,2},{4,5},{5,4},{6,7},{7,6},{8,9},{9,8},{10,11... | collective-permute-start | bytes 786440 | tf_op jit(solution)/shard_map/ppermute | solution.py:29
  34.2 9.2 %collective-permute-start.12 = (bf16[128,1024]{1,0:T(8,128)(2,1)S(1)}, bf16[128,1024]{1,0:T(8,128)(2,1)S(1)}, u32[]{:S(2)}, u32[]{:S(2)}) collective-permute-start(bf16[128,1024]{1,0:T(8,128)(2,1)S(1)} %fusion.41), channel_id=1, source_target_pairs={{0,2},{1,3},{2,0},{3,1},{4,6},{5,7},{6,4},{7,5},{8,10},{9,11},{10,... | collective-permute-start | bytes 786440 | tf_op jit(solution)/shard_map/ppermute | solution.py:29
  36.7 9.9 %collective-permute-start.7 = (bf16[128,1024]{1,0:T(8,128)(2,1)S(1)}, bf16[128,1024]{1,0:T(8,128)(2,1)S(1)}, u32[]{:S(2)}, u32[]{:S(2)}) collective-permute-start(bf16[128,1024]{1,0:T(8,128)(2,1)S(1)} %slice.143), channel_id=1, source_target_pairs={{0,1},{1,0},{2,3},{3,2},{4,5},{5,4},{6,7},{7,6},{8,9},{9,8},{10,11... | collective-permute-start | bytes 786440 | tf_op jit(solution)/shard_map/ppermute | solution.py:29
  36.9 16.2 %collective-permute-start.9 = (bf16[128,1024]{1,0:T(8,128)(2,1)S(1)}, bf16[128,1024]{1,0:T(8,128)(2,1)S(1)}, u32[]{:S(2)}, u32[]{:S(2)}) collective-permute-start(bf16[128,1024]{1,0:T(8,128)(2,1)S(1)} %fusion.44), channel_id=1, source_target_pairs={{0,2},{1,3},{2,0},{3,1},{4,6},{5,7},{6,4},{7,5},{8,10},{9,11},{10,... | collective-permute-start | bytes 786440 | tf_op jit(solution)/shard_map/ppermute | solution.py:29
  43.5 14.0 %collective-permute-start.13 = (bf16[128,1024]{1,0:T(8,128)(2,1)S(1)}, bf16[128,1024]{1,0:T(8,128)(2,1)S(1)}, u32[]{:S(2)}, u32[]{:S(2)}) collective-permute-start(bf16[128,1024]{1,0:T(8,128)(2,1)S(1)} %fusion.43), channel_id=1, source_target_pairs={{0,4},{1,5},{2,6},{3,7},{4,0},{5,1},{6,2},{7,3},{8,12},{9,13},{10,... | collective-permute-start | bytes 786440 | tf_op jit(solution)/shard_map/ppermute | solution.py:29
  57.9 9.2 %collective-permute-start.17 = (bf16[128,1024]{1,0:T(8,128)(2,1)S(1)}, bf16[128,1024]{1,0:T(8,128)(2,1)S(1)}, u32[]{:S(2)}, u32[]{:S(2)}) collective-permute-start(bf16[128,1024]{1,0:T(8,128)(2,1)S(1)} %multiply_convert_fusion.12), channel_id=1, source_target_pairs={{0,4},{1,5},{2,6},{3,7},{4,0},{5,1},{6,2},{7,3},{8,12},{9,13},{10,... | collective-permute-start | bytes 786440 | tf_op jit(solution)/shard_map/ppermute | solution.py:29
  58.0 15.6 %collective-permute-start.15 = (bf16[128,1024]{1,0:T(8,128)(2,1)S(1)}, bf16[128,1024]{1,0:T(8,128)(2,1)S(1)}, u32[]{:S(2)}, u32[]{:S(2)}) collective-permute-start(bf16[128,1024]{1,0:T(8,128)(2,1)S(1)} %multiply_convert_fusion.12), channel_id=1, source_target_pairs={{0,2},{1,3},{2,0},{3,1},{4,6},{5,7},{6,4},{7,5},{8,10},{9,11},{10,... | collective-permute-start | bytes 786440 | tf_op jit(solution)/shard_map/ppermute | solution.py:29
  67.1 6.5 %collective-permute-start.14 = (bf16[128,1024]{1,0:T(8,128)(2,1)S(1)}, bf16[128,1024]{1,0:T(8,128)(2,1)S(1)}, u32[]{:S(2)}, u32[]{:S(2)}) collective-permute-start(bf16[128,1024]{1,0:T(8,128)(2,1)S(1)} %multiply_convert_fusion.12), channel_id=1, source_target_pairs={{0,1},{1,0},{2,3},{3,2},{4,5},{5,4},{6,7},{7,6},{8,9},{9,8},{10,11... | collective-permute-start | bytes 786440 | tf_op jit(solution)/shard_map/ppermute | solution.py:29
  67.1 10.0 %collective-permute-start.19 = (bf16[128,1024]{1,0:T(8,128)(2,1)S(1)}, bf16[128,1024]{1,0:T(8,128)(2,1)S(1)}, u32[]{:S(2)}, u32[]{:S(2)}) collective-permute-start(bf16[128,1024]{1,0:T(8,128)(2,1)S(1)} %collective-permute-done.17), channel_id=1, source_target_pairs={{0,2},{1,3},{2,0},{3,1},{4,6},{5,7},{6,4},{7,5},{8,10},{9,11},{10,... | collective-permute-start | bytes 786440 | tf_op jit(solution)/shard_map/ppermute | solution.py:29
  72.2 4.9 %collective-permute-start.18 = (bf16[128,1024]{1,0:T(8,128)(2,1)S(1)}, bf16[128,1024]{1,0:T(8,128)(2,1)S(1)}, u32[]{:S(2)}, u32[]{:S(2)}) collective-permute-start(bf16[128,1024]{1,0:T(8,128)(2,1)S(1)} %collective-permute-done.17), channel_id=1, source_target_pairs={{0,1},{1,0},{2,3},{3,2},{4,5},{5,4},{6,7},{7,6},{8,9},{9,8},{10,11... | collective-permute-start | bytes 786440 | tf_op jit(solution)/shard_map/ppermute | solution.py:29
  73.6 4.8 %collective-permute-start.16 = (bf16[128,1024]{1,0:T(8,128)(2,1)S(1)}, bf16[128,1024]{1,0:T(8,128)(2,1)S(1)}, u32[]{:S(2)}, u32[]{:S(2)}) collective-permute-start(bf16[128,1024]{1,0:T(8,128)(2,1)S(1)} %collective-permute-done.15), channel_id=1, source_target_pairs={{0,1},{1,0},{2,3},{3,2},{4,5},{5,4},{6,7},{7,6},{8,9},{9,8},{10,11... | collective-permute-start | bytes 786440 | tf_op jit(solution)/shard_map/ppermute | solution.py:29
  77.1 2.4 %collective-permute-start.20 = (bf16[128,1024]{1,0:T(8,128)(2,1)S(1)}, bf16[128,1024]{1,0:T(8,128)(2,1)S(1)}, u32[]{:S(2)}, u32[]{:S(2)}) collective-permute-start(bf16[128,1024]{1,0:T(8,128)(2,1)S(1)} %collective-permute-done.19), channel_id=1, source_target_pairs={{0,1},{1,0},{2,3},{3,2},{4,5},{5,4},{6,7},{7,6},{8,9},{9,8},{10,11... | collective-permute-start | bytes 786440 | tf_op jit(solution)/shard_map/ppermute | solution.py:29
  79.5 1.1 copy-start.5
  80.6 5.4 %copy-start.1 = (f32[256,1536]{1,0:T(8,128)}, f32[256,1536]{1,0:T(8,128)S(1)}, u32[]{:S(2)}) copy-start(f32[256,1536]{1,0:T(8,128)S(1)} %get-tuple-element.11) | copy-start | bytes 4718596
  83.6 2.3 %copy-start.3 = (f32[256,1024]{1,0:T(8,128)}, f32[256,1024]{1,0:T(8,128)S(1)}, u32[]{:S(2)}) copy-start(f32[256,1024]{1,0:T(8,128)S(1)} %fusion.60) | copy-start | bytes 3145732
  84.4 19.9 %collective-permute-start.21 = (bf16[128,1024]{1,0:T(8,128)(2,1)}, bf16[128,1024]{1,0:T(8,128)(2,1)S(1)}, u32[]{:S(2)}, u32[]{:S(2)}) collective-permute-start(bf16[128,1024]{1,0:T(8,128)(2,1)} %slice.139), channel_id=1, source_target_pairs={{0,1},{1,0},{2,3},{3,2},{4,5},{5,4},{6,7},{7,6},{8,9},{9,8},{10,11... | collective-permute-start | bytes 786440 | tf_op jit(solution)/shard_map/ppermute | solution.py:29
  86.0 6.3 %collective-permute-start.22 = (bf16[128,1024]{1,0:T(8,128)(2,1)S(1)}, bf16[128,1024]{1,0:T(8,128)(2,1)S(1)}, u32[]{:S(2)}, u32[]{:S(2)}) collective-permute-start(bf16[128,1024]{1,0:T(8,128)(2,1)S(1)} %slice.138), channel_id=1, source_target_pairs={{0,1},{1,0},{2,3},{3,2},{4,5},{5,4},{6,7},{7,6},{8,9},{9,8},{10,11... | collective-permute-start | bytes 786440 | tf_op jit(solution)/shard_map/ppermute | solution.py:29
  87.1 5.4 %collective-permute-start.24 = (bf16[128,1024]{1,0:T(8,128)(2,1)S(1)}, bf16[128,1024]{1,0:T(8,128)(2,1)S(1)}, u32[]{:S(2)}, u32[]{:S(2)}) collective-permute-start(bf16[128,1024]{1,0:T(8,128)(2,1)S(1)} %slice.137), channel_id=1, source_target_pairs={{0,1},{1,0},{2,3},{3,2},{4,5},{5,4},{6,7},{7,6},{8,9},{9,8},{10,11... | collective-permute-start | bytes 786440 | tf_op jit(solution)/shard_map/ppermute | solution.py:29
  87.7 1.5 %collective-permute-start.25 = (bf16[128,1024]{1,0:T(8,128)(2,1)S(1)}, bf16[128,1024]{1,0:T(8,128)(2,1)S(1)}, u32[]{:S(2)}, u32[]{:S(2)}) collective-permute-start(bf16[128,1024]{1,0:T(8,128)(2,1)S(1)} %slice.136), channel_id=1, source_target_pairs={{0,1},{1,0},{2,3},{3,2},{4,5},{5,4},{6,7},{7,6},{8,9},{9,8},{10,11... | collective-permute-start | bytes 786440 | tf_op jit(solution)/shard_map/ppermute | solution.py:29
  89.3 9.2 %collective-permute-start.26 = (bf16[128,1024]{1,0:T(8,128)(2,1)S(1)}, bf16[128,1024]{1,0:T(8,128)(2,1)S(1)}, u32[]{:S(2)}, u32[]{:S(2)}) collective-permute-start(bf16[128,1024]{1,0:T(8,128)(2,1)S(1)} %fusion.35), channel_id=1, source_target_pairs={{0,2},{1,3},{2,0},{3,1},{4,6},{5,7},{6,4},{7,5},{8,10},{9,11},{10,... | collective-permute-start | bytes 786440 | tf_op jit(solution)/shard_map/ppermute | solution.py:29
  92.2 9.4 %copy-start.2 = (f32[256,1536]{1,0:T(8,128)S(1)}, f32[256,1536]{1,0:T(8,128)}, u32[]{:S(2)}) copy-start(f32[256,1536]{1,0:T(8,128)} %copy-done.1) | copy-start | bytes 4718596
  92.2 9.4 %copy-start.6 = (bf16[256,1024]{1,0:T(8,128)(2,1)S(1)}, bf16[256,1024]{1,0:T(8,128)(2,1)}, u32[]{:S(2)}) copy-start(bf16[256,1024]{1,0:T(8,128)(2,1)} %copy-done.5) | copy-start | bytes 1572868
  92.3 15.6 %collective-permute-start.23 = (bf16[128,1024]{1,0:T(8,128)(2,1)S(1)}, bf16[128,1024]{1,0:T(8,128)(2,1)S(1)}, u32[]{:S(2)}, u32[]{:S(2)}) collective-permute-start(bf16[128,1024]{1,0:T(8,128)(2,1)S(1)} %fusion.38), channel_id=1, source_target_pairs={{0,2},{1,3},{2,0},{3,1},{4,6},{5,7},{6,4},{7,5},{8,10},{9,11},{10,... | collective-permute-start | bytes 786440 | tf_op jit(solution)/shard_map/ppermute | solution.py:29
  98.6 14.6 %copy-start.4 = (f32[256,1024]{1,0:T(8,128)S(1)}, f32[256,1024]{1,0:T(8,128)}, u32[]{:S(2)}) copy-start(f32[256,1024]{1,0:T(8,128)} %copy-done.3) | copy-start | bytes 3145732
  98.6 14.6 %collective-permute-start.27 = (bf16[128,1024]{1,0:T(8,128)(2,1)S(1)}, bf16[128,1024]{1,0:T(8,128)(2,1)S(1)}, u32[]{:S(2)}, u32[]{:S(2)}) collective-permute-start(bf16[128,1024]{1,0:T(8,128)(2,1)S(1)} %fusion.37), channel_id=1, source_target_pairs={{0,4},{1,5},{2,6},{3,7},{4,0},{5,1},{6,2},{7,3},{8,12},{9,13},{10,... | collective-permute-start | bytes 786440 | tf_op jit(solution)/shard_map/ppermute | solution.py:29

commit v2 on v1

v2 whole, which is shorter than its diff:
```python
import functools

import jax
import jax.numpy as jnp
from jax import lax
from jax.experimental import pallas as pl
from jax.experimental.pallas import tpu as pltpu
from jax.sharding import PartitionSpec as P

TILE = 128
ITERS = 2


sharpness_factor = 48.0
epsilon = 1e-06


def rms_unit(values):
    return values * lax.rsqrt(jnp.mean(values * values, axis=-1, keepdims=True) + epsilon)


def pick_entry(lookup_table, wanted):
    positions = jnp.arange(lookup_table.shape[0], dtype=jnp.int32)
    return jnp.sum(jnp.where(positions == wanted, lookup_table, 0))


def held_tiles(tile_total, shard_place, shard_count, slot_count):
    return jnp.clip((tile_total - shard_place + shard_count - 1) // shard_count, 0, slot_count)


def swap(values, offset):
    places = lax.axis_size("shard")
    return lax.ppermute(values, "shard", [(place, place ^ offset) for place in range(places)])


def low_bit(number):
    return number & -number


def after(values, *others):
    return lax.optimization_barrier((values, others))[0]


DIRECT_PART = 0
GDIR = 0
IN_VMEM = pl.BlockSpec(memory_space=pltpu.VMEM)
IN_SMEM = pl.BlockSpec(memory_space=pltpu.SMEM)
VMEM_ROOM = pltpu.CompilerParams(vmem_limit_bytes=24 << 20)


def cost(weight):
    return pl.CostEstimate(
        flops=weight * 2 * 256 * 1024 * 1536, bytes_accessed=5 << 20, transcendentals=0
    )


def local_call(kernel, name, outs, operands, weight=4):
    return pl.pallas_call(
        kernel,
        out_shape=outs,
        in_specs=[IN_VMEM] * len(operands),
        out_specs=[IN_VMEM] * len(outs),
        name=name,
        compiler_params=VMEM_ROOM,
        cost_estimate=cost(weight),
    )(*operands)


def live_kernel(held, out):
    place = lax.broadcasted_iota(jnp.int32, out.shape, 1)
    out[...] = (place < held[0] * TILE).astype(jnp.float32)


def live_row(held, points):
    return pl.pallas_call(
        live_kernel,
        out_shape=jax.ShapeDtypeStruct((1, points), jnp.float32),
        in_specs=[IN_SMEM],
        out_specs=IN_VMEM,
        name="live",
    )(held[None])


def scores_kernel(*refs):
    *rows, unit, terms, normal = refs
    table = jnp.concatenate([r[...] for r in rows], axis=0)
    scores = lax.dot_general(
        table, unit[...], (((1,), (1,)), ((), ())), preferred_element_type=jnp.float32
    )
    raised = jnp.exp(scores * (sharpness_factor / unit.shape[1]))
    terms[...] = raised.astype(jnp.bfloat16)
    normal[...] = jnp.sum(raised, axis=0, keepdims=True)


def scores_of(rows, unit):
    count, points = sum(r.shape[0] for r in rows), unit.shape[0]
    outs = [
        jax.ShapeDtypeStruct((count, points), jnp.bfloat16),
        jax.ShapeDtypeStruct((1, points), jnp.float32),
    ]
    return local_call(scores_kernel, "scores", outs, [*rows, unit])


def sums_kernel(terms, factor, unit, kept, given):
    half = kept.shape[0]
    weights = (terms[...].astype(jnp.float32) * factor[...]).astype(jnp.bfloat16)
    sums = jnp.dot(weights, unit[...], preferred_element_type=jnp.float32)
    kept[...] = sums[:half]
    given[...] = sums[half:].astype(jnp.bfloat16)


def sums_of(terms, factor, unit):
    shape = (terms.shape[0] // 2, unit.shape[1])
    outs = [jax.ShapeDtypeStruct(shape, t) for t in (jnp.float32, jnp.bfloat16)]
    return local_call(sums_kernel, "sums", outs, [terms, factor, unit])


def blend_kernel(blocks, *refs):
    terms, tables, factor, out = refs[:blocks], refs[blocks:-2], refs[-2], refs[-1]
    total = jnp.zeros(out.shape, jnp.float32)
    for block, table in zip(terms, tables):
        weights = (block[...].astype(jnp.float32) * factor[...]).astype(jnp.bfloat16)
        total = total + lax.dot_general(
            weights, table[...], (((0,), (0,)), ((), ())), preferred_element_type=jnp.float32
        )
    out[...] = total.astype(jnp.bfloat16)


def blend(terms, tables, factor, tile):
    blocks, points = len(terms), factor.shape[1]
    tables = [jnp.concatenate(t) for t in tables]
    width = tables[0].shape[1]
    return pl.pallas_call(
        functools.partial(blend_kernel, blocks),
        grid=(points // tile,),
        out_shape=jax.ShapeDtypeStruct((points, width), jnp.bfloat16),
        in_specs=[pl.BlockSpec((t.shape[0], tile), lambda i: (0, i)) for t in terms]
        + [pl.BlockSpec(t.shape, lambda i: (0, 0)) for t in tables]
        + [pl.BlockSpec((1, tile), lambda i: (0, i))],
        out_specs=pl.BlockSpec((tile, width), lambda i: (i, 0)),
        name="blend",
        compiler_params=VMEM_ROOM,
        cost_estimate=cost(16),
    )(*terms, *tables, factor)


def bits_of(chips):
    return [1 << b for b in range(chips.bit_length() - 1)]


def direct_rows(count):
    return count // DIRECT_PART // 16 * 16 if DIRECT_PART else 0


def gather_terms(own, unit, chips):
    bits, cut = bits_of(chips), GDIR and direct_rows(own.shape[0])
    beside = swap(own, 1)
    near = swap(own, 2)
    stepped = {0: own[cut:]}
    for bit in reversed(bits):
        for j in sorted(stepped):
            if j ^ bit not in stepped and j ^ bit != 1:
                stepped[j ^ bit] = swap(stepped[j], 2 * bit)
    rows = {0: [own], 1: [near]}
    for j in range(2, chips):
        straight = [swap(after(own[:cut], beside), 2 * j)] if cut else []
        rows[j] = [*straight, stepped[j]]
    tables, terms = {}, {}
    for j in range(chips):
        if j:
            held = after(rows[j][-1], *terms.values()) if j == chips - 1 else rows[j][-1]
            others = [swap(r, 1) for r in (*rows[j][:-1], held)]
        else:
            others = [beside]
        tables[j] = [*rows[j], *others]
        terms[j] = scores_of(tables[j], unit)
    return tables, terms


def scatter_sums(terms, factor, unit, chips, beside):
    bits = bits_of(chips)
    order = sorted(terms, key=lambda j: (low_bit(j) or chips, -j))
    kept, given, totals, gate = {}, {}, {}, ()
    for place, j in enumerate(order):
        kept[j], given[j] = sums_of(after(terms[j], *gate), factor, unit)
        if j:
            totals[j] = kept[j] + swap(given[j], 1).astype(jnp.float32)
        gate = (totals[order[0]],) if place else (given[j],)
    cut = direct_rows(kept[0].shape[0])
    straight = []
    stepped = {j: totals[j][cut:] for j in totals if j > 1}
    for j in order:
        if j > 1:
            bit = low_bit(j)
            if cut:
                straight.append(swap(totals[j][:cut].astype(jnp.bfloat16), 2 * j))
            gate = stepped[j]
            got = swap(stepped[j].astype(jnp.bfloat16), 2 * bit).astype(jnp.float32)
            stepped[j ^ bit] = stepped[j ^ bit] + got if j ^ bit else got
    near = swap(after(totals[1].astype(jnp.bfloat16), given[0]), 2)
    done = beside(gate)
    mine = kept[0] + swap(after(given[0], *done), 1).astype(jnp.float32) + near.astype(jnp.float32)
    far = stepped[0]
    if cut:
        far = jnp.concatenate([sum(s.astype(jnp.float32) for s in straight), far])
    return mine + far, done


def body(points, centroids, tile_counts):
    slot_count = points.shape[1] // TILE
    shard_count = lax.axis_size("shard")
    shard_place = lax.axis_index("shard")
    group_index = lax.axis_index("grp")
    chips = shard_count // 2
    own_held = held_tiles(
        pick_entry(tile_counts, group_index), shard_place, shard_count, slot_count
    )
    live = live_row(own_held, slot_count * TILE)
    unit = rms_unit(after(points[0], live).astype(jnp.float32)).astype(jnp.bfloat16)
    current = centroids[0]
    for iteration in range(ITERS):
        tables, scored = gather_terms(current, unit, chips)
        terms = {j: scored[j][0] for j in scored}
        factor = live / sum(scored[j][1] for j in sorted(scored))

        def posterior(gate):
            if iteration < ITERS - 1:
                return ()
            blocks = sorted(tables)
            return (
                blend([after(terms[j], gate) for j in blocks], [tables[j] for j in blocks], factor, 2 * TILE),
            )

        reduced, out_rows = scatter_sums(terms, factor, unit, chips, posterior)
        updated = rms_unit(reduced)
        current = updated.astype(jnp.bfloat16)
    return (updated[None], out_rows[0][None])


def solution(mesh):
    return jax.shard_map(
        body,
        mesh=mesh,
        in_specs=(P("grp", "shard", None), P("grp", "shard", None), P()),
        out_specs=(P("grp", "shard", None), P("grp", "shard", None)),
        check_vma=False,
    )
```

time: 115 us -> 104 us (0.904)
  matrix products: 25.2 us -> 0 us
  Pallas kernels: 0 us -> 23.2 us
  waiting for transfers between devices: 46.4 us -> 38 us
    dot_general x20 -> x0, matrix products: 25.2 us -> none  [the longest x8 11.5 us: body(): lax.dot_general(tables[j], unit, (((1,), (1,)), ((), ())), preferred_elem...]
    pallas_call x0 -> x18, Pallas kernels: none -> 23.2 us  [the longest x16 16.9 us: local_call(): pl.pallas_call(kernel, out_shape=outs, in_specs=[IN_VMEM] * len(operands)...]
    ppermute x28, waiting for transfers between devices: 46.4 us -> 38 us  [swap(): lax.ppermute(values, 'shard', [(place, place ^ offset) for place in range...]
  transfers between devices with their start and end apart: 28 -> 28, of which waited for: 11 -> 14; matrix products, arithmetic and copies ran while one was open for 20% -> 5% of each run, Pallas kernels for 0% -> 18%
where the time goes in v2:
time: 104 us
  waiting for transfers between devices  38 us (37%)
  starting transfers between devices  34.2 us (33%)
  Pallas kernels  23.2 us (22%)
  other arithmetic  6.78 us (7%)
  between operations  1.63 us (2%)
    ppermute x28, waiting for transfers between devices, swap(): lax.ppermute(values, 'shard', [(place, place ^ offset) for place in range...  38 us
    ppermute x28, starting transfers between devices, swap(): lax.ppermute(values, 'shard', [(place, place ^ offset) for place in range...  34.2 us
    pallas_call x16, Pallas kernels, local_call(): pl.pallas_call(kernel, out_shape=outs, in_specs=[IN_VMEM] * len(operands)...  16.9 us
    pallas_call x1, Pallas kernels, blend(): pl.pallas_call(functools.partial(blend_kernel, blocks), grid=(points // t...  5.64 us
    reduce_sum x3, other arithmetic, rms_unit(): jnp.mean(values * values, axis=-1, keepdims=True) + epsilon  3.17 us
  transfers between devices with their start and end apart: 28, of which 14 were waited for; matrix products, arithmetic and copies ran while one was open for 5% of the time, Pallas kernels for 18%

profile of v2, /device:TPU:0, one launch (start us, length us, event | category | flops | bytes accessed | tf_op | source)
XLA Modules:
  0.0 103.8 jit_solution(11965523703308876441)
XLA Ops:
  0.6 4.1 %collective-permute-start.1 = (bf16[128,1024]{1,0:T(8,128)(2,1)}, bf16[128,1024]{1,0:T(8,128)(2,1)S(1)}, u32[]{:S(2)}, u32[]{:S(2)}) collective-permute-start(bf16[128,1024]{1,0:T(8,128)(2,1)} %bitcast.6), channel_id=1, source_target_pairs={{0,4},{1,5},{2,6},{3,7},{4,0},{5,1},{6,2},{7,3},{8,12},{9,13},{10,... | collective-permute-start | bytes 786440 | tf_op jit(solution)/shard_map/ppermute | solution.py:33
  4.7 1.6 %collective-permute-start.3 = (bf16[128,1024]{1,0:T(8,128)(2,1)}, bf16[128,1024]{1,0:T(8,128)(2,1)S(1)}, u32[]{:S(2)}, u32[]{:S(2)}) collective-permute-start(bf16[128,1024]{1,0:T(8,128)(2,1)} %bitcast.8), channel_id=1, source_target_pairs={{0,2},{1,3},{2,0},{3,1},{4,6},{5,7},{6,4},{7,5},{8,10},{9,11},{10,... | collective-permute-start | bytes 786440 | tf_op jit(solution)/shard_map/ppermute | solution.py:33
  6.3 1.3 %fusion.2 = s32[]{:T(128)} fusion(s32[4]{0:T(128)} %param.5, s32[]{:T(128)S(6)} %axis_index.23), kind=kLoop, calls=%fused_computation.24 | loop fusion | flops 11 | bytes 24 | tf_op jit(solution)/shard_map/reduce_sum | solution.py:24
  8.3 0.6 live.1
  8.9 2.7 %fusion = f32[1536]{0:T(1024)S(1)} fusion(bf16[1536,1024]{1,0:T(8,128)(2,1)} %bitcast.10), kind=kLoop, calls=%fused_computation.2 | loop fusion | flops 4717056 | bytes 3151872 | tf_op jit(solution)/shard_map/reduce_sum | solution.py:19
  11.6 0.1 copy-done.1
  11.7 0.6 fusion.1.refs_2_.unit
  12.3 4.7 %collective-permute-done.1.refs_0_ = bf16[128,1024]{1,0:T(8,128)(2,1)S(1)} collective-permute-done((bf16[128,1024]{1,0:T(8,128)(2,1)}, bf16[128,1024]{1,0:T(8,128)(2,1)S(1)}, u32[]{:S(2)}, u32[]{:S(2)}) %collective-permute-start.1) | collective-permute-done | bytes 262176 | tf_op jit(solution)/shard_map/ppermute | solution.py:33
  17.0 0.8 collective-permute-start.2
  17.7 0.4 collective-permute-done.3.refs_0_
  18.1 0.1 collective-permute-start.4
  18.3 1.1 %scores.8 = (bf16[256,1536]{1,0:T(8,128)(2,1)S(1)}, f32[1,1536]{1,0:T(1,128)S(1)}) custom-call(bf16[128,1024]{1,0:T(8,128)(2,1)S(1)} %bitcast.9, bf16[128,1024]{1,0:T(8,128)(2,1)S(1)} %collective-permute-done.refs_1_, bf16[1536,1024]{1,0:T(8,128)(2,1)S(1)} %fusion.1.refs_2_.unit), custom_call_target="tpu_custom_call" | custom-call | flops 3221225472 | bytes 5242880 | tf_op jit(solution)/shard_map/scores/pallas_call | solution.py:58
  19.4 0.3 collective-permute-done.4.refs_1_
  19.7 1.1 %scores.9 = (bf16[256,1536]{1,0:T(8,128)(2,1)S(1)}, f32[1,1536]{1,0:T(1,128)S(1)}) custom-call(bf16[128,1024]{1,0:T(8,128)(2,1)S(1)} %collective-permute-done.3.refs_0_, bf16[128,1024]{1,0:T(8,128)(2,1)S(1)} %collective-permute-done.4.refs_1_, bf16[1536,1024]{1,0:T(8,128)(2,1)S(1)} %fusion.1.refs_2_.unit), custom_call_target="tpu_custom_call" | custom-call | flops 3221225472 | bytes 5242880 | tf_op jit(solution)/shard_map/scores/pallas_call | solution.py:58
  20.8 1.1 %scores.10 = (bf16[256,1536]{1,0:T(8,128)(2,1)S(1)}, f32[1,1536]{1,0:T(1,128)S(1)}) custom-call(bf16[128,1024]{1,0:T(8,128)(2,1)S(1)} %collective-permute-done.1.refs_0_, bf16[128,1024]{1,0:T(8,128)(2,1)S(1)} %collective-permute-done.5.refs_1_, bf16[1536,1024]{1,0:T(8,128)(2,1)S(1)} %fusion.1.refs_2_.unit), custom_call_target="tpu_custom_call" | custom-call | flops 3221225472 | bytes 5242880 | tf_op jit(solution)/shard_map/scores/pallas_call | solution.py:58
  21.9 2.5 %collective-permute-done.2.refs_0_ = bf16[128,1024]{1,0:T(8,128)(2,1)S(1)} collective-permute-done((bf16[128,1024]{1,0:T(8,128)(2,1)S(1)}, bf16[128,1024]{1,0:T(8,128)(2,1)S(1)}, u32[]{:S(2)}, u32[]{:S(2)}) %collective-permute-start.2) | collective-permute-done | bytes 262176 | tf_op jit(solution)/shard_map/ppermute | solution.py:33
  24.4 1.5 %collective-permute-done.6.refs_1_ = bf16[128,1024]{1,0:T(8,128)(2,1)S(1)} collective-permute-done((bf16[128,1024]{1,0:T(8,128)(2,1)S(1)}, bf16[128,1024]{1,0:T(8,128)(2,1)S(1)}, u32[]{:S(2)}, u32[]{:S(2)}) %collective-permute-start.6) | collective-permute-done | bytes 262176 | tf_op jit(solution)/shard_map/ppermute | solution.py:33
  25.9 1.1 %scores.11 = (bf16[256,1536]{1,0:T(8,128)(2,1)S(1)}, f32[1,1536]{1,0:T(1,128)S(1)}) custom-call(bf16[128,1024]{1,0:T(8,128)(2,1)S(1)} %collective-permute-done.2.refs_0_, bf16[128,1024]{1,0:T(8,128)(2,1)S(1)} %collective-permute-done.6.refs_1_, bf16[1536,1024]{1,0:T(8,128)(2,1)S(1)} %fusion.1.refs_2_.unit), custom_call_target="tpu_custom_call" | custom-call | flops 3221225472 | bytes 5242880 | tf_op jit(solution)/shard_map/scores/pallas_call | solution.py:58
  27.1 1.0 sums.8
  28.1 0.2 collective-permute-start.7
  28.3 1.0 sums.10
  29.3 0.4 collective-permute-start.9
  29.8 1.6 %collective-permute-start.12 = (bf16[128,1024]{1,0:T(8,128)(2,1)S(1)}, bf16[128,1024]{1,0:T(8,128)(2,1)S(1)}, u32[]{:S(2)}, u32[]{:S(2)}) collective-permute-start(bf16[128,1024]{1,0:T(8,128)(2,1)S(1)} %convert_add_fusion.4), channel_id=1, source_target_pairs={{0,2},{1,3},{2,0},{3,1},{4,6},{5,7},{6,4},{7,5},{8,10},{9,11},{10,... | collective-permute-start | bytes 786440 | tf_op jit(solution)/shard_map/ppermute | solution.py:33
  31.4 1.0 sums.11
  32.4 0.1 collective-permute-start.11
  32.5 1.0 sums.9
  33.6 0.5 collective-permute-start.10
  34.1 0.2 collective-permute-start.8
  34.3 4.7 %collective-permute-done.12 = bf16[128,1024]{1,0:T(8,128)(2,1)S(1)} collective-permute-done((bf16[128,1024]{1,0:T(8,128)(2,1)S(1)}, bf16[128,1024]{1,0:T(8,128)(2,1)S(1)}, u32[]{:S(2)}, u32[]{:S(2)}) %collective-permute-start.12) | collective-permute-done | bytes 262176 | tf_op jit(solution)/shard_map/ppermute | solution.py:33
  39.0 0.1 add_convert_fusion.1
  39.1 3.2 %collective-permute-start.13 = (bf16[128,1024]{1,0:T(8,128)(2,1)S(1)}, bf16[128,1024]{1,0:T(8,128)(2,1)S(1)}, u32[]{:S(2)}, u32[]{:S(2)}) collective-permute-start(bf16[128,1024]{1,0:T(8,128)(2,1)S(1)} %add_convert_fusion.1), channel_id=1, source_target_pairs={{0,4},{1,5},{2,6},{3,7},{4,0},{5,1},{6,2},{7,3},{8,12},{9,13},{10,... | collective-permute-start | bytes 786440 | tf_op jit(solution)/shard_map/ppermute | solution.py:33
  42.3 6.3 %collective-permute-done.10 = bf16[128,1024]{1,0:T(8,128)(2,1)S(1)} collective-permute-done((bf16[128,1024]{1,0:T(8,128)(2,1)S(1)}, bf16[128,1024]{1,0:T(8,128)(2,1)S(1)}, u32[]{:S(2)}, u32[]{:S(2)}) %collective-permute-start.10) | collective-permute-done | bytes 262176 | tf_op jit(solution)/shard_map/ppermute | solution.py:33
  48.6 4.6 %collective-permute-done.13 = bf16[128,1024]{1,0:T(8,128)(2,1)S(1)} collective-permute-done((bf16[128,1024]{1,0:T(8,128)(2,1)S(1)}, bf16[128,1024]{1,0:T(8,128)(2,1)S(1)}, u32[]{:S(2)}, u32[]{:S(2)}) %collective-permute-start.13) | collective-permute-done | bytes 262176 | tf_op jit(solution)/shard_map/ppermute | solution.py:33
  53.2 0.2 multiply_reduce_fusion.1
  53.5 0.2 multiply_convert_fusion.refs_0_
  53.6 0.1 collective-permute-start.15
  53.7 9.2 %collective-permute-start.17 = (bf16[128,1024]{1,0:T(8,128)(2,1)S(1)}, bf16[128,1024]{1,0:T(8,128)(2,1)S(1)}, u32[]{:S(2)}, u32[]{:S(2)}) collective-permute-start(bf16[128,1024]{1,0:T(8,128)(2,1)S(1)} %multiply_convert_fusion.refs_0_), channel_id=1, source_target_pairs={{0,2},{1,3},{2,0},{3,1},{4,6},{5,7},{6,4},{7,5},{8,10},{9,11},{10,... | collective-permute-start | bytes 786440 | tf_op jit(solution)/shard_map/ppermute | solution.py:33
  63.0 5.2 %collective-permute-start.16 = (bf16[128,1024]{1,0:T(8,128)(2,1)S(1)}, bf16[128,1024]{1,0:T(8,128)(2,1)S(1)}, u32[]{:S(2)}, u32[]{:S(2)}) collective-permute-start(bf16[128,1024]{1,0:T(8,128)(2,1)S(1)} %collective-permute-done.15.refs_0_), channel_id=1, source_target_pairs={{0,2},{1,3},{2,0},{3,1},{4,6},{5,7},{6,4},{7,5},{8,10},{9,11},{10,... | collective-permute-start | bytes 786440 | tf_op jit(solution)/shard_map/ppermute | solution.py:33
  68.2 1.3 %collective-permute-done.17.refs_0_ = bf16[128,1024]{1,0:T(8,128)(2,1)S(1)} collective-permute-done((bf16[128,1024]{1,0:T(8,128)(2,1)S(1)}, bf16[128,1024]{1,0:T(8,128)(2,1)S(1)}, u32[]{:S(2)}, u32[]{:S(2)}) %collective-permute-start.17) | collective-permute-done | bytes 262176 | tf_op jit(solution)/shard_map/ppermute | solution.py:33
  69.5 1.1 %scores.12 = (bf16[256,1536]{1,0:T(8,128)(2,1)S(1)}, f32[1,1536]{1,0:T(1,128)S(1)}) custom-call(bf16[128,1024]{1,0:T(8,128)(2,1)S(1)} %multiply_convert_fusion.refs_0_, bf16[128,1024]{1,0:T(8,128)(2,1)S(1)} %collective-permute-done.14.refs_1_, bf16[1536,1024]{1,0:T(8,128)(2,1)S(1)} %fusion.1.refs_2_.unit), custom_call_target="tpu_custom_call" | custom-call | flops 3221225472 | bytes 5242880 | tf_op jit(solution)/shard_map/scores/pallas_call | solution.py:58
  70.6 0.4 collective-permute-done.18.refs_1_
  71.0 1.1 %scores.13 = (bf16[256,1536]{1,0:T(8,128)(2,1)S(1)}, f32[1,1536]{1,0:T(1,128)S(1)}) custom-call(bf16[128,1024]{1,0:T(8,128)(2,1)S(1)} %collective-permute-done.17.refs_0_, bf16[128,1024]{1,0:T(8,128)(2,1)S(1)} %collective-permute-done.18.refs_1_, bf16[1536,1024]{1,0:T(8,128)(2,1)S(1)} %fusion.1.refs_2_.unit), custom_call_target="tpu_custom_call" | custom-call | flops 3221225472 | bytes 5242880 | tf_op jit(solution)/shard_map/scores/pallas_call | solution.py:58
  72.1 1.3 %scores.14 = (bf16[256,1536]{1,0:T(8,128)(2,1)S(1)}, f32[1,1536]{1,0:T(1,128)S(1)}) custom-call(bf16[128,1024]{1,0:T(8,128)(2,1)S(1)} %collective-permute-done.15.refs_0_, bf16[128,1024]{1,0:T(8,128)(2,1)S(1)} %collective-permute-done.19.refs_1_, bf16[1536,1024]{1,0:T(8,128)(2,1)S(1)} %fusion.1.refs_2_.unit), custom_call_target="tpu_custom_call" | custom-call | flops 3221225472 | bytes 5242880 | tf_op jit(solution)/shard_map/scores/pallas_call | solution.py:58
  73.4 0.2 collective-permute-start.20
  73.8 1.3 %collective-permute-done.20.refs_1_ = bf16[128,1024]{1,0:T(8,128)(2,1)S(1)} collective-permute-done((bf16[128,1024]{1,0:T(8,128)(2,1)S(1)}, bf16[128,1024]{1,0:T(8,128)(2,1)S(1)}, u32[]{:S(2)}, u32[]{:S(2)}) %collective-permute-start.20) | collective-permute-done | bytes 262176 | tf_op jit(solution)/shard_map/ppermute | solution.py:33
  75.0 1.1 %scores.15 = (bf16[256,1536]{1,0:T(8,128)(2,1)S(1)}, f32[1,1536]{1,0:T(1,128)S(1)}) custom-call(bf16[128,1024]{1,0:T(8,128)(2,1)S(1)} %collective-permute-done.16.refs_0_, bf16[128,1024]{1,0:T(8,128)(2,1)S(1)} %collective-permute-done.20.refs_1_, bf16[1536,1024]{1,0:T(8,128)(2,1)S(1)} %fusion.1.refs_2_.unit), custom_call_target="tpu_custom_call" | custom-call | flops 3221225472 | bytes 5242880 | tf_op jit(solution)/shard_map/scores/pallas_call | solution.py:58
  76.2 1.0 sums.12
  77.2 0.2 collective-permute-start.21
  77.4 1.0 sums.15
  78.4 0.4 collective-permute-start.25
  78.9 0.1 convert_add_fusion.2
  78.9 2.5 %collective-permute-start.23 = (bf16[128,1024]{1,0:T(8,128)(2,1)S(1)}, bf16[128,1024]{1,0:T(8,128)(2,1)S(1)}, u32[]{:S(2)}, u32[]{:S(2)}) collective-permute-start(bf16[128,1024]{1,0:T(8,128)(2,1)S(1)} %convert_add_fusion.2), channel_id=1, source_target_pairs={{0,2},{1,3},{2,0},{3,1},{4,6},{5,7},{6,4},{7,5},{8,10},{9,11},{10,... | collective-permute-start | bytes 786440 | tf_op jit(solution)/shard_map/ppermute | solution.py:33
  81.5 1.0 sums.14
  82.5 0.1 collective-permute-start.22
  82.6 1.0 sums.13
  83.6 0.2 collective-permute-start.26
  83.9 4.7 %collective-permute-done.23 = bf16[128,1024]{1,0:T(8,128)(2,1)S(1)} collective-permute-done((bf16[128,1024]{1,0:T(8,128)(2,1)S(1)}, bf16[128,1024]{1,0:T(8,128)(2,1)S(1)}, u32[]{:S(2)}, u32[]{:S(2)}) %collective-permute-start.23) | collective-permute-done | bytes 262176 | tf_op jit(solution)/shard_map/ppermute | solution.py:33
  88.6 0.1 convert_add_fusion.1
  88.7 3.1 %collective-permute-start.27 = (bf16[128,1024]{1,0:T(8,128)(2,1)S(1)}, bf16[128,1024]{1,0:T(8,128)(2,1)S(1)}, u32[]{:S(2)}, u32[]{:S(2)}) collective-permute-start(bf16[128,1024]{1,0:T(8,128)(2,1)S(1)} %convert_add_fusion.1), channel_id=1, source_target_pairs={{0,4},{1,5},{2,6},{3,7},{4,0},{5,1},{6,2},{7,3},{8,12},{9,13},{10,... | collective-permute-start | bytes 786440 | tf_op jit(solution)/shard_map/ppermute | solution.py:33
  91.8 5.6 %blend.1 = bf16[1536,1024]{1,0:T(8,128)(2,1)} custom-call(bf16[256,1536]{1,0:T(8,128)(2,1)S(1)} %get-tuple-element.89.terms.refs_0_, bf16[256,1536]{1,0:T(8,128)(2,1)S(1)} %get-tuple-element.90.refs_1_.terms, bf16[256,1536]{1,0:T(8,128)(2,1)S(1)} %get-tuple-element.91.terms.refs_2_, bf16[256,1536]{1,0:T(8,128)(2,1)S(1)} %get-tuple-element.92.terms.refs_3_, ...), custom_call_target="tpu_custom_call" | custom-call | flops 12884901888 | bytes 5242880 | tf_op jit(solution)/shard_map/blend/pallas_call | solution.py:133
  97.4 0.8 collective-permute-done.26
  98.2 4.4 %collective-permute-done.27 = bf16[128,1024]{1,0:T(8,128)(2,1)S(1)} collective-permute-done((bf16[128,1024]{1,0:T(8,128)(2,1)S(1)}, bf16[128,1024]{1,0:T(8,128)(2,1)S(1)}, u32[]{:S(2)}, u32[]{:S(2)}) %collective-permute-start.27) | collective-permute-done | bytes 262176 | tf_op jit(solution)/shard_map/ppermute | solution.py:33
  102.7 0.2 multiply_reduce_fusion
  102.9 0.9 multiply_bitcast_fusion
  (38 shorter events, 0.4 us)
Async XLA Ops:
  0.6 16.3 %collective-permute-start.1 = (bf16[128,1024]{1,0:T(8,128)(2,1)}, bf16[128,1024]{1,0:T(8,128)(2,1)S(1)}, u32[]{:S(2)}, u32[]{:S(2)}) collective-permute-start(bf16[128,1024]{1,0:T(8,128)(2,1)} %bitcast.6), channel_id=1, source_target_pairs={{0,4},{1,5},{2,6},{3,7},{4,0},{5,1},{6,2},{7,3},{8,12},{9,13},{10,... | collective-permute-start | bytes 786440 | tf_op jit(solution)/shard_map/ppermute | solution.py:33
  4.7 13.5 %collective-permute-start = (bf16[128,1024]{1,0:T(8,128)(2,1)}, bf16[128,1024]{1,0:T(8,128)(2,1)S(1)}, u32[]{:S(2)}, u32[]{:S(2)}) collective-permute-start(bf16[128,1024]{1,0:T(8,128)(2,1)} %bitcast.7), channel_id=1, source_target_pairs={{0,1},{1,0},{2,3},{3,2},{4,5},{5,4},{6,7},{7,6},{8,9},{9,8},{10,11... | collective-permute-start | bytes 786440 | tf_op jit(solution)/shard_map/ppermute | solution.py:33
  4.7 13.4 %collective-permute-start.3 = (bf16[128,1024]{1,0:T(8,128)(2,1)}, bf16[128,1024]{1,0:T(8,128)(2,1)S(1)}, u32[]{:S(2)}, u32[]{:S(2)}) collective-permute-start(bf16[128,1024]{1,0:T(8,128)(2,1)} %bitcast.8), channel_id=1, source_target_pairs={{0,2},{1,3},{2,0},{3,1},{4,6},{5,7},{6,4},{7,5},{8,10},{9,11},{10,... | collective-permute-start | bytes 786440 | tf_op jit(solution)/shard_map/ppermute | solution.py:33
  8.9 2.8 %copy-start.1 = (bf16[1,1536,1024]{2,1,0:T(8,128)(2,1)S(1)}, bf16[1,1536,1024]{2,1,0:T(8,128)(2,1)}, u32[]{:S(2)}) copy-start(bf16[1,1536,1024]{2,1,0:T(8,128)(2,1)} %param.3) | copy-start | bytes 9437188
  11.7 6.5 %copy-start = (bf16[1,128,1024]{2,1,0:T(8,128)(2,1)S(1)}, bf16[1,128,1024]{2,1,0:T(8,128)(2,1)}, u32[]{:S(2)}) copy-start(bf16[1,128,1024]{2,1,0:T(8,128)(2,1)} %param.4) | copy-start | bytes 786436
  17.0 7.4 %collective-permute-start.2 = (bf16[128,1024]{1,0:T(8,128)(2,1)S(1)}, bf16[128,1024]{1,0:T(8,128)(2,1)S(1)}, u32[]{:S(2)}, u32[]{:S(2)}) collective-permute-start(bf16[128,1024]{1,0:T(8,128)(2,1)S(1)} %collective-permute-done.1.refs_0_), channel_id=1, source_target_pairs={{0,2},{1,3},{2,0},{3,1},{4,6},{5,7},{6,4},{7,5},{8,10},{9,11},{10,... | collective-permute-start | bytes 786440 | tf_op jit(solution)/shard_map/ppermute | solution.py:33
  17.7 3.0 %collective-permute-start.5 = (bf16[128,1024]{1,0:T(8,128)(2,1)S(1)}, bf16[128,1024]{1,0:T(8,128)(2,1)S(1)}, u32[]{:S(2)}, u32[]{:S(2)}) collective-permute-start(bf16[128,1024]{1,0:T(8,128)(2,1)S(1)} %collective-permute-done.1.refs_0_), channel_id=1, source_target_pairs={{0,1},{1,0},{2,3},{3,2},{4,5},{5,4},{6,7},{7,6},{8,9},{9,8},{10,11... | collective-permute-start | bytes 786440 | tf_op jit(solution)/shard_map/ppermute | solution.py:33
  18.1 1.5 %collective-permute-start.4 = (bf16[128,1024]{1,0:T(8,128)(2,1)S(1)}, bf16[128,1024]{1,0:T(8,128)(2,1)S(1)}, u32[]{:S(2)}, u32[]{:S(2)}) collective-permute-start(bf16[128,1024]{1,0:T(8,128)(2,1)S(1)} %collective-permute-done.3.refs_0_), channel_id=1, source_target_pairs={{0,1},{1,0},{2,3},{3,2},{4,5},{5,4},{6,7},{7,6},{8,9},{9,8},{10,11... | collective-permute-start | bytes 786440 | tf_op jit(solution)/shard_map/ppermute | solution.py:33
  24.4 2.6 %copy-start.2 = (f32[1,1536]{1,0:T(1,128)S(1)}, f32[1,1536]{1,0:T(1,128)}, u32[]{:S(2)}) copy-start(f32[1,1536]{1,0:T(1,128)} %live.1) | copy-start | bytes 18436
  24.4 1.5 %collective-permute-start.6 = (bf16[128,1024]{1,0:T(8,128)(2,1)S(1)}, bf16[128,1024]{1,0:T(8,128)(2,1)S(1)}, u32[]{:S(2)}, u32[]{:S(2)}) collective-permute-start(bf16[128,1024]{1,0:T(8,128)(2,1)S(1)} %collective-permute-done.2.refs_0_), channel_id=1, source_target_pairs={{0,1},{1,0},{2,3},{3,2},{4,5},{5,4},{6,7},{7,6},{8,9},{9,8},{10,11... | collective-permute-start | bytes 786440 | tf_op jit(solution)/shard_map/ppermute | solution.py:33
  28.1 1.6 %collective-permute-start.7 = (bf16[128,1024]{1,0:T(8,128)(2,1)S(1)}, bf16[128,1024]{1,0:T(8,128)(2,1)S(1)}, u32[]{:S(2)}, u32[]{:S(2)}) collective-permute-start(bf16[128,1024]{1,0:T(8,128)(2,1)S(1)} %get-tuple-element.61), channel_id=1, source_target_pairs={{0,1},{1,0},{2,3},{3,2},{4,5},{5,4},{6,7},{7,6},{8,9},{9,8},{10,11... | collective-permute-start | bytes 786440 | tf_op jit(solution)/shard_map/ppermute | solution.py:33
  29.3 4.2 %collective-permute-start.9 = (bf16[128,1024]{1,0:T(8,128)(2,1)S(1)}, bf16[128,1024]{1,0:T(8,128)(2,1)S(1)}, u32[]{:S(2)}, u32[]{:S(2)}) collective-permute-start(bf16[128,1024]{1,0:T(8,128)(2,1)S(1)} %get-tuple-element.67), channel_id=1, source_target_pairs={{0,1},{1,0},{2,3},{3,2},{4,5},{5,4},{6,7},{7,6},{8,9},{9,8},{10,11... | collective-permute-start | bytes 786440 | tf_op jit(solution)/shard_map/ppermute | solution.py:33
  29.8 9.2 %collective-permute-start.12 = (bf16[128,1024]{1,0:T(8,128)(2,1)S(1)}, bf16[128,1024]{1,0:T(8,128)(2,1)S(1)}, u32[]{:S(2)}, u32[]{:S(2)}) collective-permute-start(bf16[128,1024]{1,0:T(8,128)(2,1)S(1)} %convert_add_fusion.4), channel_id=1, source_target_pairs={{0,2},{1,3},{2,0},{3,1},{4,6},{5,7},{6,4},{7,5},{8,10},{9,11},{10,... | collective-permute-start | bytes 786440 | tf_op jit(solution)/shard_map/ppermute | solution.py:33
  32.4 6.6 %collective-permute-start.11 = (bf16[128,1024]{1,0:T(8,128)(2,1)S(1)}, bf16[128,1024]{1,0:T(8,128)(2,1)S(1)}, u32[]{:S(2)}, u32[]{:S(2)}) collective-permute-start(bf16[128,1024]{1,0:T(8,128)(2,1)S(1)} %get-tuple-element.71), channel_id=1, source_target_pairs={{0,1},{1,0},{2,3},{3,2},{4,5},{5,4},{6,7},{7,6},{8,9},{9,8},{10,11... | collective-permute-start | bytes 786440 | tf_op jit(solution)/shard_map/ppermute | solution.py:33
  33.6 15.0 %collective-permute-start.10 = (bf16[128,1024]{1,0:T(8,128)(2,1)S(1)}, bf16[128,1024]{1,0:T(8,128)(2,1)S(1)}, u32[]{:S(2)}, u32[]{:S(2)}) collective-permute-start(bf16[128,1024]{1,0:T(8,128)(2,1)S(1)} %add_convert_fusion.2), channel_id=1, source_target_pairs={{0,2},{1,3},{2,0},{3,1},{4,6},{5,7},{6,4},{7,5},{8,10},{9,11},{10,... | collective-permute-start | bytes 786440 | tf_op jit(solution)/shard_map/ppermute | solution.py:33
  34.1 14.5 %collective-permute-start.8 = (bf16[128,1024]{1,0:T(8,128)(2,1)S(1)}, bf16[128,1024]{1,0:T(8,128)(2,1)S(1)}, u32[]{:S(2)}, u32[]{:S(2)}) collective-permute-start(bf16[128,1024]{1,0:T(8,128)(2,1)S(1)} %get-tuple-element.64), channel_id=1, source_target_pairs={{0,1},{1,0},{2,3},{3,2},{4,5},{5,4},{6,7},{7,6},{8,9},{9,8},{10,11... | collective-permute-start | bytes 786440 | tf_op jit(solution)/shard_map/ppermute | solution.py:33
  39.1 14.1 %collective-permute-start.13 = (bf16[128,1024]{1,0:T(8,128)(2,1)S(1)}, bf16[128,1024]{1,0:T(8,128)(2,1)S(1)}, u32[]{:S(2)}, u32[]{:S(2)}) collective-permute-start(bf16[128,1024]{1,0:T(8,128)(2,1)S(1)} %add_convert_fusion.1), channel_id=1, source_target_pairs={{0,4},{1,5},{2,6},{3,7},{4,0},{5,1},{6,2},{7,3},{8,12},{9,13},{10,... | collective-permute-start | bytes 786440 | tf_op jit(solution)/shard_map/ppermute | solution.py:33
  53.6 9.3 %collective-permute-start.15 = (bf16[128,1024]{1,0:T(8,128)(2,1)S(1)}, bf16[128,1024]{1,0:T(8,128)(2,1)S(1)}, u32[]{:S(2)}, u32[]{:S(2)}) collective-permute-start(bf16[128,1024]{1,0:T(8,128)(2,1)S(1)} %multiply_convert_fusion.refs_0_), channel_id=1, source_target_pairs={{0,4},{1,5},{2,6},{3,7},{4,0},{5,1},{6,2},{7,3},{8,12},{9,13},{10,... | collective-permute-start | bytes 786440 | tf_op jit(solution)/shard_map/ppermute | solution.py:33
  53.7 15.8 %collective-permute-start.17 = (bf16[128,1024]{1,0:T(8,128)(2,1)S(1)}, bf16[128,1024]{1,0:T(8,128)(2,1)S(1)}, u32[]{:S(2)}, u32[]{:S(2)}) collective-permute-start(bf16[128,1024]{1,0:T(8,128)(2,1)S(1)} %multiply_convert_fusion.refs_0_), channel_id=1, source_target_pairs={{0,2},{1,3},{2,0},{3,1},{4,6},{5,7},{6,4},{7,5},{8,10},{9,11},{10,... | collective-permute-start | bytes 786440 | tf_op jit(solution)/shard_map/ppermute | solution.py:33
  62.9 6.5 %collective-permute-start.14 = (bf16[128,1024]{1,0:T(8,128)(2,1)S(1)}, bf16[128,1024]{1,0:T(8,128)(2,1)S(1)}, u32[]{:S(2)}, u32[]{:S(2)}) collective-permute-start(bf16[128,1024]{1,0:T(8,128)(2,1)S(1)} %multiply_convert_fusion.refs_0_), channel_id=1, source_target_pairs={{0,1},{1,0},{2,3},{3,2},{4,5},{5,4},{6,7},{7,6},{8,9},{9,8},{10,11... | collective-permute-start | bytes 786440 | tf_op jit(solution)/shard_map/ppermute | solution.py:33
  63.0 10.5 %collective-permute-start.16 = (bf16[128,1024]{1,0:T(8,128)(2,1)S(1)}, bf16[128,1024]{1,0:T(8,128)(2,1)S(1)}, u32[]{:S(2)}, u32[]{:S(2)}) collective-permute-start(bf16[128,1024]{1,0:T(8,128)(2,1)S(1)} %collective-permute-done.15.refs_0_), channel_id=1, source_target_pairs={{0,2},{1,3},{2,0},{3,1},{4,6},{5,7},{6,4},{7,5},{8,10},{9,11},{10,... | collective-permute-start | bytes 786440 | tf_op jit(solution)/shard_map/ppermute | solution.py:33
  68.2 3.9 %collective-permute-start.19 = (bf16[128,1024]{1,0:T(8,128)(2,1)S(1)}, bf16[128,1024]{1,0:T(8,128)(2,1)S(1)}, u32[]{:S(2)}, u32[]{:S(2)}) collective-permute-start(bf16[128,1024]{1,0:T(8,128)(2,1)S(1)} %collective-permute-done.15.refs_0_), channel_id=1, source_target_pairs={{0,1},{1,0},{2,3},{3,2},{4,5},{5,4},{6,7},{7,6},{8,9},{9,8},{10,11... | collective-permute-start | bytes 786440 | tf_op jit(solution)/shard_map/ppermute | solution.py:33
  69.5 1.5 %collective-permute-start.18 = (bf16[128,1024]{1,0:T(8,128)(2,1)S(1)}, bf16[128,1024]{1,0:T(8,128)(2,1)S(1)}, u32[]{:S(2)}, u32[]{:S(2)}) collective-permute-start(bf16[128,1024]{1,0:T(8,128)(2,1)S(1)} %collective-permute-done.17.refs_0_), channel_id=1, source_target_pairs={{0,1},{1,0},{2,3},{3,2},{4,5},{5,4},{6,7},{7,6},{8,9},{9,8},{10,11... | collective-permute-start | bytes 786440 | tf_op jit(solution)/shard_map/ppermute | solution.py:33
  73.4 1.6 %collective-permute-start.20 = (bf16[128,1024]{1,0:T(8,128)(2,1)S(1)}, bf16[128,1024]{1,0:T(8,128)(2,1)S(1)}, u32[]{:S(2)}, u32[]{:S(2)}) collective-permute-start(bf16[128,1024]{1,0:T(8,128)(2,1)S(1)} %collective-permute-done.16.refs_0_), channel_id=1, source_target_pairs={{0,1},{1,0},{2,3},{3,2},{4,5},{5,4},{6,7},{7,6},{8,9},{9,8},{10,11... | collective-permute-start | bytes 786440 | tf_op jit(solution)/shard_map/ppermute | solution.py:33
  77.2 1.7 %collective-permute-start.21 = (bf16[128,1024]{1,0:T(8,128)(2,1)S(1)}, bf16[128,1024]{1,0:T(8,128)(2,1)S(1)}, u32[]{:S(2)}, u32[]{:S(2)}) collective-permute-start(bf16[128,1024]{1,0:T(8,128)(2,1)S(1)} %get-tuple-element.82), channel_id=1, source_target_pairs={{0,1},{1,0},{2,3},{3,2},{4,5},{5,4},{6,7},{7,6},{8,9},{9,8},{10,11... | collective-permute-start | bytes 786440 | tf_op jit(solution)/shard_map/ppermute | solution.py:33
  78.4 5.2 %collective-permute-start.25 = (bf16[128,1024]{1,0:T(8,128)(2,1)S(1)}, bf16[128,1024]{1,0:T(8,128)(2,1)S(1)}, u32[]{:S(2)}, u32[]{:S(2)}) collective-permute-start(bf16[128,1024]{1,0:T(8,128)(2,1)S(1)} %get-tuple-element.96), channel_id=1, source_target_pairs={{0,1},{1,0},{2,3},{3,2},{4,5},{5,4},{6,7},{7,6},{8,9},{9,8},{10,11... | collective-permute-start | bytes 786440 | tf_op jit(solution)/shard_map/ppermute | solution.py:33
  78.9 9.6 %collective-permute-start.23 = (bf16[128,1024]{1,0:T(8,128)(2,1)S(1)}, bf16[128,1024]{1,0:T(8,128)(2,1)S(1)}, u32[]{:S(2)}, u32[]{:S(2)}) collective-permute-start(bf16[128,1024]{1,0:T(8,128)(2,1)S(1)} %convert_add_fusion.2), channel_id=1, source_target_pairs={{0,2},{1,3},{2,0},{3,1},{4,6},{5,7},{6,4},{7,5},{8,10},{9,11},{10,... | collective-permute-start | bytes 786440 | tf_op jit(solution)/shard_map/ppermute | solution.py:33
  82.5 6.1 %collective-permute-start.22 = (bf16[128,1024]{1,0:T(8,128)(2,1)S(1)}, bf16[128,1024]{1,0:T(8,128)(2,1)S(1)}, u32[]{:S(2)}, u32[]{:S(2)}) collective-permute-start(bf16[128,1024]{1,0:T(8,128)(2,1)S(1)} %get-tuple-element.88), channel_id=1, source_target_pairs={{0,1},{1,0},{2,3},{3,2},{4,5},{5,4},{6,7},{7,6},{8,9},{9,8},{10,11... | collective-permute-start | bytes 786440 | tf_op jit(solution)/shard_map/ppermute | solution.py:33
  83.6 14.6 %collective-permute-start.26 = (bf16[128,1024]{1,0:T(8,128)(2,1)S(1)}, bf16[128,1024]{1,0:T(8,128)(2,1)S(1)}, u32[]{:S(2)}, u32[]{:S(2)}) collective-permute-start(bf16[128,1024]{1,0:T(8,128)(2,1)S(1)} %add_convert_fusion), channel_id=1, source_target_pairs={{0,2},{1,3},{2,0},{3,1},{4,6},{5,7},{6,4},{7,5},{8,10},{9,11},{10,... | collective-permute-start | bytes 786440 | tf_op jit(solution)/shard_map/ppermute | solution.py:33
  88.7 14.0 %collective-permute-start.27 = (bf16[128,1024]{1,0:T(8,128)(2,1)S(1)}, bf16[128,1024]{1,0:T(8,128)(2,1)S(1)}, u32[]{:S(2)}, u32[]{:S(2)}) collective-permute-start(bf16[128,1024]{1,0:T(8,128)(2,1)S(1)} %convert_add_fusion.1), channel_id=1, source_target_pairs={{0,4},{1,5},{2,6},{3,7},{4,0},{5,1},{6,2},{7,3},{8,12},{9,13},{10,... | collective-permute-start | bytes 786440 | tf_op jit(solution)/shard_map/ppermute | solution.py:33
  97.4 5.3 %collective-permute-start.24 = (bf16[128,1024]{1,0:T(8,128)(2,1)S(1)}, bf16[128,1024]{1,0:T(8,128)(2,1)S(1)}, u32[]{:S(2)}, u32[]{:S(2)}) collective-permute-start(bf16[128,1024]{1,0:T(8,128)(2,1)S(1)} %get-tuple-element.93), channel_id=1, source_target_pairs={{0,1},{1,0},{2,3},{3,2},{4,5},{5,4},{6,7},{7,6},{8,9},{9,8},{10,11... | collective-permute-start | bytes 786440 | tf_op jit(solution)/shard_map/ppermute | solution.py:33

commit v3 on v2

--- a/solution.py
+++ b/solution.py
@@ -33,16 +33,10 @@
     return lax.ppermute(values, "shard", [(place, place ^ offset) for place in range(places)])
 
 
-def low_bit(number):
-    return number & -number
-
-
 def after(values, *others):
     return lax.optimization_barrier((values, others))[0]
 
 
-DIRECT_PART = 0
-GDIR = 0
 IN_VMEM = pl.BlockSpec(memory_space=pltpu.VMEM)
 IN_SMEM = pl.BlockSpec(memory_space=pltpu.SMEM)
 VMEM_ROOM = pltpu.CompilerParams(vmem_limit_bytes=24 << 20)
@@ -144,41 +138,36 @@
     )(*terms, *tables, factor)
 
 
+def low_bit(number):
+    return number & -number
+
+
+def offset(j):
+    return j ^ (j >> 1) ^ (j >> 2) ^ (j >> 3) ^ (j >> 4)
+
+
+def step(values, j):
+    return swap(values, 2 * offset(j))
+
+
 def bits_of(chips):
     return [1 << b for b in range(chips.bit_length() - 1)]
 
 
-def direct_rows(count):
-    return count // DIRECT_PART // 16 * 16 if DIRECT_PART else 0
-
-
 def gather_terms(own, unit, chips):
-    bits, cut = bits_of(chips), GDIR and direct_rows(own.shape[0])
-    beside = swap(own, 1)
-    near = swap(own, 2)
-    stepped = {0: own[cut:]}
-    for bit in reversed(bits):
-        for j in sorted(stepped):
-            if j ^ bit not in stepped and j ^ bit != 1:
-                stepped[j ^ bit] = swap(stepped[j], 2 * bit)
-    rows = {0: [own], 1: [near]}
-    for j in range(2, chips):
-        straight = [swap(after(own[:cut], beside), 2 * j)] if cut else []
-        rows[j] = [*straight, stepped[j]]
+    rows = {0: own}
+    for bit in reversed(bits_of(chips)):
+        for j in sorted(rows):
+            rows[j ^ bit] = step(rows[j], bit)
     tables, terms = {}, {}
     for j in range(chips):
-        if j:
-            held = after(rows[j][-1], *terms.values()) if j == chips - 1 else rows[j][-1]
-            others = [swap(r, 1) for r in (*rows[j][:-1], held)]
-        else:
-            others = [beside]
-        tables[j] = [*rows[j], *others]
+        held = after(rows[j], *terms.values()) if j == chips - 1 else rows[j]
+        tables[j] = [rows[j], swap(held, 1)]
         terms[j] = scores_of(tables[j], unit)
     return tables, terms
 
 
 def scatter_sums(terms, factor, unit, chips, beside):
-    bits = bits_of(chips)
     order = sorted(terms, key=lambda j: (low_bit(j) or chips, -j))
     kept, given, totals, gate = {}, {}, {}, ()
     for place, j in enumerate(order):
@@ -186,24 +175,17 @@
         if j:
             totals[j] = kept[j] + swap(given[j], 1).astype(jnp.float32)
         gate = (totals[order[0]],) if place else (given[j],)
-    cut = direct_rows(kept[0].shape[0])
-    straight = []
-    stepped = {j: totals[j][cut:] for j in totals if j > 1}
+    got = {}
     for j in order:
         if j > 1:
-            bit = low_bit(j)
-            if cut:
-                straight.append(swap(totals[j][:cut].astype(jnp.bfloat16), 2 * j))
-            gate = stepped[j]
-            got = swap(stepped[j].astype(jnp.bfloat16), 2 * bit).astype(jnp.float32)
-            stepped[j ^ bit] = stepped[j ^ bit] + got if j ^ bit else got
-    near = swap(after(totals[1].astype(jnp.bfloat16), given[0]), 2)
+            bit, gate = low_bit(j), totals[j]
+            got[j] = step(totals[j].astype(jnp.bfloat16), bit).astype(jnp.float32)
+            if j ^ bit:
+                totals[j ^ bit] = totals[j ^ bit] + got.pop(j)
+    near = step(after(totals[1].astype(jnp.bfloat16), given[0]), 1).astype(jnp.float32)
     done = beside(gate)
-    mine = kept[0] + swap(after(given[0], *done), 1).astype(jnp.float32) + near.astype(jnp.float32)
-    far = stepped[0]
-    if cut:
-        far = jnp.concatenate([sum(s.astype(jnp.float32) for s in straight), far])
-    return mine + far, done
+    mine = kept[0] + swap(after(given[0], *done), 1).astype(jnp.float32) + near
+    return mine + sum(got.values()), done
 
 
 def body(points, centroids, tile_counts):

time: 104 us -> 98 us (0.942)
  starting transfers between devices: 34.2 us -> 26.5 us
  waiting for transfers between devices: 38 us -> 39.7 us
    ppermute x28, starting transfers between devices: 34.2 us -> 26.5 us  [swap(): lax.ppermute(values, 'shard', [(place, place ^ offset) for place in range...]
    ppermute x28, waiting for transfers between devices: 38 us -> 39.7 us  [swap(): lax.ppermute(values, 'shard', [(place, place ^ offset) for place in range...]
  transfers between devices with their start and end apart: 28 -> 28, of which waited for: 14 -> 15; matrix products, arithmetic and copies ran while one was open for 5% -> 5% of each run, Pallas kernels for 18% -> 19%
where the time goes in v3:
time: 98 us; the launch traced here: 97.9 us
  waiting for transfers between devices  39.7 us (41%)
  starting transfers between devices  26.5 us (27%)
  Pallas kernels  23.2 us (24%)
  other arithmetic  6.78 us (7%)
  between operations  1.62 us (2%)
    ppermute x28, waiting for transfers between devices, swap(): lax.ppermute(values, 'shard', [(place, place ^ offset) for place in range...  39.7 us
    ppermute x28, starting transfers between devices, swap(): lax.ppermute(values, 'shard', [(place, place ^ offset) for place in range...  26.5 us
    pallas_call x16, Pallas kernels, local_call(): pl.pallas_call(kernel, out_shape=outs, in_specs=[IN_VMEM] * len(operands)...  16.9 us
    pallas_call x1, Pallas kernels, blend(): pl.pallas_call(functools.partial(blend_kernel, blocks), grid=(points // t...  5.64 us
    reduce_sum x3, other arithmetic, rms_unit(): jnp.mean(values * values, axis=-1, keepdims=True) + epsilon  3.17 us
  transfers between devices with their start and end apart: 28, of which 15 were waited for; matrix products, arithmetic and copies ran while one was open for 5% of the time, Pallas kernels for 19%

profile of v3, /device:TPU:0, one launch (start us, length us, event | category | flops | bytes accessed | tf_op | source)
XLA Modules:
  0.0 97.9 jit_solution(14030524757874802298)
XLA Ops:
  0.6 5.1 %collective-permute-start.1 = (bf16[128,1024]{1,0:T(8,128)(2,1)}, bf16[128,1024]{1,0:T(8,128)(2,1)S(1)}, u32[]{:S(2)}, u32[]{:S(2)}) collective-permute-start(bf16[128,1024]{1,0:T(8,128)(2,1)} %bitcast.6), channel_id=1, source_target_pairs={{0,6},{1,7},{2,4},{3,5},{4,2},{5,3},{6,0},{7,1},{8,14},{9,15},{10,... | collective-permute-start | bytes 786440 | tf_op jit(solution)/shard_map/ppermute | solution.py:33
  5.8 1.3 %fusion.2 = s32[]{:T(128)} fusion(s32[4]{0:T(128)} %param.5, s32[]{:T(128)S(6)} %axis_index.23), kind=kLoop, calls=%fused_computation.24 | loop fusion | flops 11 | bytes 24 | tf_op jit(solution)/shard_map/reduce_sum | solution.py:24
  7.7 0.6 live.1
  8.3 2.7 %fusion = f32[1536]{0:T(1024)S(1)} fusion(bf16[1536,1024]{1,0:T(8,128)(2,1)} %bitcast.10), kind=kLoop, calls=%fused_computation.2 | loop fusion | flops 4717056 | bytes 3151872 | tf_op jit(solution)/shard_map/reduce_sum | solution.py:19
  11.1 0.1 copy-done.1
  11.2 0.6 fusion.1.refs_2_.unit
  11.7 1.4 %collective-permute-done.1.refs_0_ = bf16[128,1024]{1,0:T(8,128)(2,1)S(1)} collective-permute-done((bf16[128,1024]{1,0:T(8,128)(2,1)}, bf16[128,1024]{1,0:T(8,128)(2,1)S(1)}, u32[]{:S(2)}, u32[]{:S(2)}) %collective-permute-start.1) | collective-permute-done | bytes 262176 | tf_op jit(solution)/shard_map/ppermute | solution.py:33
  13.1 4.4 %collective-permute-start.2 = (bf16[128,1024]{1,0:T(8,128)(2,1)S(1)}, bf16[128,1024]{1,0:T(8,128)(2,1)S(1)}, u32[]{:S(2)}, u32[]{:S(2)}) collective-permute-start(bf16[128,1024]{1,0:T(8,128)(2,1)S(1)} %collective-permute-done.1.refs_0_), channel_id=1, source_target_pairs={{0,2},{1,3},{2,0},{3,1},{4,6},{5,7},{6,4},{7,5},{8,10},{9,11},{10,... | collective-permute-start | bytes 786440 | tf_op jit(solution)/shard_map/ppermute | solution.py:33
  17.6 0.4 collective-permute-done.3.refs_0_
  18.0 0.1 collective-permute-start.4
  18.1 1.1 %scores.8 = (bf16[256,1536]{1,0:T(8,128)(2,1)S(1)}, f32[1,1536]{1,0:T(1,128)S(1)}) custom-call(bf16[128,1024]{1,0:T(8,128)(2,1)S(1)} %bitcast.9, bf16[128,1024]{1,0:T(8,128)(2,1)S(1)} %collective-permute-done.refs_1_, bf16[1536,1024]{1,0:T(8,128)(2,1)S(1)} %fusion.1.refs_2_.unit), custom_call_target="tpu_custom_call" | custom-call | flops 3221225472 | bytes 5242880 | tf_op jit(solution)/shard_map/scores/pallas_call | solution.py:52
  19.2 0.3 collective-permute-done.4.refs_1_
  19.6 1.1 %scores.9 = (bf16[256,1536]{1,0:T(8,128)(2,1)S(1)}, f32[1,1536]{1,0:T(1,128)S(1)}) custom-call(bf16[128,1024]{1,0:T(8,128)(2,1)S(1)} %collective-permute-done.3.refs_0_, bf16[128,1024]{1,0:T(8,128)(2,1)S(1)} %collective-permute-done.4.refs_1_, bf16[1536,1024]{1,0:T(8,128)(2,1)S(1)} %fusion.1.refs_2_.unit), custom_call_target="tpu_custom_call" | custom-call | flops 3221225472 | bytes 5242880 | tf_op jit(solution)/shard_map/scores/pallas_call | solution.py:52
  20.7 1.1 %scores.10 = (bf16[256,1536]{1,0:T(8,128)(2,1)S(1)}, f32[1,1536]{1,0:T(1,128)S(1)}) custom-call(bf16[128,1024]{1,0:T(8,128)(2,1)S(1)} %collective-permute-done.1.refs_0_, bf16[128,1024]{1,0:T(8,128)(2,1)S(1)} %collective-permute-done.5.refs_1_, bf16[1536,1024]{1,0:T(8,128)(2,1)S(1)} %fusion.1.refs_2_.unit), custom_call_target="tpu_custom_call" | custom-call | flops 3221225472 | bytes 5242880 | tf_op jit(solution)/shard_map/scores/pallas_call | solution.py:52
  21.8 1.8 %collective-permute-done.2.refs_0_ = bf16[128,1024]{1,0:T(8,128)(2,1)S(1)} collective-permute-done((bf16[128,1024]{1,0:T(8,128)(2,1)S(1)}, bf16[128,1024]{1,0:T(8,128)(2,1)S(1)}, u32[]{:S(2)}, u32[]{:S(2)}) %collective-permute-start.2) | collective-permute-done | bytes 262176 | tf_op jit(solution)/shard_map/ppermute | solution.py:33
  23.6 1.5 %collective-permute-done.6.refs_1_ = bf16[128,1024]{1,0:T(8,128)(2,1)S(1)} collective-permute-done((bf16[128,1024]{1,0:T(8,128)(2,1)S(1)}, bf16[128,1024]{1,0:T(8,128)(2,1)S(1)}, u32[]{:S(2)}, u32[]{:S(2)}) %collective-permute-start.6) | collective-permute-done | bytes 262176 | tf_op jit(solution)/shard_map/ppermute | solution.py:33
  25.1 1.1 %scores.11 = (bf16[256,1536]{1,0:T(8,128)(2,1)S(1)}, f32[1,1536]{1,0:T(1,128)S(1)}) custom-call(bf16[128,1024]{1,0:T(8,128)(2,1)S(1)} %collective-permute-done.2.refs_0_, bf16[128,1024]{1,0:T(8,128)(2,1)S(1)} %collective-permute-done.6.refs_1_, bf16[1536,1024]{1,0:T(8,128)(2,1)S(1)} %fusion.1.refs_2_.unit), custom_call_target="tpu_custom_call" | custom-call | flops 3221225472 | bytes 5242880 | tf_op jit(solution)/shard_map/scores/pallas_call | solution.py:52
  26.3 1.0 %sums.8 = (f32[128,1024]{1,0:T(8,128)S(1)}, bf16[128,1024]{1,0:T(8,128)(2,1)S(1)}) custom-call(bf16[256,1536]{1,0:T(8,128)(2,1)S(1)} %get-tuple-element.58.terms, f32[1,1536]{1,0:T(1,128)S(1)} %add_divide_fusion.1.factor, bf16[1536,1024]{1,0:T(8,128)(2,1)S(1)} %fusion.1.refs_2_.unit), custom_call_target="tpu_custom_call" | custom-call | flops 3221225472 | bytes 5242880 | tf_op jit(solution)/shard_map/sums/pallas_call | solution.py:52
  27.3 0.2 collective-permute-start.7
  27.5 1.0 %sums.10 = (f32[128,1024]{1,0:T(8,128)S(1)}, bf16[128,1024]{1,0:T(8,128)(2,1)S(1)}) custom-call(bf16[256,1536]{1,0:T(8,128)(2,1)S(1)} %get-tuple-element.65.terms, f32[1,1536]{1,0:T(1,128)S(1)} %add_divide_fusion.1.factor, bf16[1536,1024]{1,0:T(8,128)(2,1)S(1)} %fusion.1.refs_2_.unit), custom_call_target="tpu_custom_call" | custom-call | flops 3221225472 | bytes 5242880 | tf_op jit(solution)/shard_map/sums/pallas_call | solution.py:52
  28.5 0.4 collective-permute-start.9
  29.0 1.7 %collective-permute-start.12 = (bf16[128,1024]{1,0:T(8,128)(2,1)S(1)}, bf16[128,1024]{1,0:T(8,128)(2,1)S(1)}, u32[]{:S(2)}, u32[]{:S(2)}) collective-permute-start(bf16[128,1024]{1,0:T(8,128)(2,1)S(1)} %convert_add_fusion.4), channel_id=1, source_target_pairs={{0,2},{1,3},{2,0},{3,1},{4,6},{5,7},{6,4},{7,5},{8,10},{9,11},{10,... | collective-permute-start | bytes 786440 | tf_op jit(solution)/shard_map/ppermute | solution.py:33
  30.7 1.0 %sums.11 = (f32[128,1024]{1,0:T(8,128)S(1)}, bf16[128,1024]{1,0:T(8,128)(2,1)S(1)}) custom-call(bf16[256,1536]{1,0:T(8,128)(2,1)S(1)} %get-tuple-element.69.terms, f32[1,1536]{1,0:T(1,128)S(1)} %add_divide_fusion.1.factor, bf16[1536,1024]{1,0:T(8,128)(2,1)S(1)} %fusion.1.refs_2_.unit), custom_call_target="tpu_custom_call" | custom-call | flops 3221225472 | bytes 5242880 | tf_op jit(solution)/shard_map/sums/pallas_call | solution.py:52
  31.7 0.1 collective-permute-start.11
  31.8 1.0 %sums.9 = (f32[128,1024]{1,0:T(8,128)S(1)}, bf16[128,1024]{1,0:T(8,128)(2,1)S(1)}) custom-call(bf16[256,1536]{1,0:T(8,128)(2,1)S(1)} %get-tuple-element.62.terms, f32[1,1536]{1,0:T(1,128)S(1)} %add_divide_fusion.1.factor, bf16[1536,1024]{1,0:T(8,128)(2,1)S(1)} %fusion.1.refs_2_.unit), custom_call_target="tpu_custom_call" | custom-call | flops 3221225472 | bytes 5242880 | tf_op jit(solution)/shard_map/sums/pallas_call | solution.py:52
  32.8 0.1 add_convert_fusion.2
  32.9 0.4 collective-permute-start.10
  33.3 0.2 collective-permute-start.8
  33.5 4.7 %collective-permute-done.12 = bf16[128,1024]{1,0:T(8,128)(2,1)S(1)} collective-permute-done((bf16[128,1024]{1,0:T(8,128)(2,1)S(1)}, bf16[128,1024]{1,0:T(8,128)(2,1)S(1)}, u32[]{:S(2)}, u32[]{:S(2)}) %collective-permute-start.12) | collective-permute-done | bytes 262176 | tf_op jit(solution)/shard_map/ppermute | solution.py:33
  38.2 0.1 add_convert_fusion.1
  38.3 2.5 %collective-permute-start.13 = (bf16[128,1024]{1,0:T(8,128)(2,1)S(1)}, bf16[128,1024]{1,0:T(8,128)(2,1)S(1)}, u32[]{:S(2)}, u32[]{:S(2)}) collective-permute-start(bf16[128,1024]{1,0:T(8,128)(2,1)S(1)} %add_convert_fusion.1), channel_id=1, source_target_pairs={{0,6},{1,7},{2,4},{3,5},{4,2},{5,3},{6,0},{7,1},{8,14},{9,15},{10,... | collective-permute-start | bytes 786440 | tf_op jit(solution)/shard_map/ppermute | solution.py:33
  40.8 2.2 %collective-permute-done.10 = bf16[128,1024]{1,0:T(8,128)(2,1)S(1)} collective-permute-done((bf16[128,1024]{1,0:T(8,128)(2,1)S(1)}, bf16[128,1024]{1,0:T(8,128)(2,1)S(1)}, u32[]{:S(2)}, u32[]{:S(2)}) %collective-permute-start.10) | collective-permute-done | bytes 262176 | tf_op jit(solution)/shard_map/ppermute | solution.py:33
  43.0 7.3 %collective-permute-done.13 = bf16[128,1024]{1,0:T(8,128)(2,1)S(1)} collective-permute-done((bf16[128,1024]{1,0:T(8,128)(2,1)S(1)}, bf16[128,1024]{1,0:T(8,128)(2,1)S(1)}, u32[]{:S(2)}, u32[]{:S(2)}) %collective-permute-start.13) | collective-permute-done | bytes 262176 | tf_op jit(solution)/shard_map/ppermute | solution.py:33
  50.4 0.2 multiply_reduce_fusion.1
  50.6 0.2 multiply_convert_fusion.refs_0_
  50.7 1.9 %collective-permute-start.15 = (bf16[128,1024]{1,0:T(8,128)(2,1)S(1)}, bf16[128,1024]{1,0:T(8,128)(2,1)S(1)}, u32[]{:S(2)}, u32[]{:S(2)}) collective-permute-start(bf16[128,1024]{1,0:T(8,128)(2,1)S(1)} %multiply_convert_fusion.refs_0_), channel_id=1, source_target_pairs={{0,6},{1,7},{2,4},{3,5},{4,2},{5,3},{6,0},{7,1},{8,14},{9,15},{10,... | collective-permute-start | bytes 786440 | tf_op jit(solution)/shard_map/ppermute | solution.py:33
  52.7 2.7 %collective-permute-start.17 = (bf16[128,1024]{1,0:T(8,128)(2,1)S(1)}, bf16[128,1024]{1,0:T(8,128)(2,1)S(1)}, u32[]{:S(2)}, u32[]{:S(2)}) collective-permute-start(bf16[128,1024]{1,0:T(8,128)(2,1)S(1)} %multiply_convert_fusion.refs_0_), channel_id=1, source_target_pairs={{0,2},{1,3},{2,0},{3,1},{4,6},{5,7},{6,4},{7,5},{8,10},{9,11},{10,... | collective-permute-start | bytes 786440 | tf_op jit(solution)/shard_map/ppermute | solution.py:33
  55.4 6.4 %collective-permute-done.15.refs_0_ = bf16[128,1024]{1,0:T(8,128)(2,1)S(1)} collective-permute-done((bf16[128,1024]{1,0:T(8,128)(2,1)S(1)}, bf16[128,1024]{1,0:T(8,128)(2,1)S(1)}, u32[]{:S(2)}, u32[]{:S(2)}) %collective-permute-start.15) | collective-permute-done | bytes 262176 | tf_op jit(solution)/shard_map/ppermute | solution.py:33
  61.9 1.8 %collective-permute-start.16 = (bf16[128,1024]{1,0:T(8,128)(2,1)S(1)}, bf16[128,1024]{1,0:T(8,128)(2,1)S(1)}, u32[]{:S(2)}, u32[]{:S(2)}) collective-permute-start(bf16[128,1024]{1,0:T(8,128)(2,1)S(1)} %collective-permute-done.15.refs_0_), channel_id=1, source_target_pairs={{0,2},{1,3},{2,0},{3,1},{4,6},{5,7},{6,4},{7,5},{8,10},{9,11},{10,... | collective-permute-start | bytes 786440 | tf_op jit(solution)/shard_map/ppermute | solution.py:33
  63.6 2.3 %collective-permute-done.17.refs_0_ = bf16[128,1024]{1,0:T(8,128)(2,1)S(1)} collective-permute-done((bf16[128,1024]{1,0:T(8,128)(2,1)S(1)}, bf16[128,1024]{1,0:T(8,128)(2,1)S(1)}, u32[]{:S(2)}, u32[]{:S(2)}) %collective-permute-start.17) | collective-permute-done | bytes 262176 | tf_op jit(solution)/shard_map/ppermute | solution.py:33
  65.9 1.1 %scores.12 = (bf16[256,1536]{1,0:T(8,128)(2,1)S(1)}, f32[1,1536]{1,0:T(1,128)S(1)}) custom-call(bf16[128,1024]{1,0:T(8,128)(2,1)S(1)} %multiply_convert_fusion.refs_0_, bf16[128,1024]{1,0:T(8,128)(2,1)S(1)} %collective-permute-done.14.refs_1_, bf16[1536,1024]{1,0:T(8,128)(2,1)S(1)} %fusion.1.refs_2_.unit), custom_call_target="tpu_custom_call" | custom-call | flops 3221225472 | bytes 5242880 | tf_op jit(solution)/shard_map/scores/pallas_call | solution.py:52
  67.0 0.4 collective-permute-done.18.refs_1_
  67.4 1.1 %scores.13 = (bf16[256,1536]{1,0:T(8,128)(2,1)S(1)}, f32[1,1536]{1,0:T(1,128)S(1)}) custom-call(bf16[128,1024]{1,0:T(8,128)(2,1)S(1)} %collective-permute-done.17.refs_0_, bf16[128,1024]{1,0:T(8,128)(2,1)S(1)} %collective-permute-done.18.refs_1_, bf16[1536,1024]{1,0:T(8,128)(2,1)S(1)} %fusion.1.refs_2_.unit), custom_call_target="tpu_custom_call" | custom-call | flops 3221225472 | bytes 5242880 | tf_op jit(solution)/shard_map/scores/pallas_call | solution.py:52
  68.5 1.3 %scores.14 = (bf16[256,1536]{1,0:T(8,128)(2,1)S(1)}, f32[1,1536]{1,0:T(1,128)S(1)}) custom-call(bf16[128,1024]{1,0:T(8,128)(2,1)S(1)} %collective-permute-done.15.refs_0_, bf16[128,1024]{1,0:T(8,128)(2,1)S(1)} %collective-permute-done.19.refs_1_, bf16[1536,1024]{1,0:T(8,128)(2,1)S(1)} %fusion.1.refs_2_.unit), custom_call_target="tpu_custom_call" | custom-call | flops 3221225472 | bytes 5242880 | tf_op jit(solution)/shard_map/scores/pallas_call | solution.py:52
  69.8 1.3 %collective-permute-done.16.refs_0_ = bf16[128,1024]{1,0:T(8,128)(2,1)S(1)} collective-permute-done((bf16[128,1024]{1,0:T(8,128)(2,1)S(1)}, bf16[128,1024]{1,0:T(8,128)(2,1)S(1)}, u32[]{:S(2)}, u32[]{:S(2)}) %collective-permute-start.16) | collective-permute-done | bytes 262176 | tf_op jit(solution)/shard_map/ppermute | solution.py:33
  71.2 1.4 %collective-permute-done.20.refs_1_ = bf16[128,1024]{1,0:T(8,128)(2,1)S(1)} collective-permute-done((bf16[128,1024]{1,0:T(8,128)(2,1)S(1)}, bf16[128,1024]{1,0:T(8,128)(2,1)S(1)}, u32[]{:S(2)}, u32[]{:S(2)}) %collective-permute-start.20) | collective-permute-done | bytes 262176 | tf_op jit(solution)/shard_map/ppermute | solution.py:33
  72.6 1.1 %scores.15 = (bf16[256,1536]{1,0:T(8,128)(2,1)S(1)}, f32[1,1536]{1,0:T(1,128)S(1)}) custom-call(bf16[128,1024]{1,0:T(8,128)(2,1)S(1)} %collective-permute-done.16.refs_0_, bf16[128,1024]{1,0:T(8,128)(2,1)S(1)} %collective-permute-done.20.refs_1_, bf16[1536,1024]{1,0:T(8,128)(2,1)S(1)} %fusion.1.refs_2_.unit), custom_call_target="tpu_custom_call" | custom-call | flops 3221225472 | bytes 5242880 | tf_op jit(solution)/shard_map/scores/pallas_call | solution.py:52
  73.8 1.0 %sums.12 = (f32[128,1024]{1,0:T(8,128)S(1)}, bf16[128,1024]{1,0:T(8,128)(2,1)S(1)}) custom-call(bf16[256,1536]{1,0:T(8,128)(2,1)S(1)} %get-tuple-element.92.terms.refs_3_, f32[1,1536]{1,0:T(1,128)S(1)} %add_divide_fusion.factor.refs_8_, bf16[1536,1024]{1,0:T(8,128)(2,1)S(1)} %fusion.1.refs_2_.unit), custom_call_target="tpu_custom_call" | custom-call | flops 3221225472 | bytes 5242880 | tf_op jit(solution)/shard_map/sums/pallas_call | solution.py:52
  74.8 0.2 collective-permute-start.21
  75.0 1.0 %sums.15 = (f32[128,1024]{1,0:T(8,128)S(1)}, bf16[128,1024]{1,0:T(8,128)(2,1)S(1)}) custom-call(bf16[256,1536]{1,0:T(8,128)(2,1)S(1)} %get-tuple-element.90.refs_1_.terms, f32[1,1536]{1,0:T(1,128)S(1)} %add_divide_fusion.factor.refs_8_, bf16[1536,1024]{1,0:T(8,128)(2,1)S(1)} %fusion.1.refs_2_.unit), custom_call_target="tpu_custom_call" | custom-call | flops 3221225472 | bytes 5242880 | tf_op jit(solution)/shard_map/sums/pallas_call | solution.py:52
  76.0 0.4 collective-permute-start.25
  76.5 0.1 convert_add_fusion.2
  76.5 0.5 collective-permute-start.23
  77.1 1.0 %sums.14 = (f32[128,1024]{1,0:T(8,128)S(1)}, bf16[128,1024]{1,0:T(8,128)(2,1)S(1)}) custom-call(bf16[256,1536]{1,0:T(8,128)(2,1)S(1)} %get-tuple-element.91.terms.refs_2_, f32[1,1536]{1,0:T(1,128)S(1)} %add_divide_fusion.factor.refs_8_, bf16[1536,1024]{1,0:T(8,128)(2,1)S(1)} %fusion.1.refs_2_.unit), custom_call_target="tpu_custom_call" | custom-call | flops 3221225472 | bytes 5242880 | tf_op jit(solution)/shard_map/sums/pallas_call | solution.py:52
  78.1 0.1 collective-permute-start.22
  78.1 1.0 %sums.13 = (f32[128,1024]{1,0:T(8,128)S(1)}, bf16[128,1024]{1,0:T(8,128)(2,1)S(1)}) custom-call(bf16[256,1536]{1,0:T(8,128)(2,1)S(1)} %get-tuple-element.89.terms.refs_0_, f32[1,1536]{1,0:T(1,128)S(1)} %add_divide_fusion.factor.refs_8_, bf16[1536,1024]{1,0:T(8,128)(2,1)S(1)} %fusion.1.refs_2_.unit), custom_call_target="tpu_custom_call" | custom-call | flops 3221225472 | bytes 5242880 | tf_op jit(solution)/shard_map/sums/pallas_call | solution.py:52
  79.2 1.6 %collective-permute-start.26 = (bf16[128,1024]{1,0:T(8,128)(2,1)S(1)}, bf16[128,1024]{1,0:T(8,128)(2,1)S(1)}, u32[]{:S(2)}, u32[]{:S(2)}) collective-permute-start(bf16[128,1024]{1,0:T(8,128)(2,1)S(1)} %add_convert_fusion), channel_id=1, source_target_pairs={{0,2},{1,3},{2,0},{3,1},{4,6},{5,7},{6,4},{7,5},{8,10},{9,11},{10,... | collective-permute-start | bytes 786440 | tf_op jit(solution)/shard_map/ppermute | solution.py:33
  80.8 4.9 %collective-permute-done.23 = bf16[128,1024]{1,0:T(8,128)(2,1)S(1)} collective-permute-done((bf16[128,1024]{1,0:T(8,128)(2,1)S(1)}, bf16[128,1024]{1,0:T(8,128)(2,1)S(1)}, u32[]{:S(2)}, u32[]{:S(2)}) %collective-permute-start.23) | collective-permute-done | bytes 262176 | tf_op jit(solution)/shard_map/ppermute | solution.py:33
  85.7 0.1 convert_add_fusion.1
  85.9 2.0 %collective-permute-start.27 = (bf16[128,1024]{1,0:T(8,128)(2,1)S(1)}, bf16[128,1024]{1,0:T(8,128)(2,1)S(1)}, u32[]{:S(2)}, u32[]{:S(2)}) collective-permute-start(bf16[128,1024]{1,0:T(8,128)(2,1)S(1)} %convert_add_fusion.1), channel_id=1, source_target_pairs={{0,6},{1,7},{2,4},{3,5},{4,2},{5,3},{6,0},{7,1},{8,14},{9,15},{10,... | collective-permute-start | bytes 786440 | tf_op jit(solution)/shard_map/ppermute | solution.py:33
  87.9 5.6 %blend.1 = bf16[1536,1024]{1,0:T(8,128)(2,1)} custom-call(bf16[256,1536]{1,0:T(8,128)(2,1)S(1)} %get-tuple-element.89.terms.refs_0_, bf16[256,1536]{1,0:T(8,128)(2,1)S(1)} %get-tuple-element.90.refs_1_.terms, bf16[256,1536]{1,0:T(8,128)(2,1)S(1)} %get-tuple-element.91.terms.refs_2_, bf16[256,1536]{1,0:T(8,128)(2,1)S(1)} %get-tuple-element.92.terms.refs_3_, ...), custom_call_target="tpu_custom_call" | custom-call | flops 12884901888 | bytes 5242880 | tf_op jit(solution)/shard_map/blend/pallas_call | solution.py:127
  93.5 3.2 %collective-permute-done.27 = bf16[128,1024]{1,0:T(8,128)(2,1)S(1)} collective-permute-done((bf16[128,1024]{1,0:T(8,128)(2,1)S(1)}, bf16[128,1024]{1,0:T(8,128)(2,1)S(1)}, u32[]{:S(2)}, u32[]{:S(2)}) %collective-permute-start.27) | collective-permute-done | bytes 262176 | tf_op jit(solution)/shard_map/ppermute | solution.py:33
  96.7 0.2 multiply_reduce_fusion
  96.9 0.9 multiply_bitcast_fusion
  (38 shorter events, 0.4 us)
Async XLA Ops:
  0.6 12.5 %collective-permute-start.1 = (bf16[128,1024]{1,0:T(8,128)(2,1)}, bf16[128,1024]{1,0:T(8,128)(2,1)S(1)}, u32[]{:S(2)}, u32[]{:S(2)}) collective-permute-start(bf16[128,1024]{1,0:T(8,128)(2,1)} %bitcast.6), channel_id=1, source_target_pairs={{0,6},{1,7},{2,4},{3,5},{4,2},{5,3},{6,0},{7,1},{8,14},{9,15},{10,... | collective-permute-start | bytes 786440 | tf_op jit(solution)/shard_map/ppermute | solution.py:33
  5.7 12.4 %collective-permute-start = (bf16[128,1024]{1,0:T(8,128)(2,1)}, bf16[128,1024]{1,0:T(8,128)(2,1)S(1)}, u32[]{:S(2)}, u32[]{:S(2)}) collective-permute-start(bf16[128,1024]{1,0:T(8,128)(2,1)} %bitcast.7), channel_id=1, source_target_pairs={{0,1},{1,0},{2,3},{3,2},{4,5},{5,4},{6,7},{7,6},{8,9},{9,8},{10,11... | collective-permute-start | bytes 786440 | tf_op jit(solution)/shard_map/ppermute | solution.py:33
  5.7 12.3 %collective-permute-start.3 = (bf16[128,1024]{1,0:T(8,128)(2,1)}, bf16[128,1024]{1,0:T(8,128)(2,1)S(1)}, u32[]{:S(2)}, u32[]{:S(2)}) collective-permute-start(bf16[128,1024]{1,0:T(8,128)(2,1)} %bitcast.8), channel_id=1, source_target_pairs={{0,2},{1,3},{2,0},{3,1},{4,6},{5,7},{6,4},{7,5},{8,10},{9,11},{10,... | collective-permute-start | bytes 786440 | tf_op jit(solution)/shard_map/ppermute | solution.py:33
  8.3 2.8 %copy-start.1 = (bf16[1,1536,1024]{2,1,0:T(8,128)(2,1)S(1)}, bf16[1,1536,1024]{2,1,0:T(8,128)(2,1)}, u32[]{:S(2)}) copy-start(bf16[1,1536,1024]{2,1,0:T(8,128)(2,1)} %param.3) | copy-start | bytes 9437188
  11.2 7.0 %copy-start = (bf16[1,128,1024]{2,1,0:T(8,128)(2,1)S(1)}, bf16[1,128,1024]{2,1,0:T(8,128)(2,1)}, u32[]{:S(2)}) copy-start(bf16[1,128,1024]{2,1,0:T(8,128)(2,1)} %param.4) | copy-start | bytes 786436
  13.1 10.5 %collective-permute-start.2 = (bf16[128,1024]{1,0:T(8,128)(2,1)S(1)}, bf16[128,1024]{1,0:T(8,128)(2,1)S(1)}, u32[]{:S(2)}, u32[]{:S(2)}) collective-permute-start(bf16[128,1024]{1,0:T(8,128)(2,1)S(1)} %collective-permute-done.1.refs_0_), channel_id=1, source_target_pairs={{0,2},{1,3},{2,0},{3,1},{4,6},{5,7},{6,4},{7,5},{8,10},{9,11},{10,... | collective-permute-start | bytes 786440 | tf_op jit(solution)/shard_map/ppermute | solution.py:33
  17.6 3.1 %collective-permute-start.5 = (bf16[128,1024]{1,0:T(8,128)(2,1)S(1)}, bf16[128,1024]{1,0:T(8,128)(2,1)S(1)}, u32[]{:S(2)}, u32[]{:S(2)}) collective-permute-start(bf16[128,1024]{1,0:T(8,128)(2,1)S(1)} %collective-permute-done.1.refs_0_), channel_id=1, source_target_pairs={{0,1},{1,0},{2,3},{3,2},{4,5},{5,4},{6,7},{7,6},{8,9},{9,8},{10,11... | collective-permute-start | bytes 786440 | tf_op jit(solution)/shard_map/ppermute | solution.py:33
  18.0 1.5 %collective-permute-start.4 = (bf16[128,1024]{1,0:T(8,128)(2,1)S(1)}, bf16[128,1024]{1,0:T(8,128)(2,1)S(1)}, u32[]{:S(2)}, u32[]{:S(2)}) collective-permute-start(bf16[128,1024]{1,0:T(8,128)(2,1)S(1)} %collective-permute-done.3.refs_0_), channel_id=1, source_target_pairs={{0,1},{1,0},{2,3},{3,2},{4,5},{5,4},{6,7},{7,6},{8,9},{9,8},{10,11... | collective-permute-start | bytes 786440 | tf_op jit(solution)/shard_map/ppermute | solution.py:33
  23.6 2.6 %copy-start.2 = (f32[1,1536]{1,0:T(1,128)S(1)}, f32[1,1536]{1,0:T(1,128)}, u32[]{:S(2)}) copy-start(f32[1,1536]{1,0:T(1,128)} %live.1) | copy-start | bytes 18436
  23.6 1.5 %collective-permute-start.6 = (bf16[128,1024]{1,0:T(8,128)(2,1)S(1)}, bf16[128,1024]{1,0:T(8,128)(2,1)S(1)}, u32[]{:S(2)}, u32[]{:S(2)}) collective-permute-start(bf16[128,1024]{1,0:T(8,128)(2,1)S(1)} %collective-permute-done.2.refs_0_), channel_id=1, source_target_pairs={{0,1},{1,0},{2,3},{3,2},{4,5},{5,4},{6,7},{7,6},{8,9},{9,8},{10,11... | collective-permute-start | bytes 786440 | tf_op jit(solution)/shard_map/ppermute | solution.py:33
  27.3 1.6 %collective-permute-start.7 = (bf16[128,1024]{1,0:T(8,128)(2,1)S(1)}, bf16[128,1024]{1,0:T(8,128)(2,1)S(1)}, u32[]{:S(2)}, u32[]{:S(2)}) collective-permute-start(bf16[128,1024]{1,0:T(8,128)(2,1)S(1)} %get-tuple-element.61), channel_id=1, source_target_pairs={{0,1},{1,0},{2,3},{3,2},{4,5},{5,4},{6,7},{7,6},{8,9},{9,8},{10,11... | collective-permute-start | bytes 786440 | tf_op jit(solution)/shard_map/ppermute | solution.py:33
  28.5 4.3 %collective-permute-start.9 = (bf16[128,1024]{1,0:T(8,128)(2,1)S(1)}, bf16[128,1024]{1,0:T(8,128)(2,1)S(1)}, u32[]{:S(2)}, u32[]{:S(2)}) collective-permute-start(bf16[128,1024]{1,0:T(8,128)(2,1)S(1)} %get-tuple-element.67), channel_id=1, source_target_pairs={{0,1},{1,0},{2,3},{3,2},{4,5},{5,4},{6,7},{7,6},{8,9},{9,8},{10,11... | collective-permute-start | bytes 786440 | tf_op jit(solution)/shard_map/ppermute | solution.py:33
  29.0 9.2 %collective-permute-start.12 = (bf16[128,1024]{1,0:T(8,128)(2,1)S(1)}, bf16[128,1024]{1,0:T(8,128)(2,1)S(1)}, u32[]{:S(2)}, u32[]{:S(2)}) collective-permute-start(bf16[128,1024]{1,0:T(8,128)(2,1)S(1)} %convert_add_fusion.4), channel_id=1, source_target_pairs={{0,2},{1,3},{2,0},{3,1},{4,6},{5,7},{6,4},{7,5},{8,10},{9,11},{10,... | collective-permute-start | bytes 786440 | tf_op jit(solution)/shard_map/ppermute | solution.py:33
  31.7 6.5 %collective-permute-start.11 = (bf16[128,1024]{1,0:T(8,128)(2,1)S(1)}, bf16[128,1024]{1,0:T(8,128)(2,1)S(1)}, u32[]{:S(2)}, u32[]{:S(2)}) collective-permute-start(bf16[128,1024]{1,0:T(8,128)(2,1)S(1)} %get-tuple-element.71), channel_id=1, source_target_pairs={{0,1},{1,0},{2,3},{3,2},{4,5},{5,4},{6,7},{7,6},{8,9},{9,8},{10,11... | collective-permute-start | bytes 786440 | tf_op jit(solution)/shard_map/ppermute | solution.py:33
  32.9 10.1 %collective-permute-start.10 = (bf16[128,1024]{1,0:T(8,128)(2,1)S(1)}, bf16[128,1024]{1,0:T(8,128)(2,1)S(1)}, u32[]{:S(2)}, u32[]{:S(2)}) collective-permute-start(bf16[128,1024]{1,0:T(8,128)(2,1)S(1)} %add_convert_fusion.2), channel_id=1, source_target_pairs={{0,2},{1,3},{2,0},{3,1},{4,6},{5,7},{6,4},{7,5},{8,10},{9,11},{10,... | collective-permute-start | bytes 786440 | tf_op jit(solution)/shard_map/ppermute | solution.py:33
  33.3 9.7 %collective-permute-start.8 = (bf16[128,1024]{1,0:T(8,128)(2,1)S(1)}, bf16[128,1024]{1,0:T(8,128)(2,1)S(1)}, u32[]{:S(2)}, u32[]{:S(2)}) collective-permute-start(bf16[128,1024]{1,0:T(8,128)(2,1)S(1)} %get-tuple-element.64), channel_id=1, source_target_pairs={{0,1},{1,0},{2,3},{3,2},{4,5},{5,4},{6,7},{7,6},{8,9},{9,8},{10,11... | collective-permute-start | bytes 786440 | tf_op jit(solution)/shard_map/ppermute | solution.py:33
  38.3 12.0 %collective-permute-start.13 = (bf16[128,1024]{1,0:T(8,128)(2,1)S(1)}, bf16[128,1024]{1,0:T(8,128)(2,1)S(1)}, u32[]{:S(2)}, u32[]{:S(2)}) collective-permute-start(bf16[128,1024]{1,0:T(8,128)(2,1)S(1)} %add_convert_fusion.1), channel_id=1, source_target_pairs={{0,6},{1,7},{2,4},{3,5},{4,2},{5,3},{6,0},{7,1},{8,14},{9,15},{10,... | collective-permute-start | bytes 786440 | tf_op jit(solution)/shard_map/ppermute | solution.py:33
  50.7 11.1 %collective-permute-start.15 = (bf16[128,1024]{1,0:T(8,128)(2,1)S(1)}, bf16[128,1024]{1,0:T(8,128)(2,1)S(1)}, u32[]{:S(2)}, u32[]{:S(2)}) collective-permute-start(bf16[128,1024]{1,0:T(8,128)(2,1)S(1)} %multiply_convert_fusion.refs_0_), channel_id=1, source_target_pairs={{0,6},{1,7},{2,4},{3,5},{4,2},{5,3},{6,0},{7,1},{8,14},{9,15},{10,... | collective-permute-start | bytes 786440 | tf_op jit(solution)/shard_map/ppermute | solution.py:33
  52.7 13.2 %collective-permute-start.17 = (bf16[128,1024]{1,0:T(8,128)(2,1)S(1)}, bf16[128,1024]{1,0:T(8,128)(2,1)S(1)}, u32[]{:S(2)}, u32[]{:S(2)}) collective-permute-start(bf16[128,1024]{1,0:T(8,128)(2,1)S(1)} %multiply_convert_fusion.refs_0_), channel_id=1, source_target_pairs={{0,2},{1,3},{2,0},{3,1},{4,6},{5,7},{6,4},{7,5},{8,10},{9,11},{10,... | collective-permute-start | bytes 786440 | tf_op jit(solution)/shard_map/ppermute | solution.py:33
  55.4 10.5 %collective-permute-start.14 = (bf16[128,1024]{1,0:T(8,128)(2,1)S(1)}, bf16[128,1024]{1,0:T(8,128)(2,1)S(1)}, u32[]{:S(2)}, u32[]{:S(2)}) collective-permute-start(bf16[128,1024]{1,0:T(8,128)(2,1)S(1)} %multiply_convert_fusion.refs_0_), channel_id=1, source_target_pairs={{0,1},{1,0},{2,3},{3,2},{4,5},{5,4},{6,7},{7,6},{8,9},{9,8},{10,11... | collective-permute-start | bytes 786440 | tf_op jit(solution)/shard_map/ppermute | solution.py:33
  61.9 9.2 %collective-permute-start.16 = (bf16[128,1024]{1,0:T(8,128)(2,1)S(1)}, bf16[128,1024]{1,0:T(8,128)(2,1)S(1)}, u32[]{:S(2)}, u32[]{:S(2)}) collective-permute-start(bf16[128,1024]{1,0:T(8,128)(2,1)S(1)} %collective-permute-done.15.refs_0_), channel_id=1, source_target_pairs={{0,2},{1,3},{2,0},{3,1},{4,6},{5,7},{6,4},{7,5},{8,10},{9,11},{10,... | collective-permute-start | bytes 786440 | tf_op jit(solution)/shard_map/ppermute | solution.py:33
  63.6 4.9 %collective-permute-start.19 = (bf16[128,1024]{1,0:T(8,128)(2,1)S(1)}, bf16[128,1024]{1,0:T(8,128)(2,1)S(1)}, u32[]{:S(2)}, u32[]{:S(2)}) collective-permute-start(bf16[128,1024]{1,0:T(8,128)(2,1)S(1)} %collective-permute-done.15.refs_0_), channel_id=1, source_target_pairs={{0,1},{1,0},{2,3},{3,2},{4,5},{5,4},{6,7},{7,6},{8,9},{9,8},{10,11... | collective-permute-start | bytes 786440 | tf_op jit(solution)/shard_map/ppermute | solution.py:33
  65.9 1.5 %collective-permute-start.18 = (bf16[128,1024]{1,0:T(8,128)(2,1)S(1)}, bf16[128,1024]{1,0:T(8,128)(2,1)S(1)}, u32[]{:S(2)}, u32[]{:S(2)}) collective-permute-start(bf16[128,1024]{1,0:T(8,128)(2,1)S(1)} %collective-permute-done.17.refs_0_), channel_id=1, source_target_pairs={{0,1},{1,0},{2,3},{3,2},{4,5},{5,4},{6,7},{7,6},{8,9},{9,8},{10,11... | collective-permute-start | bytes 786440 | tf_op jit(solution)/shard_map/ppermute | solution.py:33
  71.1 1.5 %collective-permute-start.20 = (bf16[128,1024]{1,0:T(8,128)(2,1)S(1)}, bf16[128,1024]{1,0:T(8,128)(2,1)S(1)}, u32[]{:S(2)}, u32[]{:S(2)}) collective-permute-start(bf16[128,1024]{1,0:T(8,128)(2,1)S(1)} %collective-permute-done.16.refs_0_), channel_id=1, source_target_pairs={{0,1},{1,0},{2,3},{3,2},{4,5},{5,4},{6,7},{7,6},{8,9},{9,8},{10,11... | collective-permute-start | bytes 786440 | tf_op jit(solution)/shard_map/ppermute | solution.py:33
  74.8 1.7 %collective-permute-start.21 = (bf16[128,1024]{1,0:T(8,128)(2,1)S(1)}, bf16[128,1024]{1,0:T(8,128)(2,1)S(1)}, u32[]{:S(2)}, u32[]{:S(2)}) collective-permute-start(bf16[128,1024]{1,0:T(8,128)(2,1)S(1)} %get-tuple-element.82), channel_id=1, source_target_pairs={{0,1},{1,0},{2,3},{3,2},{4,5},{5,4},{6,7},{7,6},{8,9},{9,8},{10,11... | collective-permute-start | bytes 786440 | tf_op jit(solution)/shard_map/ppermute | solution.py:33
  76.0 3.2 %collective-permute-start.25 = (bf16[128,1024]{1,0:T(8,128)(2,1)S(1)}, bf16[128,1024]{1,0:T(8,128)(2,1)S(1)}, u32[]{:S(2)}, u32[]{:S(2)}) collective-permute-start(bf16[128,1024]{1,0:T(8,128)(2,1)S(1)} %get-tuple-element.96), channel_id=1, source_target_pairs={{0,1},{1,0},{2,3},{3,2},{4,5},{5,4},{6,7},{7,6},{8,9},{9,8},{10,11... | collective-permute-start | bytes 786440 | tf_op jit(solution)/shard_map/ppermute | solution.py:33
  76.5 9.2 %collective-permute-start.23 = (bf16[128,1024]{1,0:T(8,128)(2,1)S(1)}, bf16[128,1024]{1,0:T(8,128)(2,1)S(1)}, u32[]{:S(2)}, u32[]{:S(2)}) collective-permute-start(bf16[128,1024]{1,0:T(8,128)(2,1)S(1)} %convert_add_fusion.2), channel_id=1, source_target_pairs={{0,2},{1,3},{2,0},{3,1},{4,6},{5,7},{6,4},{7,5},{8,10},{9,11},{10,... | collective-permute-start | bytes 786440 | tf_op jit(solution)/shard_map/ppermute | solution.py:33
  78.1 7.7 %collective-permute-start.22 = (bf16[128,1024]{1,0:T(8,128)(2,1)S(1)}, bf16[128,1024]{1,0:T(8,128)(2,1)S(1)}, u32[]{:S(2)}, u32[]{:S(2)}) collective-permute-start(bf16[128,1024]{1,0:T(8,128)(2,1)S(1)} %get-tuple-element.88), channel_id=1, source_target_pairs={{0,1},{1,0},{2,3},{3,2},{4,5},{5,4},{6,7},{7,6},{8,9},{9,8},{10,11... | collective-permute-start | bytes 786440 | tf_op jit(solution)/shard_map/ppermute | solution.py:33
  79.2 14.3 %collective-permute-start.26 = (bf16[128,1024]{1,0:T(8,128)(2,1)S(1)}, bf16[128,1024]{1,0:T(8,128)(2,1)S(1)}, u32[]{:S(2)}, u32[]{:S(2)}) collective-permute-start(bf16[128,1024]{1,0:T(8,128)(2,1)S(1)} %add_convert_fusion), channel_id=1, source_target_pairs={{0,2},{1,3},{2,0},{3,1},{4,6},{5,7},{6,4},{7,5},{8,10},{9,11},{10,... | collective-permute-start | bytes 786440 | tf_op jit(solution)/shard_map/ppermute | solution.py:33
  85.9 10.8 %collective-permute-start.27 = (bf16[128,1024]{1,0:T(8,128)(2,1)S(1)}, bf16[128,1024]{1,0:T(8,128)(2,1)S(1)}, u32[]{:S(2)}, u32[]{:S(2)}) collective-permute-start(bf16[128,1024]{1,0:T(8,128)(2,1)S(1)} %convert_add_fusion.1), channel_id=1, source_target_pairs={{0,6},{1,7},{2,4},{3,5},{4,2},{5,3},{6,0},{7,1},{8,14},{9,15},{10,... | collective-permute-start | bytes 786440 | tf_op jit(solution)/shard_map/ppermute | solution.py:33
  93.5 3.2 %collective-permute-start.24 = (bf16[128,1024]{1,0:T(8,128)(2,1)S(1)}, bf16[128,1024]{1,0:T(8,128)(2,1)S(1)}, u32[]{:S(2)}, u32[]{:S(2)}) collective-permute-start(bf16[128,1024]{1,0:T(8,128)(2,1)S(1)} %get-tuple-element.93), channel_id=1, source_target_pairs={{0,1},{1,0},{2,3},{3,2},{4,5},{5,4},{6,7},{7,6},{8,9},{9,8},{10,11... | collective-permute-start | bytes 786440 | tf_op jit(solution)/shard_map/ppermute | solution.py:33

commit v4 on v3

--- a/solution.py
+++ b/solution.py
@@ -82,14 +82,14 @@
         table, unit[...], (((1,), (1,)), ((), ())), preferred_element_type=jnp.float32
     )
     raised = jnp.exp(scores * (sharpness_factor / unit.shape[1]))
-    terms[...] = raised.astype(jnp.bfloat16)
+    terms[...] = raised
     normal[...] = jnp.sum(raised, axis=0, keepdims=True)
 
 
 def scores_of(rows, unit):
     count, points = sum(r.shape[0] for r in rows), unit.shape[0]
     outs = [
-        jax.ShapeDtypeStruct((count, points), jnp.bfloat16),
+        jax.ShapeDtypeStruct((count, points), jnp.float32),
         jax.ShapeDtypeStruct((1, points), jnp.float32),
     ]
     return local_call(scores_kernel, "scores", outs, [*rows, unit])
@@ -97,7 +97,7 @@
 
 def sums_kernel(terms, factor, unit, kept, given):
     half = kept.shape[0]
-    weights = (terms[...].astype(jnp.float32) * factor[...]).astype(jnp.bfloat16)
+    weights = (terms[...] * factor[...]).astype(jnp.bfloat16)
     sums = jnp.dot(weights, unit[...], preferred_element_type=jnp.float32)
     kept[...] = sums[:half]
     given[...] = sums[half:].astype(jnp.bfloat16)
@@ -109,11 +109,41 @@
     return local_call(sums_kernel, "sums", outs, [terms, factor, unit])
 
 
+def last_kernel(blocks, own_rows, other_rows, unit, live, *refs):
+    *refs, factor, kept, given = refs
+    normals, kept_terms = refs[:blocks], refs[blocks:]
+    half = kept.shape[0]
+    table = jnp.concatenate([own_rows[...], other_rows[...]], axis=0)
+    scores = lax.dot_general(
+        table, unit[...], (((1,), (1,)), ((), ())), preferred_element_type=jnp.float32
+    )
+    raised = jnp.exp(scores * (sharpness_factor / unit.shape[1]))
+    for terms in kept_terms:
+        terms[...] = raised
+    normal = jnp.sum(raised, axis=0, keepdims=True) + sum(n[...] for n in normals)
+    scale = live[...] / normal
+    factor[...] = scale
+    sums = jnp.dot((raised * scale).astype(jnp.bfloat16), unit[...], preferred_element_type=jnp.float32)
+    kept[...] = sums[:half]
+    given[...] = sums[half:].astype(jnp.bfloat16)
+
+
+def last_block(rows, unit, live, normals, with_terms):
+    own, points = rows[0].shape, unit.shape[0]
+    outs = [jax.ShapeDtypeStruct((2 * own[0], points), jnp.float32)] * with_terms + [
+        jax.ShapeDtypeStruct((1, points), jnp.float32),
+        jax.ShapeDtypeStruct(own, jnp.float32),
+        jax.ShapeDtypeStruct(own, jnp.bfloat16),
+    ]
+    kernel = functools.partial(last_kernel, len(normals))
+    return local_call(kernel, "last", outs, [*rows, unit, live, *normals], 4)
+
+
 def blend_kernel(blocks, *refs):
     terms, tables, factor, out = refs[:blocks], refs[blocks:-2], refs[-2], refs[-1]
     total = jnp.zeros(out.shape, jnp.float32)
     for block, table in zip(terms, tables):
-        weights = (block[...].astype(jnp.float32) * factor[...]).astype(jnp.bfloat16)
+        weights = (block[...] * factor[...]).astype(jnp.bfloat16)
         total = total + lax.dot_general(
             weights, table[...], (((0,), (0,)), ((), ())), preferred_element_type=jnp.float32
         )
@@ -163,15 +193,19 @@
     for j in range(chips):
         held = after(rows[j], *terms.values()) if j == chips - 1 else rows[j]
         tables[j] = [rows[j], swap(held, 1)]
-        terms[j] = scores_of(tables[j], unit)
+        if j < chips - 1:
+            terms[j] = scores_of(tables[j], unit)
     return tables, terms
 
 
-def scatter_sums(terms, factor, unit, chips, beside):
-    order = sorted(terms, key=lambda j: (low_bit(j) or chips, -j))
+def scatter_sums(terms, factor, first, unit, chips, beside):
+    order = sorted(range(chips), key=lambda j: (low_bit(j) or chips, -j))
     kept, given, totals, gate = {}, {}, {}, ()
     for place, j in enumerate(order):
-        kept[j], given[j] = sums_of(after(terms[j], *gate), factor, unit)
+        if place:
+            kept[j], given[j] = sums_of(after(terms[j], *gate), factor, unit)
+        else:
+            kept[j], given[j] = first
         if j:
             totals[j] = kept[j] + swap(given[j], 1).astype(jnp.float32)
         gate = (totals[order[0]],) if place else (given[j],)
@@ -203,17 +237,21 @@
     for iteration in range(ITERS):
         tables, scored = gather_terms(current, unit, chips)
         terms = {j: scored[j][0] for j in scored}
-        factor = live / sum(scored[j][1] for j in sorted(scored))
+        normals = [scored[j][1] for j in sorted(scored)]
+        is_last = iteration == ITERS - 1
+        *kept_terms, factor, kept, given = last_block(tables[chips - 1], unit, live, normals, is_last)
+        if is_last:
+            terms[chips - 1] = kept_terms[0]
 
         def posterior(gate):
-            if iteration < ITERS - 1:
+            if not is_last:
                 return ()
             blocks = sorted(tables)
             return (
                 blend([after(terms[j], gate) for j in blocks], [tables[j] for j in blocks], factor, 2 * TILE),
             )
 
-        reduced, out_rows = scatter_sums(terms, factor, unit, chips, posterior)
+        reduced, out_rows = scatter_sums(terms, factor, (kept, given), unit, chips, posterior)
         updated = rms_unit(reduced)
         current = updated.astype(jnp.bfloat16)
     return (updated[None], out_rows[0][None])

time: 98 us -> 97.4 us (level)
    pallas_call x16 -> x14, Pallas kernels: 16.9 us -> 16.2 us  [local_call(): pl.pallas_call(kernel, out_shape=outs, in_specs=[IN_VMEM] * len(operands)...]
where the time goes in v4:
time: 97.4 us; the launch traced here: 97.3 us
  waiting for transfers between devices  39.6 us (41%)
  starting transfers between devices  26.5 us (27%)
  Pallas kernels  22.7 us (23%)
  other arithmetic  6.76 us (7%)
  between operations  1.59 us (2%)
    ppermute x28, waiting for transfers between devices, swap(): lax.ppermute(values, 'shard', [(place, place ^ offset) for place in range...  39.6 us
    ppermute x28, starting transfers between devices, swap(): lax.ppermute(values, 'shard', [(place, place ^ offset) for place in range...  26.5 us
    pallas_call x14, Pallas kernels, local_call(): pl.pallas_call(kernel, out_shape=outs, in_specs=[IN_VMEM] * len(operands)...  16.2 us
    pallas_call x1, Pallas kernels, blend(): pl.pallas_call(functools.partial(blend_kernel, blocks), grid=(points // t...  5.83 us
    reduce_sum x3, other arithmetic, rms_unit(): jnp.mean(values * values, axis=-1, keepdims=True) + epsilon  3.16 us
  transfers between devices with their start and end apart: 28, of which 15 were waited for; matrix products, arithmetic and copies ran while one was open for 5% of the time, Pallas kernels for 19%

profile of v4, /device:TPU:0, one launch (start us, length us, event | category | flops | bytes accessed | tf_op | source)
XLA Modules:
  0.0 97.3 jit_solution(12987976195213069461)
XLA Ops:
  0.6 5.1 %collective-permute-start.1 = (bf16[128,1024]{1,0:T(8,128)(2,1)}, bf16[128,1024]{1,0:T(8,128)(2,1)S(1)}, u32[]{:S(2)}, u32[]{:S(2)}) collective-permute-start(bf16[128,1024]{1,0:T(8,128)(2,1)} %bitcast.6), channel_id=1, source_target_pairs={{0,6},{1,7},{2,4},{3,5},{4,2},{5,3},{6,0},{7,1},{8,14},{9,15},{10,... | collective-permute-start | bytes 786440 | tf_op jit(solution)/shard_map/ppermute | solution.py:33
  5.8 1.3 %fusion.2 = s32[]{:T(128)} fusion(s32[4]{0:T(128)} %param.5, s32[]{:T(128)S(6)} %axis_index.23), kind=kLoop, calls=%fused_computation.22 | loop fusion | flops 11 | bytes 24 | tf_op jit(solution)/shard_map/reduce_sum | solution.py:24
  7.7 0.6 live.1
  8.3 2.7 %fusion = f32[1536]{0:T(1024)S(1)} fusion(bf16[1536,1024]{1,0:T(8,128)(2,1)} %bitcast.10), kind=kLoop, calls=%fused_computation.2 | loop fusion | flops 4717056 | bytes 3151872 | tf_op jit(solution)/shard_map/reduce_sum | solution.py:19
  11.1 0.1 copy-done.2
  11.2 0.6 fusion.1.refs_2_.unit
  11.7 1.4 %collective-permute-done.1.refs_0_ = bf16[128,1024]{1,0:T(8,128)(2,1)S(1)} collective-permute-done((bf16[128,1024]{1,0:T(8,128)(2,1)}, bf16[128,1024]{1,0:T(8,128)(2,1)S(1)}, u32[]{:S(2)}, u32[]{:S(2)}) %collective-permute-start.1) | collective-permute-done | bytes 262176 | tf_op jit(solution)/shard_map/ppermute | solution.py:33
  13.1 4.4 %collective-permute-start.2 = (bf16[128,1024]{1,0:T(8,128)(2,1)S(1)}, bf16[128,1024]{1,0:T(8,128)(2,1)S(1)}, u32[]{:S(2)}, u32[]{:S(2)}) collective-permute-start(bf16[128,1024]{1,0:T(8,128)(2,1)S(1)} %collective-permute-done.1.refs_0_), channel_id=1, source_target_pairs={{0,2},{1,3},{2,0},{3,1},{4,6},{5,7},{6,4},{7,5},{8,10},{9,11},{10,... | collective-permute-start | bytes 786440 | tf_op jit(solution)/shard_map/ppermute | solution.py:33
  17.6 0.4 collective-permute-done.3.refs_0_
  18.0 0.1 collective-permute-start.4
  18.1 1.1 %scores.6 = (f32[256,1536]{1,0:T(8,128)S(1)}, f32[1,1536]{1,0:T(1,128)S(1)}) custom-call(bf16[128,1024]{1,0:T(8,128)(2,1)S(1)} %bitcast.9, bf16[128,1024]{1,0:T(8,128)(2,1)S(1)} %collective-permute-done.refs_1_, bf16[1536,1024]{1,0:T(8,128)(2,1)S(1)} %fusion.1.refs_2_.unit), custom_call_target="tpu_custom_call" | custom-call | flops 3221225472 | bytes 5242880 | tf_op jit(solution)/shard_map/scores/pallas_call | solution.py:52
  19.2 0.4 collective-permute-done.4.refs_1_
  19.6 1.1 %scores.7 = (f32[256,1536]{1,0:T(8,128)S(1)}, f32[1,1536]{1,0:T(1,128)S(1)}) custom-call(bf16[128,1024]{1,0:T(8,128)(2,1)S(1)} %collective-permute-done.3.refs_0_, bf16[128,1024]{1,0:T(8,128)(2,1)S(1)} %collective-permute-done.4.refs_1_, bf16[1536,1024]{1,0:T(8,128)(2,1)S(1)} %fusion.1.refs_2_.unit), custom_call_target="tpu_custom_call" | custom-call | flops 3221225472 | bytes 5242880 | tf_op jit(solution)/shard_map/scores/pallas_call | solution.py:52
  20.6 1.1 %scores.8 = (f32[256,1536]{1,0:T(8,128)S(1)}, f32[1,1536]{1,0:T(1,128)S(1)}) custom-call(bf16[128,1024]{1,0:T(8,128)(2,1)S(1)} %collective-permute-done.1.refs_0_, bf16[128,1024]{1,0:T(8,128)(2,1)S(1)} %collective-permute-done.5.refs_1_, bf16[1536,1024]{1,0:T(8,128)(2,1)S(1)} %fusion.1.refs_2_.unit), custom_call_target="tpu_custom_call" | custom-call | flops 3221225472 | bytes 5242880 | tf_op jit(solution)/shard_map/scores/pallas_call | solution.py:52
  21.7 1.9 %collective-permute-done.2.own_rows = bf16[128,1024]{1,0:T(8,128)(2,1)S(1)} collective-permute-done((bf16[128,1024]{1,0:T(8,128)(2,1)S(1)}, bf16[128,1024]{1,0:T(8,128)(2,1)S(1)}, u32[]{:S(2)}, u32[]{:S(2)}) %collective-permute-start.2) | collective-permute-done | bytes 262176 | tf_op jit(solution)/shard_map/ppermute | solution.py:33
  23.6 1.5 %collective-permute-done.6.other_rows = bf16[128,1024]{1,0:T(8,128)(2,1)S(1)} collective-permute-done((bf16[128,1024]{1,0:T(8,128)(2,1)S(1)}, bf16[128,1024]{1,0:T(8,128)(2,1)S(1)}, u32[]{:S(2)}, u32[]{:S(2)}) %collective-permute-start.6) | collective-permute-done | bytes 262176 | tf_op jit(solution)/shard_map/ppermute | solution.py:33
  25.1 1.9 %last.2 = (f32[1,1536]{1,0:T(1,128)S(1)}, f32[128,1024]{1,0:T(8,128)S(1)}, bf16[128,1024]{1,0:T(8,128)(2,1)S(1)}) custom-call(bf16[128,1024]{1,0:T(8,128)(2,1)S(1)} %collective-permute-done.2.own_rows, bf16[128,1024]{1,0:T(8,128)(2,1)S(1)} %collective-permute-done.6.other_rows, bf16[1536,1024]{1,0:T(8,128)(2,1)S(1)} %fusion.1.refs_2_.unit, ...), custom_call_target="tpu_custom_call" | custom-call | flops 3221225472 | bytes 5242880 | tf_op jit(solution)/shard_map/last/pallas_call | solution.py:52
  27.0 0.2 collective-permute-start.7
  27.2 1.0 %sums.7 = (f32[128,1024]{1,0:T(8,128)S(1)}, bf16[128,1024]{1,0:T(8,128)(2,1)S(1)}) custom-call(f32[256,1536]{1,0:T(8,128)S(1)} %get-tuple-element.63.terms, f32[1,1536]{1,0:T(1,128)S(1)} %get-tuple-element.60.factor, bf16[1536,1024]{1,0:T(8,128)(2,1)S(1)} %fusion.1.refs_2_.unit), custom_call_target="tpu_custom_call" | custom-call | flops 3221225472 | bytes 5242880 | tf_op jit(solution)/shard_map/sums/pallas_call | solution.py:52
  28.2 0.4 collective-permute-start.9
  28.7 0.1 convert_add_fusion.4
  28.7 1.7 %collective-permute-start.12 = (bf16[128,1024]{1,0:T(8,128)(2,1)S(1)}, bf16[128,1024]{1,0:T(8,128)(2,1)S(1)}, u32[]{:S(2)}, u32[]{:S(2)}) collective-permute-start(bf16[128,1024]{1,0:T(8,128)(2,1)S(1)} %convert_add_fusion.4), channel_id=1, source_target_pairs={{0,2},{1,3},{2,0},{3,1},{4,6},{5,7},{6,4},{7,5},{8,10},{9,11},{10,... | collective-permute-start | bytes 786440 | tf_op jit(solution)/shard_map/ppermute | solution.py:33
  30.5 1.0 %sums.8 = (f32[128,1024]{1,0:T(8,128)S(1)}, bf16[128,1024]{1,0:T(8,128)(2,1)S(1)}) custom-call(f32[256,1536]{1,0:T(8,128)S(1)} %get-tuple-element.67.terms, f32[1,1536]{1,0:T(1,128)S(1)} %get-tuple-element.60.factor, bf16[1536,1024]{1,0:T(8,128)(2,1)S(1)} %fusion.1.refs_2_.unit), custom_call_target="tpu_custom_call" | custom-call | flops 3221225472 | bytes 5242880 | tf_op jit(solution)/shard_map/sums/pallas_call | solution.py:52
  31.5 0.1 collective-permute-start.11
  31.6 1.0 %sums.6 = (f32[128,1024]{1,0:T(8,128)S(1)}, bf16[128,1024]{1,0:T(8,128)(2,1)S(1)}) custom-call(f32[256,1536]{1,0:T(8,128)S(1)} %get-tuple-element.59.terms, f32[1,1536]{1,0:T(1,128)S(1)} %get-tuple-element.60.factor, bf16[1536,1024]{1,0:T(8,128)(2,1)S(1)} %fusion.1.refs_2_.unit), custom_call_target="tpu_custom_call" | custom-call | flops 3221225472 | bytes 5242880 | tf_op jit(solution)/shard_map/sums/pallas_call | solution.py:52
  32.6 0.1 add_convert_fusion.2
  32.7 0.4 collective-permute-start.10
  33.1 0.2 collective-permute-start.8
  33.3 4.7 %collective-permute-done.12 = bf16[128,1024]{1,0:T(8,128)(2,1)S(1)} collective-permute-done((bf16[128,1024]{1,0:T(8,128)(2,1)S(1)}, bf16[128,1024]{1,0:T(8,128)(2,1)S(1)}, u32[]{:S(2)}, u32[]{:S(2)}) %collective-permute-start.12) | collective-permute-done | bytes 262176 | tf_op jit(solution)/shard_map/ppermute | solution.py:33
  38.0 0.1 add_convert_fusion.1
  38.1 2.5 %collective-permute-start.13 = (bf16[128,1024]{1,0:T(8,128)(2,1)S(1)}, bf16[128,1024]{1,0:T(8,128)(2,1)S(1)}, u32[]{:S(2)}, u32[]{:S(2)}) collective-permute-start(bf16[128,1024]{1,0:T(8,128)(2,1)S(1)} %add_convert_fusion.1), channel_id=1, source_target_pairs={{0,6},{1,7},{2,4},{3,5},{4,2},{5,3},{6,0},{7,1},{8,14},{9,15},{10,... | collective-permute-start | bytes 786440 | tf_op jit(solution)/shard_map/ppermute | solution.py:33
  40.5 2.2 %collective-permute-done.10 = bf16[128,1024]{1,0:T(8,128)(2,1)S(1)} collective-permute-done((bf16[128,1024]{1,0:T(8,128)(2,1)S(1)}, bf16[128,1024]{1,0:T(8,128)(2,1)S(1)}, u32[]{:S(2)}, u32[]{:S(2)}) %collective-permute-start.10) | collective-permute-done | bytes 262176 | tf_op jit(solution)/shard_map/ppermute | solution.py:33
  42.8 7.3 %collective-permute-done.13 = bf16[128,1024]{1,0:T(8,128)(2,1)S(1)} collective-permute-done((bf16[128,1024]{1,0:T(8,128)(2,1)S(1)}, bf16[128,1024]{1,0:T(8,128)(2,1)S(1)}, u32[]{:S(2)}, u32[]{:S(2)}) %collective-permute-start.13) | collective-permute-done | bytes 262176 | tf_op jit(solution)/shard_map/ppermute | solution.py:33
  50.1 0.2 multiply_reduce_fusion.1
  50.3 0.2 multiply_convert_fusion.refs_0_
  50.5 1.9 %collective-permute-start.15 = (bf16[128,1024]{1,0:T(8,128)(2,1)S(1)}, bf16[128,1024]{1,0:T(8,128)(2,1)S(1)}, u32[]{:S(2)}, u32[]{:S(2)}) collective-permute-start(bf16[128,1024]{1,0:T(8,128)(2,1)S(1)} %multiply_convert_fusion.refs_0_), channel_id=1, source_target_pairs={{0,6},{1,7},{2,4},{3,5},{4,2},{5,3},{6,0},{7,1},{8,14},{9,15},{10,... | collective-permute-start | bytes 786440 | tf_op jit(solution)/shard_map/ppermute | solution.py:33
  52.4 2.7 %collective-permute-start.17 = (bf16[128,1024]{1,0:T(8,128)(2,1)S(1)}, bf16[128,1024]{1,0:T(8,128)(2,1)S(1)}, u32[]{:S(2)}, u32[]{:S(2)}) collective-permute-start(bf16[128,1024]{1,0:T(8,128)(2,1)S(1)} %multiply_convert_fusion.refs_0_), channel_id=1, source_target_pairs={{0,2},{1,3},{2,0},{3,1},{4,6},{5,7},{6,4},{7,5},{8,10},{9,11},{10,... | collective-permute-start | bytes 786440 | tf_op jit(solution)/shard_map/ppermute | solution.py:33
  55.2 6.4 %collective-permute-done.15.refs_0_ = bf16[128,1024]{1,0:T(8,128)(2,1)S(1)} collective-permute-done((bf16[128,1024]{1,0:T(8,128)(2,1)S(1)}, bf16[128,1024]{1,0:T(8,128)(2,1)S(1)}, u32[]{:S(2)}, u32[]{:S(2)}) %collective-permute-start.15) | collective-permute-done | bytes 262176 | tf_op jit(solution)/shard_map/ppermute | solution.py:33
  61.6 1.8 %collective-permute-start.16 = (bf16[128,1024]{1,0:T(8,128)(2,1)S(1)}, bf16[128,1024]{1,0:T(8,128)(2,1)S(1)}, u32[]{:S(2)}, u32[]{:S(2)}) collective-permute-start(bf16[128,1024]{1,0:T(8,128)(2,1)S(1)} %collective-permute-done.15.refs_0_), channel_id=1, source_target_pairs={{0,2},{1,3},{2,0},{3,1},{4,6},{5,7},{6,4},{7,5},{8,10},{9,11},{10,... | collective-permute-start | bytes 786440 | tf_op jit(solution)/shard_map/ppermute | solution.py:33
  63.4 2.3 %collective-permute-done.17.refs_0_ = bf16[128,1024]{1,0:T(8,128)(2,1)S(1)} collective-permute-done((bf16[128,1024]{1,0:T(8,128)(2,1)S(1)}, bf16[128,1024]{1,0:T(8,128)(2,1)S(1)}, u32[]{:S(2)}, u32[]{:S(2)}) %collective-permute-start.17) | collective-permute-done | bytes 262176 | tf_op jit(solution)/shard_map/ppermute | solution.py:33
  65.7 1.1 %scores.9 = (f32[256,1536]{1,0:T(8,128)S(1)}, f32[1,1536]{1,0:T(1,128)S(1)}) custom-call(bf16[128,1024]{1,0:T(8,128)(2,1)S(1)} %multiply_convert_fusion.refs_0_, bf16[128,1024]{1,0:T(8,128)(2,1)S(1)} %collective-permute-done.14.refs_1_, bf16[1536,1024]{1,0:T(8,128)(2,1)S(1)} %fusion.1.refs_2_.unit), custom_call_target="tpu_custom_call" | custom-call | flops 3221225472 | bytes 5242880 | tf_op jit(solution)/shard_map/scores/pallas_call | solution.py:52
  66.7 0.5 collective-permute-done.18.refs_1_
  67.2 1.1 %scores.10 = (f32[256,1536]{1,0:T(8,128)S(1)}, f32[1,1536]{1,0:T(1,128)S(1)}) custom-call(bf16[128,1024]{1,0:T(8,128)(2,1)S(1)} %collective-permute-done.17.refs_0_, bf16[128,1024]{1,0:T(8,128)(2,1)S(1)} %collective-permute-done.18.refs_1_, bf16[1536,1024]{1,0:T(8,128)(2,1)S(1)} %fusion.1.refs_2_.unit), custom_call_target="tpu_custom_call" | custom-call | flops 3221225472 | bytes 5242880 | tf_op jit(solution)/shard_map/scores/pallas_call | solution.py:52
  68.3 1.3 %scores.11 = (f32[256,1536]{1,0:T(8,128)S(1)}, f32[1,1536]{1,0:T(1,128)S(1)}) custom-call(bf16[128,1024]{1,0:T(8,128)(2,1)S(1)} %collective-permute-done.15.refs_0_, bf16[128,1024]{1,0:T(8,128)(2,1)S(1)} %collective-permute-done.19.refs_1_, bf16[1536,1024]{1,0:T(8,128)(2,1)S(1)} %fusion.1.refs_2_.unit), custom_call_target="tpu_custom_call" | custom-call | flops 3221225472 | bytes 5242880 | tf_op jit(solution)/shard_map/scores/pallas_call | solution.py:52
  69.5 1.3 %collective-permute-done.16.own_rows = bf16[128,1024]{1,0:T(8,128)(2,1)S(1)} collective-permute-done((bf16[128,1024]{1,0:T(8,128)(2,1)S(1)}, bf16[128,1024]{1,0:T(8,128)(2,1)S(1)}, u32[]{:S(2)}, u32[]{:S(2)}) %collective-permute-start.16) | collective-permute-done | bytes 262176 | tf_op jit(solution)/shard_map/ppermute | solution.py:33
  71.0 1.4 %collective-permute-done.20.other_rows = bf16[128,1024]{1,0:T(8,128)(2,1)S(1)} collective-permute-done((bf16[128,1024]{1,0:T(8,128)(2,1)S(1)}, bf16[128,1024]{1,0:T(8,128)(2,1)S(1)}, u32[]{:S(2)}, u32[]{:S(2)}) %collective-permute-start.20) | collective-permute-done | bytes 262176 | tf_op jit(solution)/shard_map/ppermute | solution.py:33
  72.4 1.8 %last.3 = (f32[256,1536]{1,0:T(8,128)S(1)}, f32[1,1536]{1,0:T(1,128)S(1)}, f32[128,1024]{1,0:T(8,128)S(1)}, bf16[128,1024]{1,0:T(8,128)(2,1)S(1)}) custom-call(bf16[128,1024]{1,0:T(8,128)(2,1)S(1)} %collective-permute-done.16.own_rows, bf16[128,1024]{1,0:T(8,128)(2,1)S(1)} %collective-permute-done.20.other_rows, bf16[1536,1024]{1,0:T(8,128)(2,1)S(1)} %fusion.1.refs_2_.unit, ...), custom_call_target="tpu_custom_call" | custom-call | flops 3221225472 | bytes 5242880 | tf_op jit(solution)/shard_map/last/pallas_call | solution.py:52
  74.2 0.2 collective-permute-start.21
  74.4 1.0 %sums.11 = (f32[128,1024]{1,0:T(8,128)S(1)}, bf16[128,1024]{1,0:T(8,128)(2,1)S(1)}) custom-call(f32[256,1536]{1,0:T(8,128)S(1)} %get-tuple-element.87.refs_1_.terms, f32[1,1536]{1,0:T(1,128)S(1)} %get-tuple-element.80.factor.refs_8_, bf16[1536,1024]{1,0:T(8,128)(2,1)S(1)} %fusion.1.refs_2_.unit), custom_call_target="tpu_custom_call" | custom-call | flops 3221225472 | bytes 5242880 | tf_op jit(solution)/shard_map/sums/pallas_call | solution.py:52
  75.4 0.4 collective-permute-start.25
  75.9 0.1 convert_add_fusion.2
  76.0 0.5 collective-permute-start.23
  76.5 1.0 %sums.10 = (f32[128,1024]{1,0:T(8,128)S(1)}, bf16[128,1024]{1,0:T(8,128)(2,1)S(1)}) custom-call(f32[256,1536]{1,0:T(8,128)S(1)} %get-tuple-element.88.terms.refs_2_, f32[1,1536]{1,0:T(1,128)S(1)} %get-tuple-element.80.factor.refs_8_, bf16[1536,1024]{1,0:T(8,128)(2,1)S(1)} %fusion.1.refs_2_.unit), custom_call_target="tpu_custom_call" | custom-call | flops 3221225472 | bytes 5242880 | tf_op jit(solution)/shard_map/sums/pallas_call | solution.py:52
  77.5 0.1 collective-permute-start.22
  77.6 1.0 %sums.9 = (f32[128,1024]{1,0:T(8,128)S(1)}, bf16[128,1024]{1,0:T(8,128)(2,1)S(1)}) custom-call(f32[256,1536]{1,0:T(8,128)S(1)} %get-tuple-element.86.terms.refs_0_, f32[1,1536]{1,0:T(1,128)S(1)} %get-tuple-element.80.factor.refs_8_, bf16[1536,1024]{1,0:T(8,128)(2,1)S(1)} %fusion.1.refs_2_.unit), custom_call_target="tpu_custom_call" | custom-call | flops 3221225472 | bytes 5242880 | tf_op jit(solution)/shard_map/sums/pallas_call | solution.py:52
  78.6 0.1 add_convert_fusion
  78.6 1.7 %collective-permute-start.26 = (bf16[128,1024]{1,0:T(8,128)(2,1)S(1)}, bf16[128,1024]{1,0:T(8,128)(2,1)S(1)}, u32[]{:S(2)}, u32[]{:S(2)}) collective-permute-start(bf16[128,1024]{1,0:T(8,128)(2,1)S(1)} %add_convert_fusion), channel_id=1, source_target_pairs={{0,2},{1,3},{2,0},{3,1},{4,6},{5,7},{6,4},{7,5},{8,10},{9,11},{10,... | collective-permute-start | bytes 786440 | tf_op jit(solution)/shard_map/ppermute | solution.py:33
  80.3 4.9 %collective-permute-done.23 = bf16[128,1024]{1,0:T(8,128)(2,1)S(1)} collective-permute-done((bf16[128,1024]{1,0:T(8,128)(2,1)S(1)}, bf16[128,1024]{1,0:T(8,128)(2,1)S(1)}, u32[]{:S(2)}, u32[]{:S(2)}) %collective-permute-start.23) | collective-permute-done | bytes 262176 | tf_op jit(solution)/shard_map/ppermute | solution.py:33
  85.2 0.1 convert_add_fusion.1
  85.3 2.0 %collective-permute-start.27 = (bf16[128,1024]{1,0:T(8,128)(2,1)S(1)}, bf16[128,1024]{1,0:T(8,128)(2,1)S(1)}, u32[]{:S(2)}, u32[]{:S(2)}) collective-permute-start(bf16[128,1024]{1,0:T(8,128)(2,1)S(1)} %convert_add_fusion.1), channel_id=1, source_target_pairs={{0,6},{1,7},{2,4},{3,5},{4,2},{5,3},{6,0},{7,1},{8,14},{9,15},{10,... | collective-permute-start | bytes 786440 | tf_op jit(solution)/shard_map/ppermute | solution.py:33
  87.3 5.8 %blend.1 = bf16[1536,1024]{1,0:T(8,128)(2,1)} custom-call(f32[256,1536]{1,0:T(8,128)S(1)} %get-tuple-element.86.terms.refs_0_, f32[256,1536]{1,0:T(8,128)S(1)} %get-tuple-element.87.refs_1_.terms, f32[256,1536]{1,0:T(8,128)S(1)} %get-tuple-element.88.terms.refs_2_, f32[256,1536]{1,0:T(8,128)S(1)} %get-tuple-element.90.refs_3_, ...), custom_call_target="tpu_custom_call" | custom-call | flops 12884901888 | bytes 5242880 | tf_op jit(solution)/shard_map/blend/pallas_call | solution.py:157
  93.2 2.9 %collective-permute-done.27 = bf16[128,1024]{1,0:T(8,128)(2,1)S(1)} collective-permute-done((bf16[128,1024]{1,0:T(8,128)(2,1)S(1)}, bf16[128,1024]{1,0:T(8,128)(2,1)S(1)}, u32[]{:S(2)}, u32[]{:S(2)}) %collective-permute-start.27) | collective-permute-done | bytes 262176 | tf_op jit(solution)/shard_map/ppermute | solution.py:33
  96.1 0.2 multiply_reduce_fusion
  96.3 0.9 multiply_bitcast_fusion
  (34 shorter events, 0.2 us)
Async XLA Ops:
  0.6 12.5 %collective-permute-start.1 = (bf16[128,1024]{1,0:T(8,128)(2,1)}, bf16[128,1024]{1,0:T(8,128)(2,1)S(1)}, u32[]{:S(2)}, u32[]{:S(2)}) collective-permute-start(bf16[128,1024]{1,0:T(8,128)(2,1)} %bitcast.6), channel_id=1, source_target_pairs={{0,6},{1,7},{2,4},{3,5},{4,2},{5,3},{6,0},{7,1},{8,14},{9,15},{10,... | collective-permute-start | bytes 786440 | tf_op jit(solution)/shard_map/ppermute | solution.py:33
  5.7 12.4 %collective-permute-start = (bf16[128,1024]{1,0:T(8,128)(2,1)}, bf16[128,1024]{1,0:T(8,128)(2,1)S(1)}, u32[]{:S(2)}, u32[]{:S(2)}) collective-permute-start(bf16[128,1024]{1,0:T(8,128)(2,1)} %bitcast.7), channel_id=1, source_target_pairs={{0,1},{1,0},{2,3},{3,2},{4,5},{5,4},{6,7},{7,6},{8,9},{9,8},{10,11... | collective-permute-start | bytes 786440 | tf_op jit(solution)/shard_map/ppermute | solution.py:33
  5.7 12.3 %collective-permute-start.3 = (bf16[128,1024]{1,0:T(8,128)(2,1)}, bf16[128,1024]{1,0:T(8,128)(2,1)S(1)}, u32[]{:S(2)}, u32[]{:S(2)}) collective-permute-start(bf16[128,1024]{1,0:T(8,128)(2,1)} %bitcast.8), channel_id=1, source_target_pairs={{0,2},{1,3},{2,0},{3,1},{4,6},{5,7},{6,4},{7,5},{8,10},{9,11},{10,... | collective-permute-start | bytes 786440 | tf_op jit(solution)/shard_map/ppermute | solution.py:33
  8.3 2.8 %copy-start.2 = (bf16[1,1536,1024]{2,1,0:T(8,128)(2,1)S(1)}, bf16[1,1536,1024]{2,1,0:T(8,128)(2,1)}, u32[]{:S(2)}) copy-start(bf16[1,1536,1024]{2,1,0:T(8,128)(2,1)} %param.3) | copy-start | bytes 9437188
  11.2 7.0 %copy-start.1 = (bf16[1,128,1024]{2,1,0:T(8,128)(2,1)S(1)}, bf16[1,128,1024]{2,1,0:T(8,128)(2,1)}, u32[]{:S(2)}) copy-start(bf16[1,128,1024]{2,1,0:T(8,128)(2,1)} %param.4) | copy-start | bytes 786436
  13.1 10.5 %collective-permute-start.2 = (bf16[128,1024]{1,0:T(8,128)(2,1)S(1)}, bf16[128,1024]{1,0:T(8,128)(2,1)S(1)}, u32[]{:S(2)}, u32[]{:S(2)}) collective-permute-start(bf16[128,1024]{1,0:T(8,128)(2,1)S(1)} %collective-permute-done.1.refs_0_), channel_id=1, source_target_pairs={{0,2},{1,3},{2,0},{3,1},{4,6},{5,7},{6,4},{7,5},{8,10},{9,11},{10,... | collective-permute-start | bytes 786440 | tf_op jit(solution)/shard_map/ppermute | solution.py:33
  17.6 3.0 %collective-permute-start.5 = (bf16[128,1024]{1,0:T(8,128)(2,1)S(1)}, bf16[128,1024]{1,0:T(8,128)(2,1)S(1)}, u32[]{:S(2)}, u32[]{:S(2)}) collective-permute-start(bf16[128,1024]{1,0:T(8,128)(2,1)S(1)} %collective-permute-done.1.refs_0_), channel_id=1, source_target_pairs={{0,1},{1,0},{2,3},{3,2},{4,5},{5,4},{6,7},{7,6},{8,9},{9,8},{10,11... | collective-permute-start | bytes 786440 | tf_op jit(solution)/shard_map/ppermute | solution.py:33
  18.0 1.5 %collective-permute-start.4 = (bf16[128,1024]{1,0:T(8,128)(2,1)S(1)}, bf16[128,1024]{1,0:T(8,128)(2,1)S(1)}, u32[]{:S(2)}, u32[]{:S(2)}) collective-permute-start(bf16[128,1024]{1,0:T(8,128)(2,1)S(1)} %collective-permute-done.3.refs_0_), channel_id=1, source_target_pairs={{0,1},{1,0},{2,3},{3,2},{4,5},{5,4},{6,7},{7,6},{8,9},{9,8},{10,11... | collective-permute-start | bytes 786440 | tf_op jit(solution)/shard_map/ppermute | solution.py:33
  20.6 4.5 %copy-start = (f32[1,1536]{1,0:T(1,128)S(1)}, f32[1,1536]{1,0:T(1,128)}, u32[]{:S(2)}) copy-start(f32[1,1536]{1,0:T(1,128)} %live.1) | copy-start | bytes 18436
  23.6 1.5 %collective-permute-start.6 = (bf16[128,1024]{1,0:T(8,128)(2,1)S(1)}, bf16[128,1024]{1,0:T(8,128)(2,1)S(1)}, u32[]{:S(2)}, u32[]{:S(2)}) collective-permute-start(bf16[128,1024]{1,0:T(8,128)(2,1)S(1)} %collective-permute-done.2.own_rows), channel_id=1, source_target_pairs={{0,1},{1,0},{2,3},{3,2},{4,5},{5,4},{6,7},{7,6},{8,9},{9,8},{10,11... | collective-permute-start | bytes 786440 | tf_op jit(solution)/shard_map/ppermute | solution.py:33
  27.0 1.6 %collective-permute-start.7 = (bf16[128,1024]{1,0:T(8,128)(2,1)S(1)}, bf16[128,1024]{1,0:T(8,128)(2,1)S(1)}, u32[]{:S(2)}, u32[]{:S(2)}) collective-permute-start(bf16[128,1024]{1,0:T(8,128)(2,1)S(1)} %get-tuple-element.58), channel_id=1, source_target_pairs={{0,1},{1,0},{2,3},{3,2},{4,5},{5,4},{6,7},{7,6},{8,9},{9,8},{10,11... | collective-permute-start | bytes 786440 | tf_op jit(solution)/shard_map/ppermute | solution.py:33
  28.2 4.4 %collective-permute-start.9 = (bf16[128,1024]{1,0:T(8,128)(2,1)S(1)}, bf16[128,1024]{1,0:T(8,128)(2,1)S(1)}, u32[]{:S(2)}, u32[]{:S(2)}) collective-permute-start(bf16[128,1024]{1,0:T(8,128)(2,1)S(1)} %get-tuple-element.65), channel_id=1, source_target_pairs={{0,1},{1,0},{2,3},{3,2},{4,5},{5,4},{6,7},{7,6},{8,9},{9,8},{10,11... | collective-permute-start | bytes 786440 | tf_op jit(solution)/shard_map/ppermute | solution.py:33
  28.7 9.2 %collective-permute-start.12 = (bf16[128,1024]{1,0:T(8,128)(2,1)S(1)}, bf16[128,1024]{1,0:T(8,128)(2,1)S(1)}, u32[]{:S(2)}, u32[]{:S(2)}) collective-permute-start(bf16[128,1024]{1,0:T(8,128)(2,1)S(1)} %convert_add_fusion.4), channel_id=1, source_target_pairs={{0,2},{1,3},{2,0},{3,1},{4,6},{5,7},{6,4},{7,5},{8,10},{9,11},{10,... | collective-permute-start | bytes 786440 | tf_op jit(solution)/shard_map/ppermute | solution.py:33
  31.5 6.5 %collective-permute-start.11 = (bf16[128,1024]{1,0:T(8,128)(2,1)S(1)}, bf16[128,1024]{1,0:T(8,128)(2,1)S(1)}, u32[]{:S(2)}, u32[]{:S(2)}) collective-permute-start(bf16[128,1024]{1,0:T(8,128)(2,1)S(1)} %get-tuple-element.69), channel_id=1, source_target_pairs={{0,1},{1,0},{2,3},{3,2},{4,5},{5,4},{6,7},{7,6},{8,9},{9,8},{10,11... | collective-permute-start | bytes 786440 | tf_op jit(solution)/shard_map/ppermute | solution.py:33
  32.7 10.1 %collective-permute-start.10 = (bf16[128,1024]{1,0:T(8,128)(2,1)S(1)}, bf16[128,1024]{1,0:T(8,128)(2,1)S(1)}, u32[]{:S(2)}, u32[]{:S(2)}) collective-permute-start(bf16[128,1024]{1,0:T(8,128)(2,1)S(1)} %add_convert_fusion.2), channel_id=1, source_target_pairs={{0,2},{1,3},{2,0},{3,1},{4,6},{5,7},{6,4},{7,5},{8,10},{9,11},{10,... | collective-permute-start | bytes 786440 | tf_op jit(solution)/shard_map/ppermute | solution.py:33
  33.1 9.7 %collective-permute-start.8 = (bf16[128,1024]{1,0:T(8,128)(2,1)S(1)}, bf16[128,1024]{1,0:T(8,128)(2,1)S(1)}, u32[]{:S(2)}, u32[]{:S(2)}) collective-permute-start(bf16[128,1024]{1,0:T(8,128)(2,1)S(1)} %get-tuple-element.62), channel_id=1, source_target_pairs={{0,1},{1,0},{2,3},{3,2},{4,5},{5,4},{6,7},{7,6},{8,9},{9,8},{10,11... | collective-permute-start | bytes 786440 | tf_op jit(solution)/shard_map/ppermute | solution.py:33
  38.1 12.0 %collective-permute-start.13 = (bf16[128,1024]{1,0:T(8,128)(2,1)S(1)}, bf16[128,1024]{1,0:T(8,128)(2,1)S(1)}, u32[]{:S(2)}, u32[]{:S(2)}) collective-permute-start(bf16[128,1024]{1,0:T(8,128)(2,1)S(1)} %add_convert_fusion.1), channel_id=1, source_target_pairs={{0,6},{1,7},{2,4},{3,5},{4,2},{5,3},{6,0},{7,1},{8,14},{9,15},{10,... | collective-permute-start | bytes 786440 | tf_op jit(solution)/shard_map/ppermute | solution.py:33
  50.5 11.1 %collective-permute-start.15 = (bf16[128,1024]{1,0:T(8,128)(2,1)S(1)}, bf16[128,1024]{1,0:T(8,128)(2,1)S(1)}, u32[]{:S(2)}, u32[]{:S(2)}) collective-permute-start(bf16[128,1024]{1,0:T(8,128)(2,1)S(1)} %multiply_convert_fusion.refs_0_), channel_id=1, source_target_pairs={{0,6},{1,7},{2,4},{3,5},{4,2},{5,3},{6,0},{7,1},{8,14},{9,15},{10,... | collective-permute-start | bytes 786440 | tf_op jit(solution)/shard_map/ppermute | solution.py:33
  52.4 13.2 %collective-permute-start.17 = (bf16[128,1024]{1,0:T(8,128)(2,1)S(1)}, bf16[128,1024]{1,0:T(8,128)(2,1)S(1)}, u32[]{:S(2)}, u32[]{:S(2)}) collective-permute-start(bf16[128,1024]{1,0:T(8,128)(2,1)S(1)} %multiply_convert_fusion.refs_0_), channel_id=1, source_target_pairs={{0,2},{1,3},{2,0},{3,1},{4,6},{5,7},{6,4},{7,5},{8,10},{9,11},{10,... | collective-permute-start | bytes 786440 | tf_op jit(solution)/shard_map/ppermute | solution.py:33
  55.2 10.5 %collective-permute-start.14 = (bf16[128,1024]{1,0:T(8,128)(2,1)S(1)}, bf16[128,1024]{1,0:T(8,128)(2,1)S(1)}, u32[]{:S(2)}, u32[]{:S(2)}) collective-permute-start(bf16[128,1024]{1,0:T(8,128)(2,1)S(1)} %multiply_convert_fusion.refs_0_), channel_id=1, source_target_pairs={{0,1},{1,0},{2,3},{3,2},{4,5},{5,4},{6,7},{7,6},{8,9},{9,8},{10,11... | collective-permute-start | bytes 786440 | tf_op jit(solution)/shard_map/ppermute | solution.py:33
  61.6 9.2 %collective-permute-start.16 = (bf16[128,1024]{1,0:T(8,128)(2,1)S(1)}, bf16[128,1024]{1,0:T(8,128)(2,1)S(1)}, u32[]{:S(2)}, u32[]{:S(2)}) collective-permute-start(bf16[128,1024]{1,0:T(8,128)(2,1)S(1)} %collective-permute-done.15.refs_0_), channel_id=1, source_target_pairs={{0,2},{1,3},{2,0},{3,1},{4,6},{5,7},{6,4},{7,5},{8,10},{9,11},{10,... | collective-permute-start | bytes 786440 | tf_op jit(solution)/shard_map/ppermute | solution.py:33
  63.4 4.9 %collective-permute-start.19 = (bf16[128,1024]{1,0:T(8,128)(2,1)S(1)}, bf16[128,1024]{1,0:T(8,128)(2,1)S(1)}, u32[]{:S(2)}, u32[]{:S(2)}) collective-permute-start(bf16[128,1024]{1,0:T(8,128)(2,1)S(1)} %collective-permute-done.15.refs_0_), channel_id=1, source_target_pairs={{0,1},{1,0},{2,3},{3,2},{4,5},{5,4},{6,7},{7,6},{8,9},{9,8},{10,11... | collective-permute-start | bytes 786440 | tf_op jit(solution)/shard_map/ppermute | solution.py:33
  65.6 1.5 %collective-permute-start.18 = (bf16[128,1024]{1,0:T(8,128)(2,1)S(1)}, bf16[128,1024]{1,0:T(8,128)(2,1)S(1)}, u32[]{:S(2)}, u32[]{:S(2)}) collective-permute-start(bf16[128,1024]{1,0:T(8,128)(2,1)S(1)} %collective-permute-done.17.refs_0_), channel_id=1, source_target_pairs={{0,1},{1,0},{2,3},{3,2},{4,5},{5,4},{6,7},{7,6},{8,9},{9,8},{10,11... | collective-permute-start | bytes 786440 | tf_op jit(solution)/shard_map/ppermute | solution.py:33
  70.8 1.5 %collective-permute-start.20 = (bf16[128,1024]{1,0:T(8,128)(2,1)S(1)}, bf16[128,1024]{1,0:T(8,128)(2,1)S(1)}, u32[]{:S(2)}, u32[]{:S(2)}) collective-permute-start(bf16[128,1024]{1,0:T(8,128)(2,1)S(1)} %collective-permute-done.16.own_rows), channel_id=1, source_target_pairs={{0,1},{1,0},{2,3},{3,2},{4,5},{5,4},{6,7},{7,6},{8,9},{9,8},{10,11... | collective-permute-start | bytes 786440 | tf_op jit(solution)/shard_map/ppermute | solution.py:33
  74.2 1.7 %collective-permute-start.21 = (bf16[128,1024]{1,0:T(8,128)(2,1)S(1)}, bf16[128,1024]{1,0:T(8,128)(2,1)S(1)}, u32[]{:S(2)}, u32[]{:S(2)}) collective-permute-start(bf16[128,1024]{1,0:T(8,128)(2,1)S(1)} %get-tuple-element.78), channel_id=1, source_target_pairs={{0,1},{1,0},{2,3},{3,2},{4,5},{5,4},{6,7},{7,6},{8,9},{9,8},{10,11... | collective-permute-start | bytes 786440 | tf_op jit(solution)/shard_map/ppermute | solution.py:33
  75.4 3.1 %collective-permute-start.25 = (bf16[128,1024]{1,0:T(8,128)(2,1)S(1)}, bf16[128,1024]{1,0:T(8,128)(2,1)S(1)}, u32[]{:S(2)}, u32[]{:S(2)}) collective-permute-start(bf16[128,1024]{1,0:T(8,128)(2,1)S(1)} %get-tuple-element.94), channel_id=1, source_target_pairs={{0,1},{1,0},{2,3},{3,2},{4,5},{5,4},{6,7},{7,6},{8,9},{9,8},{10,11... | collective-permute-start | bytes 786440 | tf_op jit(solution)/shard_map/ppermute | solution.py:33
  76.0 9.2 %collective-permute-start.23 = (bf16[128,1024]{1,0:T(8,128)(2,1)S(1)}, bf16[128,1024]{1,0:T(8,128)(2,1)S(1)}, u32[]{:S(2)}, u32[]{:S(2)}) collective-permute-start(bf16[128,1024]{1,0:T(8,128)(2,1)S(1)} %convert_add_fusion.2), channel_id=1, source_target_pairs={{0,2},{1,3},{2,0},{3,1},{4,6},{5,7},{6,4},{7,5},{8,10},{9,11},{10,... | collective-permute-start | bytes 786440 | tf_op jit(solution)/shard_map/ppermute | solution.py:33
  77.5 7.7 %collective-permute-start.22 = (bf16[128,1024]{1,0:T(8,128)(2,1)S(1)}, bf16[128,1024]{1,0:T(8,128)(2,1)S(1)}, u32[]{:S(2)}, u32[]{:S(2)}) collective-permute-start(bf16[128,1024]{1,0:T(8,128)(2,1)S(1)} %get-tuple-element.85), channel_id=1, source_target_pairs={{0,1},{1,0},{2,3},{3,2},{4,5},{5,4},{6,7},{7,6},{8,9},{9,8},{10,11... | collective-permute-start | bytes 786440 | tf_op jit(solution)/shard_map/ppermute | solution.py:33
  78.6 14.5 %collective-permute-start.26 = (bf16[128,1024]{1,0:T(8,128)(2,1)S(1)}, bf16[128,1024]{1,0:T(8,128)(2,1)S(1)}, u32[]{:S(2)}, u32[]{:S(2)}) collective-permute-start(bf16[128,1024]{1,0:T(8,128)(2,1)S(1)} %add_convert_fusion), channel_id=1, source_target_pairs={{0,2},{1,3},{2,0},{3,1},{4,6},{5,7},{6,4},{7,5},{8,10},{9,11},{10,... | collective-permute-start | bytes 786440 | tf_op jit(solution)/shard_map/ppermute | solution.py:33
  85.3 10.8 %collective-permute-start.27 = (bf16[128,1024]{1,0:T(8,128)(2,1)S(1)}, bf16[128,1024]{1,0:T(8,128)(2,1)S(1)}, u32[]{:S(2)}, u32[]{:S(2)}) collective-permute-start(bf16[128,1024]{1,0:T(8,128)(2,1)S(1)} %convert_add_fusion.1), channel_id=1, source_target_pairs={{0,6},{1,7},{2,4},{3,5},{4,2},{5,3},{6,0},{7,1},{8,14},{9,15},{10,... | collective-permute-start | bytes 786440 | tf_op jit(solution)/shard_map/ppermute | solution.py:33
  93.2 2.9 %collective-permute-start.24 = (bf16[128,1024]{1,0:T(8,128)(2,1)S(1)}, bf16[128,1024]{1,0:T(8,128)(2,1)S(1)}, u32[]{:S(2)}, u32[]{:S(2)}) collective-permute-start(bf16[128,1024]{1,0:T(8,128)(2,1)S(1)} %get-tuple-element.91), channel_id=1, source_target_pairs={{0,1},{1,0},{2,3},{3,2},{4,5},{5,4},{6,7},{7,6},{8,9},{9,8},{10,11... | collective-permute-start | bytes 786440 | tf_op jit(solution)/shard_map/ppermute | solution.py:33

commit v5 on v4

--- a/solution.py
+++ b/solution.py
@@ -207,7 +207,7 @@
         else:
             kept[j], given[j] = first
         if j:
-            totals[j] = kept[j] + swap(given[j], 1).astype(jnp.float32)
+            totals[j] = kept[j] + swap(after(given[j], *totals.values()), 1).astype(jnp.float32)
         gate = (totals[order[0]],) if place else (given[j],)
     got = {}
     for j in order:

time: 97.4 us -> 97.3 us (level)
  transfers between devices with their start and end apart: 28 -> 28, of which waited for: 15 -> 19; matrix products, arithmetic and copies ran while one was open for 5% -> 5% of each run, Pallas kernels for 19% -> 20%
where the time goes in v5:
time: 97.3 us; the launch traced here: 97.1 us
  waiting for transfers between devices  39.7 us (41%)
  starting transfers between devices  26.3 us (27%)
  Pallas kernels  22.7 us (23%)
  other arithmetic  6.72 us (7%)
  between operations  1.55 us (2%)
    ppermute x28, waiting for transfers between devices, swap(): lax.ppermute(values, 'shard', [(place, place ^ offset) for place in range...  39.7 us
    ppermute x28, starting transfers between devices, swap(): lax.ppermute(values, 'shard', [(place, place ^ offset) for place in range...  26.3 us
    pallas_call x14, Pallas kernels, local_call(): pl.pallas_call(kernel, out_shape=outs, in_specs=[IN_VMEM] * len(operands)...  16.3 us
    pallas_call x1, Pallas kernels, blend(): pl.pallas_call(functools.partial(blend_kernel, blocks), grid=(points // t...  5.81 us
    reduce_sum x3, other arithmetic, rms_unit(): jnp.mean(values * values, axis=-1, keepdims=True) + epsilon  3.16 us
  transfers between devices with their start and end apart: 28, of which 19 were waited for; matrix products, arithmetic and copies ran while one was open for 5% of the time, Pallas kernels for 20%

profile of v5, /device:TPU:0, one launch (start us, length us, event | category | flops | bytes accessed | tf_op | source)
XLA Modules:
  0.0 97.1 jit_solution(11470980511057489700)
XLA Ops:
  0.6 5.1 %collective-permute-start.1 = (bf16[128,1024]{1,0:T(8,128)(2,1)}, bf16[128,1024]{1,0:T(8,128)(2,1)S(1)}, u32[]{:S(2)}, u32[]{:S(2)}) collective-permute-start(bf16[128,1024]{1,0:T(8,128)(2,1)} %bitcast.6), channel_id=1, source_target_pairs={{0,6},{1,7},{2,4},{3,5},{4,2},{5,3},{6,0},{7,1},{8,14},{9,15},{10,... | collective-permute-start | bytes 786440 | tf_op jit(solution)/shard_map/ppermute | solution.py:33
  5.8 1.3 %fusion.2 = s32[]{:T(128)} fusion(s32[4]{0:T(128)} %param.5, s32[]{:T(128)S(6)} %axis_index.23), kind=kLoop, calls=%fused_computation.22 | loop fusion | flops 11 | bytes 24 | tf_op jit(solution)/shard_map/reduce_sum | solution.py:24
  7.7 0.6 live.1
  8.3 2.7 %fusion = f32[1536]{0:T(1024)S(1)} fusion(bf16[1536,1024]{1,0:T(8,128)(2,1)} %bitcast.10), kind=kLoop, calls=%fused_computation.2 | loop fusion | flops 4717056 | bytes 3151872 | tf_op jit(solution)/shard_map/reduce_sum | solution.py:19
  11.1 0.1 copy-done.2
  11.2 0.6 fusion.1.refs_2_.unit
  11.7 1.4 %collective-permute-done.1.refs_0_ = bf16[128,1024]{1,0:T(8,128)(2,1)S(1)} collective-permute-done((bf16[128,1024]{1,0:T(8,128)(2,1)}, bf16[128,1024]{1,0:T(8,128)(2,1)S(1)}, u32[]{:S(2)}, u32[]{:S(2)}) %collective-permute-start.1) | collective-permute-done | bytes 262176 | tf_op jit(solution)/shard_map/ppermute | solution.py:33
  13.1 4.4 %collective-permute-start.2 = (bf16[128,1024]{1,0:T(8,128)(2,1)S(1)}, bf16[128,1024]{1,0:T(8,128)(2,1)S(1)}, u32[]{:S(2)}, u32[]{:S(2)}) collective-permute-start(bf16[128,1024]{1,0:T(8,128)(2,1)S(1)} %collective-permute-done.1.refs_0_), channel_id=1, source_target_pairs={{0,2},{1,3},{2,0},{3,1},{4,6},{5,7},{6,4},{7,5},{8,10},{9,11},{10,... | collective-permute-start | bytes 786440 | tf_op jit(solution)/shard_map/ppermute | solution.py:33
  17.6 0.4 collective-permute-done.3.refs_0_
  18.0 0.1 collective-permute-start.4
  18.1 1.1 %scores.6 = (f32[256,1536]{1,0:T(8,128)S(1)}, f32[1,1536]{1,0:T(1,128)S(1)}) custom-call(bf16[128,1024]{1,0:T(8,128)(2,1)S(1)} %bitcast.9, bf16[128,1024]{1,0:T(8,128)(2,1)S(1)} %collective-permute-done.refs_1_, bf16[1536,1024]{1,0:T(8,128)(2,1)S(1)} %fusion.1.refs_2_.unit), custom_call_target="tpu_custom_call" | custom-call | flops 3221225472 | bytes 5242880 | tf_op jit(solution)/shard_map/scores/pallas_call | solution.py:52
  19.2 0.4 collective-permute-done.4.refs_1_
  19.6 1.1 %scores.7 = (f32[256,1536]{1,0:T(8,128)S(1)}, f32[1,1536]{1,0:T(1,128)S(1)}) custom-call(bf16[128,1024]{1,0:T(8,128)(2,1)S(1)} %collective-permute-done.3.refs_0_, bf16[128,1024]{1,0:T(8,128)(2,1)S(1)} %collective-permute-done.4.refs_1_, bf16[1536,1024]{1,0:T(8,128)(2,1)S(1)} %fusion.1.refs_2_.unit), custom_call_target="tpu_custom_call" | custom-call | flops 3221225472 | bytes 5242880 | tf_op jit(solution)/shard_map/scores/pallas_call | solution.py:52
  20.6 1.1 %scores.8 = (f32[256,1536]{1,0:T(8,128)S(1)}, f32[1,1536]{1,0:T(1,128)S(1)}) custom-call(bf16[128,1024]{1,0:T(8,128)(2,1)S(1)} %collective-permute-done.1.refs_0_, bf16[128,1024]{1,0:T(8,128)(2,1)S(1)} %collective-permute-done.5.refs_1_, bf16[1536,1024]{1,0:T(8,128)(2,1)S(1)} %fusion.1.refs_2_.unit), custom_call_target="tpu_custom_call" | custom-call | flops 3221225472 | bytes 5242880 | tf_op jit(solution)/shard_map/scores/pallas_call | solution.py:52
  21.7 1.9 %collective-permute-done.2.own_rows = bf16[128,1024]{1,0:T(8,128)(2,1)S(1)} collective-permute-done((bf16[128,1024]{1,0:T(8,128)(2,1)S(1)}, bf16[128,1024]{1,0:T(8,128)(2,1)S(1)}, u32[]{:S(2)}, u32[]{:S(2)}) %collective-permute-start.2) | collective-permute-done | bytes 262176 | tf_op jit(solution)/shard_map/ppermute | solution.py:33
  23.6 1.5 %collective-permute-done.6.other_rows = bf16[128,1024]{1,0:T(8,128)(2,1)S(1)} collective-permute-done((bf16[128,1024]{1,0:T(8,128)(2,1)S(1)}, bf16[128,1024]{1,0:T(8,128)(2,1)S(1)}, u32[]{:S(2)}, u32[]{:S(2)}) %collective-permute-start.6) | collective-permute-done | bytes 262176 | tf_op jit(solution)/shard_map/ppermute | solution.py:33
  25.1 1.9 %last.2 = (f32[1,1536]{1,0:T(1,128)S(1)}, f32[128,1024]{1,0:T(8,128)S(1)}, bf16[128,1024]{1,0:T(8,128)(2,1)S(1)}) custom-call(bf16[128,1024]{1,0:T(8,128)(2,1)S(1)} %collective-permute-done.2.own_rows, bf16[128,1024]{1,0:T(8,128)(2,1)S(1)} %collective-permute-done.6.other_rows, bf16[1536,1024]{1,0:T(8,128)(2,1)S(1)} %fusion.1.refs_2_.unit, ...), custom_call_target="tpu_custom_call" | custom-call | flops 3221225472 | bytes 5242880 | tf_op jit(solution)/shard_map/last/pallas_call | solution.py:52
  27.0 0.2 collective-permute-start.7
  27.2 1.0 %sums.7 = (f32[128,1024]{1,0:T(8,128)S(1)}, bf16[128,1024]{1,0:T(8,128)(2,1)S(1)}) custom-call(f32[256,1536]{1,0:T(8,128)S(1)} %get-tuple-element.67.terms, f32[1,1536]{1,0:T(1,128)S(1)} %get-tuple-element.64.factor, bf16[1536,1024]{1,0:T(8,128)(2,1)S(1)} %fusion.1.refs_2_.unit), custom_call_target="tpu_custom_call" | custom-call | flops 3221225472 | bytes 5242880 | tf_op jit(solution)/shard_map/sums/pallas_call | solution.py:52
  28.2 0.4 collective-permute-done.7
  28.6 0.1 convert_add_fusion.6
  28.7 1.7 %collective-permute-start.12 = (bf16[128,1024]{1,0:T(8,128)(2,1)S(1)}, bf16[128,1024]{1,0:T(8,128)(2,1)S(1)}, u32[]{:S(2)}, u32[]{:S(2)}) collective-permute-start(bf16[128,1024]{1,0:T(8,128)(2,1)S(1)} %convert_add_fusion.6), channel_id=1, source_target_pairs={{0,2},{1,3},{2,0},{3,1},{4,6},{5,7},{6,4},{7,5},{8,10},{9,11},{10,... | collective-permute-start | bytes 786440 | tf_op jit(solution)/shard_map/ppermute | solution.py:33
  30.5 1.0 %sums.8 = (f32[128,1024]{1,0:T(8,128)S(1)}, bf16[128,1024]{1,0:T(8,128)(2,1)S(1)}) custom-call(f32[256,1536]{1,0:T(8,128)S(1)} %get-tuple-element.72.terms, f32[1,1536]{1,0:T(1,128)S(1)} %get-tuple-element.64.factor, bf16[1536,1024]{1,0:T(8,128)(2,1)S(1)} %fusion.1.refs_2_.unit), custom_call_target="tpu_custom_call" | custom-call | flops 3221225472 | bytes 5242880 | tf_op jit(solution)/shard_map/sums/pallas_call | solution.py:52
  31.4 0.5 collective-permute-done.9
  32.0 0.1 convert_add_fusion.5
  32.1 0.2 collective-permute-start.11
  32.3 1.0 %sums.6 = (f32[128,1024]{1,0:T(8,128)S(1)}, bf16[128,1024]{1,0:T(8,128)(2,1)S(1)}) custom-call(f32[256,1536]{1,0:T(8,128)S(1)} %get-tuple-element.63.terms, f32[1,1536]{1,0:T(1,128)S(1)} %get-tuple-element.64.factor, bf16[1536,1024]{1,0:T(8,128)(2,1)S(1)} %fusion.1.refs_2_.unit), custom_call_target="tpu_custom_call" | custom-call | flops 3221225472 | bytes 5242880 | tf_op jit(solution)/shard_map/sums/pallas_call | solution.py:52
  33.3 0.4 collective-permute-start.8
  33.7 0.3 collective-permute-start.10
  34.1 3.7 %collective-permute-done.12 = bf16[128,1024]{1,0:T(8,128)(2,1)S(1)} collective-permute-done((bf16[128,1024]{1,0:T(8,128)(2,1)S(1)}, bf16[128,1024]{1,0:T(8,128)(2,1)S(1)}, u32[]{:S(2)}, u32[]{:S(2)}) %collective-permute-start.12) | collective-permute-done | bytes 262176 | tf_op jit(solution)/shard_map/ppermute | solution.py:33
  37.7 0.1 add_convert_fusion
  37.8 2.7 %collective-permute-start.13 = (bf16[128,1024]{1,0:T(8,128)(2,1)S(1)}, bf16[128,1024]{1,0:T(8,128)(2,1)S(1)}, u32[]{:S(2)}, u32[]{:S(2)}) collective-permute-start(bf16[128,1024]{1,0:T(8,128)(2,1)S(1)} %add_convert_fusion), channel_id=1, source_target_pairs={{0,6},{1,7},{2,4},{3,5},{4,2},{5,3},{6,0},{7,1},{8,14},{9,15},{10,... | collective-permute-start | bytes 786440 | tf_op jit(solution)/shard_map/ppermute | solution.py:33
  40.5 2.2 %collective-permute-done.10 = bf16[128,1024]{1,0:T(8,128)(2,1)S(1)} collective-permute-done((bf16[128,1024]{1,0:T(8,128)(2,1)S(1)}, bf16[128,1024]{1,0:T(8,128)(2,1)S(1)}, u32[]{:S(2)}, u32[]{:S(2)}) %collective-permute-start.10) | collective-permute-done | bytes 262176 | tf_op jit(solution)/shard_map/ppermute | solution.py:33
  42.7 7.3 %collective-permute-done.13 = bf16[128,1024]{1,0:T(8,128)(2,1)S(1)} collective-permute-done((bf16[128,1024]{1,0:T(8,128)(2,1)S(1)}, bf16[128,1024]{1,0:T(8,128)(2,1)S(1)}, u32[]{:S(2)}, u32[]{:S(2)}) %collective-permute-start.13) | collective-permute-done | bytes 262176 | tf_op jit(solution)/shard_map/ppermute | solution.py:33
  50.1 0.2 multiply_reduce_fusion.1
  50.3 0.2 multiply_convert_fusion.refs_0_
  50.5 1.9 %collective-permute-start.15 = (bf16[128,1024]{1,0:T(8,128)(2,1)S(1)}, bf16[128,1024]{1,0:T(8,128)(2,1)S(1)}, u32[]{:S(2)}, u32[]{:S(2)}) collective-permute-start(bf16[128,1024]{1,0:T(8,128)(2,1)S(1)} %multiply_convert_fusion.refs_0_), channel_id=1, source_target_pairs={{0,6},{1,7},{2,4},{3,5},{4,2},{5,3},{6,0},{7,1},{8,14},{9,15},{10,... | collective-permute-start | bytes 786440 | tf_op jit(solution)/shard_map/ppermute | solution.py:33
  52.4 2.8 %collective-permute-start.17 = (bf16[128,1024]{1,0:T(8,128)(2,1)S(1)}, bf16[128,1024]{1,0:T(8,128)(2,1)S(1)}, u32[]{:S(2)}, u32[]{:S(2)}) collective-permute-start(bf16[128,1024]{1,0:T(8,128)(2,1)S(1)} %multiply_convert_fusion.refs_0_), channel_id=1, source_target_pairs={{0,2},{1,3},{2,0},{3,1},{4,6},{5,7},{6,4},{7,5},{8,10},{9,11},{10,... | collective-permute-start | bytes 786440 | tf_op jit(solution)/shard_map/ppermute | solution.py:33
  55.2 6.4 %collective-permute-done.15.refs_0_ = bf16[128,1024]{1,0:T(8,128)(2,1)S(1)} collective-permute-done((bf16[128,1024]{1,0:T(8,128)(2,1)S(1)}, bf16[128,1024]{1,0:T(8,128)(2,1)S(1)}, u32[]{:S(2)}, u32[]{:S(2)}) %collective-permute-start.15) | collective-permute-done | bytes 262176 | tf_op jit(solution)/shard_map/ppermute | solution.py:33
  61.6 1.8 %collective-permute-start.16 = (bf16[128,1024]{1,0:T(8,128)(2,1)S(1)}, bf16[128,1024]{1,0:T(8,128)(2,1)S(1)}, u32[]{:S(2)}, u32[]{:S(2)}) collective-permute-start(bf16[128,1024]{1,0:T(8,128)(2,1)S(1)} %collective-permute-done.15.refs_0_), channel_id=1, source_target_pairs={{0,2},{1,3},{2,0},{3,1},{4,6},{5,7},{6,4},{7,5},{8,10},{9,11},{10,... | collective-permute-start | bytes 786440 | tf_op jit(solution)/shard_map/ppermute | solution.py:33
  63.4 2.3 %collective-permute-done.17.refs_0_ = bf16[128,1024]{1,0:T(8,128)(2,1)S(1)} collective-permute-done((bf16[128,1024]{1,0:T(8,128)(2,1)S(1)}, bf16[128,1024]{1,0:T(8,128)(2,1)S(1)}, u32[]{:S(2)}, u32[]{:S(2)}) %collective-permute-start.17) | collective-permute-done | bytes 262176 | tf_op jit(solution)/shard_map/ppermute | solution.py:33
  65.6 1.1 %scores.9 = (f32[256,1536]{1,0:T(8,128)S(1)}, f32[1,1536]{1,0:T(1,128)S(1)}) custom-call(bf16[128,1024]{1,0:T(8,128)(2,1)S(1)} %multiply_convert_fusion.refs_0_, bf16[128,1024]{1,0:T(8,128)(2,1)S(1)} %collective-permute-done.14.refs_1_, bf16[1536,1024]{1,0:T(8,128)(2,1)S(1)} %fusion.1.refs_2_.unit), custom_call_target="tpu_custom_call" | custom-call | flops 3221225472 | bytes 5242880 | tf_op jit(solution)/shard_map/scores/pallas_call | solution.py:52
  66.7 0.5 collective-permute-done.18.refs_1_
  67.2 1.1 %scores.10 = (f32[256,1536]{1,0:T(8,128)S(1)}, f32[1,1536]{1,0:T(1,128)S(1)}) custom-call(bf16[128,1024]{1,0:T(8,128)(2,1)S(1)} %collective-permute-done.17.refs_0_, bf16[128,1024]{1,0:T(8,128)(2,1)S(1)} %collective-permute-done.18.refs_1_, bf16[1536,1024]{1,0:T(8,128)(2,1)S(1)} %fusion.1.refs_2_.unit), custom_call_target="tpu_custom_call" | custom-call | flops 3221225472 | bytes 5242880 | tf_op jit(solution)/shard_map/scores/pallas_call | solution.py:52
  68.2 1.3 %scores.11 = (f32[256,1536]{1,0:T(8,128)S(1)}, f32[1,1536]{1,0:T(1,128)S(1)}) custom-call(bf16[128,1024]{1,0:T(8,128)(2,1)S(1)} %collective-permute-done.15.refs_0_, bf16[128,1024]{1,0:T(8,128)(2,1)S(1)} %collective-permute-done.19.refs_1_, bf16[1536,1024]{1,0:T(8,128)(2,1)S(1)} %fusion.1.refs_2_.unit), custom_call_target="tpu_custom_call" | custom-call | flops 3221225472 | bytes 5242880 | tf_op jit(solution)/shard_map/scores/pallas_call | solution.py:52
  69.5 1.3 %collective-permute-done.16.own_rows = bf16[128,1024]{1,0:T(8,128)(2,1)S(1)} collective-permute-done((bf16[128,1024]{1,0:T(8,128)(2,1)S(1)}, bf16[128,1024]{1,0:T(8,128)(2,1)S(1)}, u32[]{:S(2)}, u32[]{:S(2)}) %collective-permute-start.16) | collective-permute-done | bytes 262176 | tf_op jit(solution)/shard_map/ppermute | solution.py:33
  70.9 1.4 %collective-permute-done.20.other_rows = bf16[128,1024]{1,0:T(8,128)(2,1)S(1)} collective-permute-done((bf16[128,1024]{1,0:T(8,128)(2,1)S(1)}, bf16[128,1024]{1,0:T(8,128)(2,1)S(1)}, u32[]{:S(2)}, u32[]{:S(2)}) %collective-permute-start.20) | collective-permute-done | bytes 262176 | tf_op jit(solution)/shard_map/ppermute | solution.py:33
  72.3 1.8 %last.3 = (f32[256,1536]{1,0:T(8,128)S(1)}, f32[1,1536]{1,0:T(1,128)S(1)}, f32[128,1024]{1,0:T(8,128)S(1)}, bf16[128,1024]{1,0:T(8,128)(2,1)S(1)}) custom-call(bf16[128,1024]{1,0:T(8,128)(2,1)S(1)} %collective-permute-done.16.own_rows, bf16[128,1024]{1,0:T(8,128)(2,1)S(1)} %collective-permute-done.20.other_rows, bf16[1536,1024]{1,0:T(8,128)(2,1)S(1)} %fusion.1.refs_2_.unit, ...), custom_call_target="tpu_custom_call" | custom-call | flops 3221225472 | bytes 5242880 | tf_op jit(solution)/shard_map/last/pallas_call | solution.py:52
  74.2 0.2 collective-permute-start.21
  74.4 1.0 %sums.11 = (f32[128,1024]{1,0:T(8,128)S(1)}, bf16[128,1024]{1,0:T(8,128)(2,1)S(1)}) custom-call(f32[256,1536]{1,0:T(8,128)S(1)} %get-tuple-element.98.terms.refs_1_, f32[1,1536]{1,0:T(1,128)S(1)} %get-tuple-element.86.factor.refs_8_, bf16[1536,1024]{1,0:T(8,128)(2,1)S(1)} %fusion.1.refs_2_.unit), custom_call_target="tpu_custom_call" | custom-call | flops 3221225472 | bytes 5242880 | tf_op jit(solution)/shard_map/sums/pallas_call | solution.py:52
  75.4 0.4 collective-permute-done.21
  75.9 0.5 collective-permute-start.24
  76.3 1.0 %sums.10 = (f32[128,1024]{1,0:T(8,128)S(1)}, bf16[128,1024]{1,0:T(8,128)(2,1)S(1)}) custom-call(f32[256,1536]{1,0:T(8,128)S(1)} %get-tuple-element.99.terms.refs_2_, f32[1,1536]{1,0:T(1,128)S(1)} %get-tuple-element.86.factor.refs_8_, bf16[1536,1024]{1,0:T(8,128)(2,1)S(1)} %fusion.1.refs_2_.unit), custom_call_target="tpu_custom_call" | custom-call | flops 3221225472 | bytes 5242880 | tf_op jit(solution)/shard_map/sums/pallas_call | solution.py:52
  77.3 0.5 collective-permute-done.22
  77.9 0.2 collective-permute-start.23
  78.1 1.0 %sums.9 = (f32[128,1024]{1,0:T(8,128)S(1)}, bf16[128,1024]{1,0:T(8,128)(2,1)S(1)}) custom-call(f32[256,1536]{1,0:T(8,128)S(1)} %get-tuple-element.97.terms.refs_0_, f32[1,1536]{1,0:T(1,128)S(1)} %get-tuple-element.86.factor.refs_8_, bf16[1536,1024]{1,0:T(8,128)(2,1)S(1)} %fusion.1.refs_2_.unit), custom_call_target="tpu_custom_call" | custom-call | flops 3221225472 | bytes 5242880 | tf_op jit(solution)/shard_map/sums/pallas_call | solution.py:52
  79.1 1.7 %collective-permute-start.26 = (bf16[128,1024]{1,0:T(8,128)(2,1)S(1)}, bf16[128,1024]{1,0:T(8,128)(2,1)S(1)}, u32[]{:S(2)}, u32[]{:S(2)}) collective-permute-start(bf16[128,1024]{1,0:T(8,128)(2,1)S(1)} %convert_add_fusion.2), channel_id=1, source_target_pairs={{0,2},{1,3},{2,0},{3,1},{4,6},{5,7},{6,4},{7,5},{8,10},{9,11},{10,... | collective-permute-start | bytes 786440 | tf_op jit(solution)/shard_map/ppermute | solution.py:33
  80.8 4.2 %collective-permute-done.24 = bf16[128,1024]{1,0:T(8,128)(2,1)S(1)} collective-permute-done((bf16[128,1024]{1,0:T(8,128)(2,1)S(1)}, bf16[128,1024]{1,0:T(8,128)(2,1)S(1)}, u32[]{:S(2)}, u32[]{:S(2)}) %collective-permute-start.24) | collective-permute-done | bytes 262176 | tf_op jit(solution)/shard_map/ppermute | solution.py:33
  85.1 0.1 convert_add_fusion.1
  85.2 2.0 %collective-permute-start.27 = (bf16[128,1024]{1,0:T(8,128)(2,1)S(1)}, bf16[128,1024]{1,0:T(8,128)(2,1)S(1)}, u32[]{:S(2)}, u32[]{:S(2)}) collective-permute-start(bf16[128,1024]{1,0:T(8,128)(2,1)S(1)} %convert_add_fusion.1), channel_id=1, source_target_pairs={{0,6},{1,7},{2,4},{3,5},{4,2},{5,3},{6,0},{7,1},{8,14},{9,15},{10,... | collective-permute-start | bytes 786440 | tf_op jit(solution)/shard_map/ppermute | solution.py:33
  87.2 5.8 %blend.1 = bf16[1536,1024]{1,0:T(8,128)(2,1)} custom-call(f32[256,1536]{1,0:T(8,128)S(1)} %get-tuple-element.97.terms.refs_0_, f32[256,1536]{1,0:T(8,128)S(1)} %get-tuple-element.98.terms.refs_1_, f32[256,1536]{1,0:T(8,128)S(1)} %get-tuple-element.99.terms.refs_2_, f32[256,1536]{1,0:T(8,128)S(1)} %get-tuple-element.101.refs_3_, ...), custom_call_target="tpu_custom_call" | custom-call | flops 12884901888 | bytes 5242880 | tf_op jit(solution)/shard_map/blend/pallas_call | solution.py:157
  93.0 2.9 %collective-permute-done.27 = bf16[128,1024]{1,0:T(8,128)(2,1)S(1)} collective-permute-done((bf16[128,1024]{1,0:T(8,128)(2,1)S(1)}, bf16[128,1024]{1,0:T(8,128)(2,1)S(1)}, u32[]{:S(2)}, u32[]{:S(2)}) %collective-permute-start.27) | collective-permute-done | bytes 262176 | tf_op jit(solution)/shard_map/ppermute | solution.py:33
  96.0 0.2 multiply_reduce_fusion
  96.2 0.9 multiply_bitcast_fusion
  (34 shorter events, 0.3 us)
Async XLA Ops:
  0.6 12.5 %collective-permute-start.1 = (bf16[128,1024]{1,0:T(8,128)(2,1)}, bf16[128,1024]{1,0:T(8,128)(2,1)S(1)}, u32[]{:S(2)}, u32[]{:S(2)}) collective-permute-start(bf16[128,1024]{1,0:T(8,128)(2,1)} %bitcast.6), channel_id=1, source_target_pairs={{0,6},{1,7},{2,4},{3,5},{4,2},{5,3},{6,0},{7,1},{8,14},{9,15},{10,... | collective-permute-start | bytes 786440 | tf_op jit(solution)/shard_map/ppermute | solution.py:33
  5.7 12.4 %collective-permute-start = (bf16[128,1024]{1,0:T(8,128)(2,1)}, bf16[128,1024]{1,0:T(8,128)(2,1)S(1)}, u32[]{:S(2)}, u32[]{:S(2)}) collective-permute-start(bf16[128,1024]{1,0:T(8,128)(2,1)} %bitcast.7), channel_id=1, source_target_pairs={{0,1},{1,0},{2,3},{3,2},{4,5},{5,4},{6,7},{7,6},{8,9},{9,8},{10,11... | collective-permute-start | bytes 786440 | tf_op jit(solution)/shard_map/ppermute | solution.py:33
  5.7 12.3 %collective-permute-start.3 = (bf16[128,1024]{1,0:T(8,128)(2,1)}, bf16[128,1024]{1,0:T(8,128)(2,1)S(1)}, u32[]{:S(2)}, u32[]{:S(2)}) collective-permute-start(bf16[128,1024]{1,0:T(8,128)(2,1)} %bitcast.8), channel_id=1, source_target_pairs={{0,2},{1,3},{2,0},{3,1},{4,6},{5,7},{6,4},{7,5},{8,10},{9,11},{10,... | collective-permute-start | bytes 786440 | tf_op jit(solution)/shard_map/ppermute | solution.py:33
  8.3 2.8 %copy-start.2 = (bf16[1,1536,1024]{2,1,0:T(8,128)(2,1)S(1)}, bf16[1,1536,1024]{2,1,0:T(8,128)(2,1)}, u32[]{:S(2)}) copy-start(bf16[1,1536,1024]{2,1,0:T(8,128)(2,1)} %param.3) | copy-start | bytes 9437188
  11.2 7.0 %copy-start.1 = (bf16[1,128,1024]{2,1,0:T(8,128)(2,1)S(1)}, bf16[1,128,1024]{2,1,0:T(8,128)(2,1)}, u32[]{:S(2)}) copy-start(bf16[1,128,1024]{2,1,0:T(8,128)(2,1)} %param.4) | copy-start | bytes 786436
  13.1 10.5 %collective-permute-start.2 = (bf16[128,1024]{1,0:T(8,128)(2,1)S(1)}, bf16[128,1024]{1,0:T(8,128)(2,1)S(1)}, u32[]{:S(2)}, u32[]{:S(2)}) collective-permute-start(bf16[128,1024]{1,0:T(8,128)(2,1)S(1)} %collective-permute-done.1.refs_0_), channel_id=1, source_target_pairs={{0,2},{1,3},{2,0},{3,1},{4,6},{5,7},{6,4},{7,5},{8,10},{9,11},{10,... | collective-permute-start | bytes 786440 | tf_op jit(solution)/shard_map/ppermute | solution.py:33
  17.6 3.0 %collective-permute-start.5 = (bf16[128,1024]{1,0:T(8,128)(2,1)S(1)}, bf16[128,1024]{1,0:T(8,128)(2,1)S(1)}, u32[]{:S(2)}, u32[]{:S(2)}) collective-permute-start(bf16[128,1024]{1,0:T(8,128)(2,1)S(1)} %collective-permute-done.1.refs_0_), channel_id=1, source_target_pairs={{0,1},{1,0},{2,3},{3,2},{4,5},{5,4},{6,7},{7,6},{8,9},{9,8},{10,11... | collective-permute-start | bytes 786440 | tf_op jit(solution)/shard_map/ppermute | solution.py:33
  18.0 1.5 %collective-permute-start.4 = (bf16[128,1024]{1,0:T(8,128)(2,1)S(1)}, bf16[128,1024]{1,0:T(8,128)(2,1)S(1)}, u32[]{:S(2)}, u32[]{:S(2)}) collective-permute-start(bf16[128,1024]{1,0:T(8,128)(2,1)S(1)} %collective-permute-done.3.refs_0_), channel_id=1, source_target_pairs={{0,1},{1,0},{2,3},{3,2},{4,5},{5,4},{6,7},{7,6},{8,9},{9,8},{10,11... | collective-permute-start | bytes 786440 | tf_op jit(solution)/shard_map/ppermute | solution.py:33
  20.6 4.5 %copy-start = (f32[1,1536]{1,0:T(1,128)S(1)}, f32[1,1536]{1,0:T(1,128)}, u32[]{:S(2)}) copy-start(f32[1,1536]{1,0:T(1,128)} %live.1) | copy-start | bytes 18436
  23.6 1.5 %collective-permute-start.6 = (bf16[128,1024]{1,0:T(8,128)(2,1)S(1)}, bf16[128,1024]{1,0:T(8,128)(2,1)S(1)}, u32[]{:S(2)}, u32[]{:S(2)}) collective-permute-start(bf16[128,1024]{1,0:T(8,128)(2,1)S(1)} %collective-permute-done.2.own_rows), channel_id=1, source_target_pairs={{0,1},{1,0},{2,3},{3,2},{4,5},{5,4},{6,7},{7,6},{8,9},{9,8},{10,11... | collective-permute-start | bytes 786440 | tf_op jit(solution)/shard_map/ppermute | solution.py:33
  27.0 1.6 %collective-permute-start.7 = (bf16[128,1024]{1,0:T(8,128)(2,1)S(1)}, bf16[128,1024]{1,0:T(8,128)(2,1)S(1)}, u32[]{:S(2)}, u32[]{:S(2)}) collective-permute-start(bf16[128,1024]{1,0:T(8,128)(2,1)S(1)} %get-tuple-element.62), channel_id=1, source_target_pairs={{0,1},{1,0},{2,3},{3,2},{4,5},{5,4},{6,7},{7,6},{8,9},{9,8},{10,11... | collective-permute-start | bytes 786440 | tf_op jit(solution)/shard_map/ppermute | solution.py:33
  28.7 9.0 %collective-permute-start.12 = (bf16[128,1024]{1,0:T(8,128)(2,1)S(1)}, bf16[128,1024]{1,0:T(8,128)(2,1)S(1)}, u32[]{:S(2)}, u32[]{:S(2)}) collective-permute-start(bf16[128,1024]{1,0:T(8,128)(2,1)S(1)} %convert_add_fusion.6), channel_id=1, source_target_pairs={{0,2},{1,3},{2,0},{3,1},{4,6},{5,7},{6,4},{7,5},{8,10},{9,11},{10,... | collective-permute-start | bytes 786440 | tf_op jit(solution)/shard_map/ppermute | solution.py:33
  30.4 1.5 %collective-permute-start.9 = (bf16[128,1024]{1,0:T(8,128)(2,1)S(1)}, bf16[128,1024]{1,0:T(8,128)(2,1)S(1)}, u32[]{:S(2)}, u32[]{:S(2)}) collective-permute-start(bf16[128,1024]{1,0:T(8,128)(2,1)S(1)} %get-tuple-element.70), channel_id=1, source_target_pairs={{0,1},{1,0},{2,3},{3,2},{4,5},{5,4},{6,7},{7,6},{8,9},{9,8},{10,11... | collective-permute-start | bytes 786440 | tf_op jit(solution)/shard_map/ppermute | solution.py:33
  32.1 5.7 %collective-permute-start.11 = (bf16[128,1024]{1,0:T(8,128)(2,1)S(1)}, bf16[128,1024]{1,0:T(8,128)(2,1)S(1)}, u32[]{:S(2)}, u32[]{:S(2)}) collective-permute-start(bf16[128,1024]{1,0:T(8,128)(2,1)S(1)} %get-tuple-element.75), channel_id=1, source_target_pairs={{0,1},{1,0},{2,3},{3,2},{4,5},{5,4},{6,7},{7,6},{8,9},{9,8},{10,11... | collective-permute-start | bytes 786440 | tf_op jit(solution)/shard_map/ppermute | solution.py:33
  33.3 7.2 %collective-permute-start.8 = (bf16[128,1024]{1,0:T(8,128)(2,1)S(1)}, bf16[128,1024]{1,0:T(8,128)(2,1)S(1)}, u32[]{:S(2)}, u32[]{:S(2)}) collective-permute-start(bf16[128,1024]{1,0:T(8,128)(2,1)S(1)} %get-tuple-element.66), channel_id=1, source_target_pairs={{0,1},{1,0},{2,3},{3,2},{4,5},{5,4},{6,7},{7,6},{8,9},{9,8},{10,11... | collective-permute-start | bytes 786440 | tf_op jit(solution)/shard_map/ppermute | solution.py:33
  33.7 9.0 %collective-permute-start.10 = (bf16[128,1024]{1,0:T(8,128)(2,1)S(1)}, bf16[128,1024]{1,0:T(8,128)(2,1)S(1)}, u32[]{:S(2)}, u32[]{:S(2)}) collective-permute-start(bf16[128,1024]{1,0:T(8,128)(2,1)S(1)} %convert_add_fusion.5), channel_id=1, source_target_pairs={{0,2},{1,3},{2,0},{3,1},{4,6},{5,7},{6,4},{7,5},{8,10},{9,11},{10,... | collective-permute-start | bytes 786440 | tf_op jit(solution)/shard_map/ppermute | solution.py:33
  37.8 12.2 %collective-permute-start.13 = (bf16[128,1024]{1,0:T(8,128)(2,1)S(1)}, bf16[128,1024]{1,0:T(8,128)(2,1)S(1)}, u32[]{:S(2)}, u32[]{:S(2)}) collective-permute-start(bf16[128,1024]{1,0:T(8,128)(2,1)S(1)} %add_convert_fusion), channel_id=1, source_target_pairs={{0,6},{1,7},{2,4},{3,5},{4,2},{5,3},{6,0},{7,1},{8,14},{9,15},{10,... | collective-permute-start | bytes 786440 | tf_op jit(solution)/shard_map/ppermute | solution.py:33
  50.5 11.1 %collective-permute-start.15 = (bf16[128,1024]{1,0:T(8,128)(2,1)S(1)}, bf16[128,1024]{1,0:T(8,128)(2,1)S(1)}, u32[]{:S(2)}, u32[]{:S(2)}) collective-permute-start(bf16[128,1024]{1,0:T(8,128)(2,1)S(1)} %multiply_convert_fusion.refs_0_), channel_id=1, source_target_pairs={{0,6},{1,7},{2,4},{3,5},{4,2},{5,3},{6,0},{7,1},{8,14},{9,15},{10,... | collective-permute-start | bytes 786440 | tf_op jit(solution)/shard_map/ppermute | solution.py:33
  52.4 13.2 %collective-permute-start.17 = (bf16[128,1024]{1,0:T(8,128)(2,1)S(1)}, bf16[128,1024]{1,0:T(8,128)(2,1)S(1)}, u32[]{:S(2)}, u32[]{:S(2)}) collective-permute-start(bf16[128,1024]{1,0:T(8,128)(2,1)S(1)} %multiply_convert_fusion.refs_0_), channel_id=1, source_target_pairs={{0,2},{1,3},{2,0},{3,1},{4,6},{5,7},{6,4},{7,5},{8,10},{9,11},{10,... | collective-permute-start | bytes 786440 | tf_op jit(solution)/shard_map/ppermute | solution.py:33
  55.2 10.5 %collective-permute-start.14 = (bf16[128,1024]{1,0:T(8,128)(2,1)S(1)}, bf16[128,1024]{1,0:T(8,128)(2,1)S(1)}, u32[]{:S(2)}, u32[]{:S(2)}) collective-permute-start(bf16[128,1024]{1,0:T(8,128)(2,1)S(1)} %multiply_convert_fusion.refs_0_), channel_id=1, source_target_pairs={{0,1},{1,0},{2,3},{3,2},{4,5},{5,4},{6,7},{7,6},{8,9},{9,8},{10,11... | collective-permute-start | bytes 786440 | tf_op jit(solution)/shard_map/ppermute | solution.py:33
  61.6 9.2 %collective-permute-start.16 = (bf16[128,1024]{1,0:T(8,128)(2,1)S(1)}, bf16[128,1024]{1,0:T(8,128)(2,1)S(1)}, u32[]{:S(2)}, u32[]{:S(2)}) collective-permute-start(bf16[128,1024]{1,0:T(8,128)(2,1)S(1)} %collective-permute-done.15.refs_0_), channel_id=1, source_target_pairs={{0,2},{1,3},{2,0},{3,1},{4,6},{5,7},{6,4},{7,5},{8,10},{9,11},{10,... | collective-permute-start | bytes 786440 | tf_op jit(solution)/shard_map/ppermute | solution.py:33
  63.4 4.9 %collective-permute-start.19 = (bf16[128,1024]{1,0:T(8,128)(2,1)S(1)}, bf16[128,1024]{1,0:T(8,128)(2,1)S(1)}, u32[]{:S(2)}, u32[]{:S(2)}) collective-permute-start(bf16[128,1024]{1,0:T(8,128)(2,1)S(1)} %collective-permute-done.15.refs_0_), channel_id=1, source_target_pairs={{0,1},{1,0},{2,3},{3,2},{4,5},{5,4},{6,7},{7,6},{8,9},{9,8},{10,11... | collective-permute-start | bytes 786440 | tf_op jit(solution)/shard_map/ppermute | solution.py:33
  65.6 1.5 %collective-permute-start.18 = (bf16[128,1024]{1,0:T(8,128)(2,1)S(1)}, bf16[128,1024]{1,0:T(8,128)(2,1)S(1)}, u32[]{:S(2)}, u32[]{:S(2)}) collective-permute-start(bf16[128,1024]{1,0:T(8,128)(2,1)S(1)} %collective-permute-done.17.refs_0_), channel_id=1, source_target_pairs={{0,1},{1,0},{2,3},{3,2},{4,5},{5,4},{6,7},{7,6},{8,9},{9,8},{10,11... | collective-permute-start | bytes 786440 | tf_op jit(solution)/shard_map/ppermute | solution.py:33
  70.8 1.5 %collective-permute-start.20 = (bf16[128,1024]{1,0:T(8,128)(2,1)S(1)}, bf16[128,1024]{1,0:T(8,128)(2,1)S(1)}, u32[]{:S(2)}, u32[]{:S(2)}) collective-permute-start(bf16[128,1024]{1,0:T(8,128)(2,1)S(1)} %collective-permute-done.16.own_rows), channel_id=1, source_target_pairs={{0,1},{1,0},{2,3},{3,2},{4,5},{5,4},{6,7},{7,6},{8,9},{9,8},{10,11... | collective-permute-start | bytes 786440 | tf_op jit(solution)/shard_map/ppermute | solution.py:33
  74.2 1.6 %collective-permute-start.21 = (bf16[128,1024]{1,0:T(8,128)(2,1)S(1)}, bf16[128,1024]{1,0:T(8,128)(2,1)S(1)}, u32[]{:S(2)}, u32[]{:S(2)}) collective-permute-start(bf16[128,1024]{1,0:T(8,128)(2,1)S(1)} %get-tuple-element.84), channel_id=1, source_target_pairs={{0,1},{1,0},{2,3},{3,2},{4,5},{5,4},{6,7},{7,6},{8,9},{9,8},{10,11... | collective-permute-start | bytes 786440 | tf_op jit(solution)/shard_map/ppermute | solution.py:33
  75.9 9.2 %collective-permute-start.24 = (bf16[128,1024]{1,0:T(8,128)(2,1)S(1)}, bf16[128,1024]{1,0:T(8,128)(2,1)S(1)}, u32[]{:S(2)}, u32[]{:S(2)}) collective-permute-start(bf16[128,1024]{1,0:T(8,128)(2,1)S(1)} %convert_add_fusion.3), channel_id=1, source_target_pairs={{0,2},{1,3},{2,0},{3,1},{4,6},{5,7},{6,4},{7,5},{8,10},{9,11},{10,... | collective-permute-start | bytes 786440 | tf_op jit(solution)/shard_map/ppermute | solution.py:33
  76.3 1.5 %collective-permute-start.22 = (bf16[128,1024]{1,0:T(8,128)(2,1)S(1)}, bf16[128,1024]{1,0:T(8,128)(2,1)S(1)}, u32[]{:S(2)}, u32[]{:S(2)}) collective-permute-start(bf16[128,1024]{1,0:T(8,128)(2,1)S(1)} %get-tuple-element.95), channel_id=1, source_target_pairs={{0,1},{1,0},{2,3},{3,2},{4,5},{5,4},{6,7},{7,6},{8,9},{9,8},{10,11... | collective-permute-start | bytes 786440 | tf_op jit(solution)/shard_map/ppermute | solution.py:33
  77.9 7.2 %collective-permute-start.23 = (bf16[128,1024]{1,0:T(8,128)(2,1)S(1)}, bf16[128,1024]{1,0:T(8,128)(2,1)S(1)}, u32[]{:S(2)}, u32[]{:S(2)}) collective-permute-start(bf16[128,1024]{1,0:T(8,128)(2,1)S(1)} %get-tuple-element.96), channel_id=1, source_target_pairs={{0,1},{1,0},{2,3},{3,2},{4,5},{5,4},{6,7},{7,6},{8,9},{9,8},{10,11... | collective-permute-start | bytes 786440 | tf_op jit(solution)/shard_map/ppermute | solution.py:33
  79.1 13.9 %collective-permute-start.26 = (bf16[128,1024]{1,0:T(8,128)(2,1)S(1)}, bf16[128,1024]{1,0:T(8,128)(2,1)S(1)}, u32[]{:S(2)}, u32[]{:S(2)}) collective-permute-start(bf16[128,1024]{1,0:T(8,128)(2,1)S(1)} %convert_add_fusion.2), channel_id=1, source_target_pairs={{0,2},{1,3},{2,0},{3,1},{4,6},{5,7},{6,4},{7,5},{8,10},{9,11},{10,... | collective-permute-start | bytes 786440 | tf_op jit(solution)/shard_map/ppermute | solution.py:33
  85.2 10.8 %collective-permute-start.27 = (bf16[128,1024]{1,0:T(8,128)(2,1)S(1)}, bf16[128,1024]{1,0:T(8,128)(2,1)S(1)}, u32[]{:S(2)}, u32[]{:S(2)}) collective-permute-start(bf16[128,1024]{1,0:T(8,128)(2,1)S(1)} %convert_add_fusion.1), channel_id=1, source_target_pairs={{0,6},{1,7},{2,4},{3,5},{4,2},{5,3},{6,0},{7,1},{8,14},{9,15},{10,... | collective-permute-start | bytes 786440 | tf_op jit(solution)/shard_map/ppermute | solution.py:33
  93.0 2.9 %collective-permute-start.25 = (bf16[128,1024]{1,0:T(8,128)(2,1)S(1)}, bf16[128,1024]{1,0:T(8,128)(2,1)S(1)}, u32[]{:S(2)}, u32[]{:S(2)}) collective-permute-start(bf16[128,1024]{1,0:T(8,128)(2,1)S(1)} %get-tuple-element.102), channel_id=1, source_target_pairs={{0,1},{1,0},{2,3},{3,2},{4,5},{5,4},{6,7},{7,6},{8,9},{9,8},{10,11... | collective-permute-start | bytes 786440 | tf_op jit(solution)/shard_map/ppermute | solution.py:33

commit v6 on v4

--- a/solution.py
+++ b/solution.py
@@ -13,6 +13,7 @@
 
 sharpness_factor = 48.0
 epsilon = 1e-06
+LOG2_E = 1.4426950408889634
 
 
 def rms_unit(values):
@@ -81,7 +82,7 @@
     scores = lax.dot_general(
         table, unit[...], (((1,), (1,)), ((), ())), preferred_element_type=jnp.float32
     )
-    raised = jnp.exp(scores * (sharpness_factor / unit.shape[1]))
+    raised = jnp.exp2(scores * (sharpness_factor * LOG2_E / unit.shape[1]))
     terms[...] = raised
     normal[...] = jnp.sum(raised, axis=0, keepdims=True)
 
@@ -117,7 +118,7 @@
     scores = lax.dot_general(
         table, unit[...], (((1,), (1,)), ((), ())), preferred_element_type=jnp.float32
     )
-    raised = jnp.exp(scores * (sharpness_factor / unit.shape[1]))
+    raised = jnp.exp2(scores * (sharpness_factor * LOG2_E / unit.shape[1]))
     for terms in kept_terms:
         terms[...] = raised
     normal = jnp.sum(raised, axis=0, keepdims=True) + sum(n[...] for n in normals)

time: 97.4 us -> 97.3 us (level)
  no operation moved by 1% of the time
where the time goes in v6:
time: 97.3 us; the launch traced here: 97.2 us
  waiting for transfers between devices  39.7 us (41%)
  starting transfers between devices  26.5 us (27%)
  Pallas kernels  22.5 us (23%)
  other arithmetic  6.76 us (7%)
  between operations  1.59 us (2%)
    ppermute x28, waiting for transfers between devices, swap(): lax.ppermute(values, 'shard', [(place, place ^ offset) for place in range...  39.7 us
    ppermute x28, starting transfers between devices, swap(): lax.ppermute(values, 'shard', [(place, place ^ offset) for place in range...  26.5 us
    pallas_call x14, Pallas kernels, local_call(): pl.pallas_call(kernel, out_shape=outs, in_specs=[IN_VMEM] * len(operands)...  16.1 us
    pallas_call x1, Pallas kernels, blend(): pl.pallas_call(functools.partial(blend_kernel, blocks), grid=(points // t...  5.82 us
    reduce_sum x3, other arithmetic, rms_unit(): jnp.mean(values * values, axis=-1, keepdims=True) + epsilon  3.16 us
  transfers between devices with their start and end apart: 28, of which 15 were waited for; matrix products, arithmetic and copies ran while one was open for 5% of the time, Pallas kernels for 19%

profile of v6, /device:TPU:0, one launch (start us, length us, event | category | flops | bytes accessed | tf_op | source)
XLA Modules:
  0.0 97.2 jit_solution(2365640175411209954)
XLA Ops:
  0.6 5.1 %collective-permute-start.1 = (bf16[128,1024]{1,0:T(8,128)(2,1)}, bf16[128,1024]{1,0:T(8,128)(2,1)S(1)}, u32[]{:S(2)}, u32[]{:S(2)}) collective-permute-start(bf16[128,1024]{1,0:T(8,128)(2,1)} %bitcast.6), channel_id=1, source_target_pairs={{0,6},{1,7},{2,4},{3,5},{4,2},{5,3},{6,0},{7,1},{8,14},{9,15},{10,... | collective-permute-start | bytes 786440 | tf_op jit(solution)/shard_map/ppermute | solution.py:34
  5.8 1.3 %fusion.2 = s32[]{:T(128)} fusion(s32[4]{0:T(128)} %param.5, s32[]{:T(128)S(6)} %axis_index.23), kind=kLoop, calls=%fused_computation.22 | loop fusion | flops 11 | bytes 24 | tf_op jit(solution)/shard_map/reduce_sum | solution.py:25
  7.7 0.6 live.1
  8.3 2.7 %fusion = f32[1536]{0:T(1024)S(1)} fusion(bf16[1536,1024]{1,0:T(8,128)(2,1)} %bitcast.10), kind=kLoop, calls=%fused_computation.2 | loop fusion | flops 4717056 | bytes 3151872 | tf_op jit(solution)/shard_map/reduce_sum | solution.py:20
  11.1 0.1 copy-done.2
  11.2 0.6 fusion.1.refs_2_.unit
  11.7 1.4 %collective-permute-done.1.refs_0_ = bf16[128,1024]{1,0:T(8,128)(2,1)S(1)} collective-permute-done((bf16[128,1024]{1,0:T(8,128)(2,1)}, bf16[128,1024]{1,0:T(8,128)(2,1)S(1)}, u32[]{:S(2)}, u32[]{:S(2)}) %collective-permute-start.1) | collective-permute-done | bytes 262176 | tf_op jit(solution)/shard_map/ppermute | solution.py:34
  13.1 4.4 %collective-permute-start.2 = (bf16[128,1024]{1,0:T(8,128)(2,1)S(1)}, bf16[128,1024]{1,0:T(8,128)(2,1)S(1)}, u32[]{:S(2)}, u32[]{:S(2)}) collective-permute-start(bf16[128,1024]{1,0:T(8,128)(2,1)S(1)} %collective-permute-done.1.refs_0_), channel_id=1, source_target_pairs={{0,2},{1,3},{2,0},{3,1},{4,6},{5,7},{6,4},{7,5},{8,10},{9,11},{10,... | collective-permute-start | bytes 786440 | tf_op jit(solution)/shard_map/ppermute | solution.py:34
  17.6 0.4 collective-permute-done.3.refs_0_
  18.0 0.1 collective-permute-start.4
  18.1 1.0 %scores.6 = (f32[256,1536]{1,0:T(8,128)S(1)}, f32[1,1536]{1,0:T(1,128)S(1)}) custom-call(bf16[128,1024]{1,0:T(8,128)(2,1)S(1)} %bitcast.9, bf16[128,1024]{1,0:T(8,128)(2,1)S(1)} %collective-permute-done.refs_1_, bf16[1536,1024]{1,0:T(8,128)(2,1)S(1)} %fusion.1.refs_2_.unit), custom_call_target="tpu_custom_call" | custom-call | flops 3221225472 | bytes 5242880 | tf_op jit(solution)/shard_map/scores/pallas_call | solution.py:53
  19.2 0.4 collective-permute-done.4.refs_1_
  19.6 1.0 %scores.7 = (f32[256,1536]{1,0:T(8,128)S(1)}, f32[1,1536]{1,0:T(1,128)S(1)}) custom-call(bf16[128,1024]{1,0:T(8,128)(2,1)S(1)} %collective-permute-done.3.refs_0_, bf16[128,1024]{1,0:T(8,128)(2,1)S(1)} %collective-permute-done.4.refs_1_, bf16[1536,1024]{1,0:T(8,128)(2,1)S(1)} %fusion.1.refs_2_.unit), custom_call_target="tpu_custom_call" | custom-call | flops 3221225472 | bytes 5242880 | tf_op jit(solution)/shard_map/scores/pallas_call | solution.py:53
  20.6 1.0 %scores.8 = (f32[256,1536]{1,0:T(8,128)S(1)}, f32[1,1536]{1,0:T(1,128)S(1)}) custom-call(bf16[128,1024]{1,0:T(8,128)(2,1)S(1)} %collective-permute-done.1.refs_0_, bf16[128,1024]{1,0:T(8,128)(2,1)S(1)} %collective-permute-done.5.refs_1_, bf16[1536,1024]{1,0:T(8,128)(2,1)S(1)} %fusion.1.refs_2_.unit), custom_call_target="tpu_custom_call" | custom-call | flops 3221225472 | bytes 5242880 | tf_op jit(solution)/shard_map/scores/pallas_call | solution.py:53
  21.7 1.9 %collective-permute-done.2.own_rows = bf16[128,1024]{1,0:T(8,128)(2,1)S(1)} collective-permute-done((bf16[128,1024]{1,0:T(8,128)(2,1)S(1)}, bf16[128,1024]{1,0:T(8,128)(2,1)S(1)}, u32[]{:S(2)}, u32[]{:S(2)}) %collective-permute-start.2) | collective-permute-done | bytes 262176 | tf_op jit(solution)/shard_map/ppermute | solution.py:34
  23.6 1.5 %collective-permute-done.6.other_rows = bf16[128,1024]{1,0:T(8,128)(2,1)S(1)} collective-permute-done((bf16[128,1024]{1,0:T(8,128)(2,1)S(1)}, bf16[128,1024]{1,0:T(8,128)(2,1)S(1)}, u32[]{:S(2)}, u32[]{:S(2)}) %collective-permute-start.6) | collective-permute-done | bytes 262176 | tf_op jit(solution)/shard_map/ppermute | solution.py:34
  25.1 1.9 %last.2 = (f32[1,1536]{1,0:T(1,128)S(1)}, f32[128,1024]{1,0:T(8,128)S(1)}, bf16[128,1024]{1,0:T(8,128)(2,1)S(1)}) custom-call(bf16[128,1024]{1,0:T(8,128)(2,1)S(1)} %collective-permute-done.2.own_rows, bf16[128,1024]{1,0:T(8,128)(2,1)S(1)} %collective-permute-done.6.other_rows, bf16[1536,1024]{1,0:T(8,128)(2,1)S(1)} %fusion.1.refs_2_.unit, ...), custom_call_target="tpu_custom_call" | custom-call | flops 3221225472 | bytes 5242880 | tf_op jit(solution)/shard_map/last/pallas_call | solution.py:53
  27.0 0.2 collective-permute-start.7
  27.2 1.0 %sums.7 = (f32[128,1024]{1,0:T(8,128)S(1)}, bf16[128,1024]{1,0:T(8,128)(2,1)S(1)}) custom-call(f32[256,1536]{1,0:T(8,128)S(1)} %get-tuple-element.63.terms, f32[1,1536]{1,0:T(1,128)S(1)} %get-tuple-element.60.factor, bf16[1536,1024]{1,0:T(8,128)(2,1)S(1)} %fusion.1.refs_2_.unit), custom_call_target="tpu_custom_call" | custom-call | flops 3221225472 | bytes 5242880 | tf_op jit(solution)/shard_map/sums/pallas_call | solution.py:53
  28.2 0.4 collective-permute-start.9
  28.7 0.1 convert_add_fusion.4
  28.7 1.7 %collective-permute-start.12 = (bf16[128,1024]{1,0:T(8,128)(2,1)S(1)}, bf16[128,1024]{1,0:T(8,128)(2,1)S(1)}, u32[]{:S(2)}, u32[]{:S(2)}) collective-permute-start(bf16[128,1024]{1,0:T(8,128)(2,1)S(1)} %convert_add_fusion.4), channel_id=1, source_target_pairs={{0,2},{1,3},{2,0},{3,1},{4,6},{5,7},{6,4},{7,5},{8,10},{9,11},{10,... | collective-permute-start | bytes 786440 | tf_op jit(solution)/shard_map/ppermute | solution.py:34
  30.5 1.0 %sums.8 = (f32[128,1024]{1,0:T(8,128)S(1)}, bf16[128,1024]{1,0:T(8,128)(2,1)S(1)}) custom-call(f32[256,1536]{1,0:T(8,128)S(1)} %get-tuple-element.67.terms, f32[1,1536]{1,0:T(1,128)S(1)} %get-tuple-element.60.factor, bf16[1536,1024]{1,0:T(8,128)(2,1)S(1)} %fusion.1.refs_2_.unit), custom_call_target="tpu_custom_call" | custom-call | flops 3221225472 | bytes 5242880 | tf_op jit(solution)/shard_map/sums/pallas_call | solution.py:53
  31.5 0.1 collective-permute-start.11
  31.6 1.0 %sums.6 = (f32[128,1024]{1,0:T(8,128)S(1)}, bf16[128,1024]{1,0:T(8,128)(2,1)S(1)}) custom-call(f32[256,1536]{1,0:T(8,128)S(1)} %get-tuple-element.59.terms, f32[1,1536]{1,0:T(1,128)S(1)} %get-tuple-element.60.factor, bf16[1536,1024]{1,0:T(8,128)(2,1)S(1)} %fusion.1.refs_2_.unit), custom_call_target="tpu_custom_call" | custom-call | flops 3221225472 | bytes 5242880 | tf_op jit(solution)/shard_map/sums/pallas_call | solution.py:53
  32.6 0.1 add_convert_fusion.2
  32.6 0.4 collective-permute-start.10
  33.1 0.2 collective-permute-start.8
  33.3 4.7 %collective-permute-done.12 = bf16[128,1024]{1,0:T(8,128)(2,1)S(1)} collective-permute-done((bf16[128,1024]{1,0:T(8,128)(2,1)S(1)}, bf16[128,1024]{1,0:T(8,128)(2,1)S(1)}, u32[]{:S(2)}, u32[]{:S(2)}) %collective-permute-start.12) | collective-permute-done | bytes 262176 | tf_op jit(solution)/shard_map/ppermute | solution.py:34
  38.0 0.1 add_convert_fusion.1
  38.1 2.5 %collective-permute-start.13 = (bf16[128,1024]{1,0:T(8,128)(2,1)S(1)}, bf16[128,1024]{1,0:T(8,128)(2,1)S(1)}, u32[]{:S(2)}, u32[]{:S(2)}) collective-permute-start(bf16[128,1024]{1,0:T(8,128)(2,1)S(1)} %add_convert_fusion.1), channel_id=1, source_target_pairs={{0,6},{1,7},{2,4},{3,5},{4,2},{5,3},{6,0},{7,1},{8,14},{9,15},{10,... | collective-permute-start | bytes 786440 | tf_op jit(solution)/shard_map/ppermute | solution.py:34
  40.5 2.2 %collective-permute-done.10 = bf16[128,1024]{1,0:T(8,128)(2,1)S(1)} collective-permute-done((bf16[128,1024]{1,0:T(8,128)(2,1)S(1)}, bf16[128,1024]{1,0:T(8,128)(2,1)S(1)}, u32[]{:S(2)}, u32[]{:S(2)}) %collective-permute-start.10) | collective-permute-done | bytes 262176 | tf_op jit(solution)/shard_map/ppermute | solution.py:34
  42.8 7.3 %collective-permute-done.13 = bf16[128,1024]{1,0:T(8,128)(2,1)S(1)} collective-permute-done((bf16[128,1024]{1,0:T(8,128)(2,1)S(1)}, bf16[128,1024]{1,0:T(8,128)(2,1)S(1)}, u32[]{:S(2)}, u32[]{:S(2)}) %collective-permute-start.13) | collective-permute-done | bytes 262176 | tf_op jit(solution)/shard_map/ppermute | solution.py:34
  50.1 0.2 multiply_reduce_fusion.1
  50.3 0.2 multiply_convert_fusion.refs_0_
  50.5 1.9 %collective-permute-start.15 = (bf16[128,1024]{1,0:T(8,128)(2,1)S(1)}, bf16[128,1024]{1,0:T(8,128)(2,1)S(1)}, u32[]{:S(2)}, u32[]{:S(2)}) collective-permute-start(bf16[128,1024]{1,0:T(8,128)(2,1)S(1)} %multiply_convert_fusion.refs_0_), channel_id=1, source_target_pairs={{0,6},{1,7},{2,4},{3,5},{4,2},{5,3},{6,0},{7,1},{8,14},{9,15},{10,... | collective-permute-start | bytes 786440 | tf_op jit(solution)/shard_map/ppermute | solution.py:34
  52.4 2.7 %collective-permute-start.17 = (bf16[128,1024]{1,0:T(8,128)(2,1)S(1)}, bf16[128,1024]{1,0:T(8,128)(2,1)S(1)}, u32[]{:S(2)}, u32[]{:S(2)}) collective-permute-start(bf16[128,1024]{1,0:T(8,128)(2,1)S(1)} %multiply_convert_fusion.refs_0_), channel_id=1, source_target_pairs={{0,2},{1,3},{2,0},{3,1},{4,6},{5,7},{6,4},{7,5},{8,10},{9,11},{10,... | collective-permute-start | bytes 786440 | tf_op jit(solution)/shard_map/ppermute | solution.py:34
  55.2 6.4 %collective-permute-done.15.refs_0_ = bf16[128,1024]{1,0:T(8,128)(2,1)S(1)} collective-permute-done((bf16[128,1024]{1,0:T(8,128)(2,1)S(1)}, bf16[128,1024]{1,0:T(8,128)(2,1)S(1)}, u32[]{:S(2)}, u32[]{:S(2)}) %collective-permute-start.15) | collective-permute-done | bytes 262176 | tf_op jit(solution)/shard_map/ppermute | solution.py:34
  61.6 1.8 %collective-permute-start.16 = (bf16[128,1024]{1,0:T(8,128)(2,1)S(1)}, bf16[128,1024]{1,0:T(8,128)(2,1)S(1)}, u32[]{:S(2)}, u32[]{:S(2)}) collective-permute-start(bf16[128,1024]{1,0:T(8,128)(2,1)S(1)} %collective-permute-done.15.refs_0_), channel_id=1, source_target_pairs={{0,2},{1,3},{2,0},{3,1},{4,6},{5,7},{6,4},{7,5},{8,10},{9,11},{10,... | collective-permute-start | bytes 786440 | tf_op jit(solution)/shard_map/ppermute | solution.py:34
  63.4 2.3 %collective-permute-done.17.refs_0_ = bf16[128,1024]{1,0:T(8,128)(2,1)S(1)} collective-permute-done((bf16[128,1024]{1,0:T(8,128)(2,1)S(1)}, bf16[128,1024]{1,0:T(8,128)(2,1)S(1)}, u32[]{:S(2)}, u32[]{:S(2)}) %collective-permute-start.17) | collective-permute-done | bytes 262176 | tf_op jit(solution)/shard_map/ppermute | solution.py:34
  65.6 1.0 %scores.9 = (f32[256,1536]{1,0:T(8,128)S(1)}, f32[1,1536]{1,0:T(1,128)S(1)}) custom-call(bf16[128,1024]{1,0:T(8,128)(2,1)S(1)} %multiply_convert_fusion.refs_0_, bf16[128,1024]{1,0:T(8,128)(2,1)S(1)} %collective-permute-done.14.refs_1_, bf16[1536,1024]{1,0:T(8,128)(2,1)S(1)} %fusion.1.refs_2_.unit), custom_call_target="tpu_custom_call" | custom-call | flops 3221225472 | bytes 5242880 | tf_op jit(solution)/shard_map/scores/pallas_call | solution.py:53
  66.7 0.5 collective-permute-done.18.refs_1_
  67.2 1.0 %scores.10 = (f32[256,1536]{1,0:T(8,128)S(1)}, f32[1,1536]{1,0:T(1,128)S(1)}) custom-call(bf16[128,1024]{1,0:T(8,128)(2,1)S(1)} %collective-permute-done.17.refs_0_, bf16[128,1024]{1,0:T(8,128)(2,1)S(1)} %collective-permute-done.18.refs_1_, bf16[1536,1024]{1,0:T(8,128)(2,1)S(1)} %fusion.1.refs_2_.unit), custom_call_target="tpu_custom_call" | custom-call | flops 3221225472 | bytes 5242880 | tf_op jit(solution)/shard_map/scores/pallas_call | solution.py:53
  68.2 1.2 %scores.11 = (f32[256,1536]{1,0:T(8,128)S(1)}, f32[1,1536]{1,0:T(1,128)S(1)}) custom-call(bf16[128,1024]{1,0:T(8,128)(2,1)S(1)} %collective-permute-done.15.refs_0_, bf16[128,1024]{1,0:T(8,128)(2,1)S(1)} %collective-permute-done.19.refs_1_, bf16[1536,1024]{1,0:T(8,128)(2,1)S(1)} %fusion.1.refs_2_.unit), custom_call_target="tpu_custom_call" | custom-call | flops 3221225472 | bytes 5242880 | tf_op jit(solution)/shard_map/scores/pallas_call | solution.py:53
  69.4 1.4 %collective-permute-done.16.own_rows = bf16[128,1024]{1,0:T(8,128)(2,1)S(1)} collective-permute-done((bf16[128,1024]{1,0:T(8,128)(2,1)S(1)}, bf16[128,1024]{1,0:T(8,128)(2,1)S(1)}, u32[]{:S(2)}, u32[]{:S(2)}) %collective-permute-start.16) | collective-permute-done | bytes 262176 | tf_op jit(solution)/shard_map/ppermute | solution.py:34
  71.0 1.4 %collective-permute-done.20.other_rows = bf16[128,1024]{1,0:T(8,128)(2,1)S(1)} collective-permute-done((bf16[128,1024]{1,0:T(8,128)(2,1)S(1)}, bf16[128,1024]{1,0:T(8,128)(2,1)S(1)}, u32[]{:S(2)}, u32[]{:S(2)}) %collective-permute-start.20) | collective-permute-done | bytes 262176 | tf_op jit(solution)/shard_map/ppermute | solution.py:34
  72.4 1.8 %last.3 = (f32[256,1536]{1,0:T(8,128)S(1)}, f32[1,1536]{1,0:T(1,128)S(1)}, f32[128,1024]{1,0:T(8,128)S(1)}, bf16[128,1024]{1,0:T(8,128)(2,1)S(1)}) custom-call(bf16[128,1024]{1,0:T(8,128)(2,1)S(1)} %collective-permute-done.16.own_rows, bf16[128,1024]{1,0:T(8,128)(2,1)S(1)} %collective-permute-done.20.other_rows, bf16[1536,1024]{1,0:T(8,128)(2,1)S(1)} %fusion.1.refs_2_.unit, ...), custom_call_target="tpu_custom_call" | custom-call | flops 3221225472 | bytes 5242880 | tf_op jit(solution)/shard_map/last/pallas_call | solution.py:53
  74.2 0.2 collective-permute-start.21
  74.4 1.0 %sums.11 = (f32[128,1024]{1,0:T(8,128)S(1)}, bf16[128,1024]{1,0:T(8,128)(2,1)S(1)}) custom-call(f32[256,1536]{1,0:T(8,128)S(1)} %get-tuple-element.87.refs_1_.terms, f32[1,1536]{1,0:T(1,128)S(1)} %get-tuple-element.80.factor.refs_8_, bf16[1536,1024]{1,0:T(8,128)(2,1)S(1)} %fusion.1.refs_2_.unit), custom_call_target="tpu_custom_call" | custom-call | flops 3221225472 | bytes 5242880 | tf_op jit(solution)/shard_map/sums/pallas_call | solution.py:53
  75.4 0.4 collective-permute-start.25
  75.9 0.1 convert_add_fusion.2
  76.0 0.4 collective-permute-start.23
  76.4 1.0 %sums.10 = (f32[128,1024]{1,0:T(8,128)S(1)}, bf16[128,1024]{1,0:T(8,128)(2,1)S(1)}) custom-call(f32[256,1536]{1,0:T(8,128)S(1)} %get-tuple-element.88.terms.refs_2_, f32[1,1536]{1,0:T(1,128)S(1)} %get-tuple-element.80.factor.refs_8_, bf16[1536,1024]{1,0:T(8,128)(2,1)S(1)} %fusion.1.refs_2_.unit), custom_call_target="tpu_custom_call" | custom-call | flops 3221225472 | bytes 5242880 | tf_op jit(solution)/shard_map/sums/pallas_call | solution.py:53
  77.4 0.1 collective-permute-start.22
  77.5 1.0 %sums.9 = (f32[128,1024]{1,0:T(8,128)S(1)}, bf16[128,1024]{1,0:T(8,128)(2,1)S(1)}) custom-call(f32[256,1536]{1,0:T(8,128)S(1)} %get-tuple-element.86.terms.refs_0_, f32[1,1536]{1,0:T(1,128)S(1)} %get-tuple-element.80.factor.refs_8_, bf16[1536,1024]{1,0:T(8,128)(2,1)S(1)} %fusion.1.refs_2_.unit), custom_call_target="tpu_custom_call" | custom-call | flops 3221225472 | bytes 5242880 | tf_op jit(solution)/shard_map/sums/pallas_call | solution.py:53
  78.5 0.1 add_convert_fusion
  78.6 1.7 %collective-permute-start.26 = (bf16[128,1024]{1,0:T(8,128)(2,1)S(1)}, bf16[128,1024]{1,0:T(8,128)(2,1)S(1)}, u32[]{:S(2)}, u32[]{:S(2)}) collective-permute-start(bf16[128,1024]{1,0:T(8,128)(2,1)S(1)} %add_convert_fusion), channel_id=1, source_target_pairs={{0,2},{1,3},{2,0},{3,1},{4,6},{5,7},{6,4},{7,5},{8,10},{9,11},{10,... | collective-permute-start | bytes 786440 | tf_op jit(solution)/shard_map/ppermute | solution.py:34
  80.3 4.9 %collective-permute-done.23 = bf16[128,1024]{1,0:T(8,128)(2,1)S(1)} collective-permute-done((bf16[128,1024]{1,0:T(8,128)(2,1)S(1)}, bf16[128,1024]{1,0:T(8,128)(2,1)S(1)}, u32[]{:S(2)}, u32[]{:S(2)}) %collective-permute-start.23) | collective-permute-done | bytes 262176 | tf_op jit(solution)/shard_map/ppermute | solution.py:34
  85.2 0.1 convert_add_fusion.1
  85.3 2.0 %collective-permute-start.27 = (bf16[128,1024]{1,0:T(8,128)(2,1)S(1)}, bf16[128,1024]{1,0:T(8,128)(2,1)S(1)}, u32[]{:S(2)}, u32[]{:S(2)}) collective-permute-start(bf16[128,1024]{1,0:T(8,128)(2,1)S(1)} %convert_add_fusion.1), channel_id=1, source_target_pairs={{0,6},{1,7},{2,4},{3,5},{4,2},{5,3},{6,0},{7,1},{8,14},{9,15},{10,... | collective-permute-start | bytes 786440 | tf_op jit(solution)/shard_map/ppermute | solution.py:34
  87.3 5.8 %blend.1 = bf16[1536,1024]{1,0:T(8,128)(2,1)} custom-call(f32[256,1536]{1,0:T(8,128)S(1)} %get-tuple-element.86.terms.refs_0_, f32[256,1536]{1,0:T(8,128)S(1)} %get-tuple-element.87.refs_1_.terms, f32[256,1536]{1,0:T(8,128)S(1)} %get-tuple-element.88.terms.refs_2_, f32[256,1536]{1,0:T(8,128)S(1)} %get-tuple-element.90.refs_3_, ...), custom_call_target="tpu_custom_call" | custom-call | flops 12884901888 | bytes 5242880 | tf_op jit(solution)/shard_map/blend/pallas_call | solution.py:158
  93.2 2.9 %collective-permute-done.27 = bf16[128,1024]{1,0:T(8,128)(2,1)S(1)} collective-permute-done((bf16[128,1024]{1,0:T(8,128)(2,1)S(1)}, bf16[128,1024]{1,0:T(8,128)(2,1)S(1)}, u32[]{:S(2)}, u32[]{:S(2)}) %collective-permute-start.27) | collective-permute-done | bytes 262176 | tf_op jit(solution)/shard_map/ppermute | solution.py:34
  96.0 0.2 multiply_reduce_fusion
  96.3 0.9 multiply_bitcast_fusion
  (34 shorter events, 0.2 us)
Async XLA Ops:
  0.6 12.5 %collective-permute-start.1 = (bf16[128,1024]{1,0:T(8,128)(2,1)}, bf16[128,1024]{1,0:T(8,128)(2,1)S(1)}, u32[]{:S(2)}, u32[]{:S(2)}) collective-permute-start(bf16[128,1024]{1,0:T(8,128)(2,1)} %bitcast.6), channel_id=1, source_target_pairs={{0,6},{1,7},{2,4},{3,5},{4,2},{5,3},{6,0},{7,1},{8,14},{9,15},{10,... | collective-permute-start | bytes 786440 | tf_op jit(solution)/shard_map/ppermute | solution.py:34
  5.7 12.4 %collective-permute-start = (bf16[128,1024]{1,0:T(8,128)(2,1)}, bf16[128,1024]{1,0:T(8,128)(2,1)S(1)}, u32[]{:S(2)}, u32[]{:S(2)}) collective-permute-start(bf16[128,1024]{1,0:T(8,128)(2,1)} %bitcast.7), channel_id=1, source_target_pairs={{0,1},{1,0},{2,3},{3,2},{4,5},{5,4},{6,7},{7,6},{8,9},{9,8},{10,11... | collective-permute-start | bytes 786440 | tf_op jit(solution)/shard_map/ppermute | solution.py:34
  5.7 12.3 %collective-permute-start.3 = (bf16[128,1024]{1,0:T(8,128)(2,1)}, bf16[128,1024]{1,0:T(8,128)(2,1)S(1)}, u32[]{:S(2)}, u32[]{:S(2)}) collective-permute-start(bf16[128,1024]{1,0:T(8,128)(2,1)} %bitcast.8), channel_id=1, source_target_pairs={{0,2},{1,3},{2,0},{3,1},{4,6},{5,7},{6,4},{7,5},{8,10},{9,11},{10,... | collective-permute-start | bytes 786440 | tf_op jit(solution)/shard_map/ppermute | solution.py:34
  8.3 2.8 %copy-start.2 = (bf16[1,1536,1024]{2,1,0:T(8,128)(2,1)S(1)}, bf16[1,1536,1024]{2,1,0:T(8,128)(2,1)}, u32[]{:S(2)}) copy-start(bf16[1,1536,1024]{2,1,0:T(8,128)(2,1)} %param.3) | copy-start | bytes 9437188
  11.2 7.0 %copy-start.1 = (bf16[1,128,1024]{2,1,0:T(8,128)(2,1)S(1)}, bf16[1,128,1024]{2,1,0:T(8,128)(2,1)}, u32[]{:S(2)}) copy-start(bf16[1,128,1024]{2,1,0:T(8,128)(2,1)} %param.4) | copy-start | bytes 786436
  13.1 10.5 %collective-permute-start.2 = (bf16[128,1024]{1,0:T(8,128)(2,1)S(1)}, bf16[128,1024]{1,0:T(8,128)(2,1)S(1)}, u32[]{:S(2)}, u32[]{:S(2)}) collective-permute-start(bf16[128,1024]{1,0:T(8,128)(2,1)S(1)} %collective-permute-done.1.refs_0_), channel_id=1, source_target_pairs={{0,2},{1,3},{2,0},{3,1},{4,6},{5,7},{6,4},{7,5},{8,10},{9,11},{10,... | collective-permute-start | bytes 786440 | tf_op jit(solution)/shard_map/ppermute | solution.py:34
  17.6 3.0 %collective-permute-start.5 = (bf16[128,1024]{1,0:T(8,128)(2,1)S(1)}, bf16[128,1024]{1,0:T(8,128)(2,1)S(1)}, u32[]{:S(2)}, u32[]{:S(2)}) collective-permute-start(bf16[128,1024]{1,0:T(8,128)(2,1)S(1)} %collective-permute-done.1.refs_0_), channel_id=1, source_target_pairs={{0,1},{1,0},{2,3},{3,2},{4,5},{5,4},{6,7},{7,6},{8,9},{9,8},{10,11... | collective-permute-start | bytes 786440 | tf_op jit(solution)/shard_map/ppermute | solution.py:34
  18.0 1.5 %collective-permute-start.4 = (bf16[128,1024]{1,0:T(8,128)(2,1)S(1)}, bf16[128,1024]{1,0:T(8,128)(2,1)S(1)}, u32[]{:S(2)}, u32[]{:S(2)}) collective-permute-start(bf16[128,1024]{1,0:T(8,128)(2,1)S(1)} %collective-permute-done.3.refs_0_), channel_id=1, source_target_pairs={{0,1},{1,0},{2,3},{3,2},{4,5},{5,4},{6,7},{7,6},{8,9},{9,8},{10,11... | collective-permute-start | bytes 786440 | tf_op jit(solution)/shard_map/ppermute | solution.py:34
  20.6 4.5 %copy-start = (f32[1,1536]{1,0:T(1,128)S(1)}, f32[1,1536]{1,0:T(1,128)}, u32[]{:S(2)}) copy-start(f32[1,1536]{1,0:T(1,128)} %live.1) | copy-start | bytes 18436
  23.6 1.5 %collective-permute-start.6 = (bf16[128,1024]{1,0:T(8,128)(2,1)S(1)}, bf16[128,1024]{1,0:T(8,128)(2,1)S(1)}, u32[]{:S(2)}, u32[]{:S(2)}) collective-permute-start(bf16[128,1024]{1,0:T(8,128)(2,1)S(1)} %collective-permute-done.2.own_rows), channel_id=1, source_target_pairs={{0,1},{1,0},{2,3},{3,2},{4,5},{5,4},{6,7},{7,6},{8,9},{9,8},{10,11... | collective-permute-start | bytes 786440 | tf_op jit(solution)/shard_map/ppermute | solution.py:34
  27.0 1.6 %collective-permute-start.7 = (bf16[128,1024]{1,0:T(8,128)(2,1)S(1)}, bf16[128,1024]{1,0:T(8,128)(2,1)S(1)}, u32[]{:S(2)}, u32[]{:S(2)}) collective-permute-start(bf16[128,1024]{1,0:T(8,128)(2,1)S(1)} %get-tuple-element.58), channel_id=1, source_target_pairs={{0,1},{1,0},{2,3},{3,2},{4,5},{5,4},{6,7},{7,6},{8,9},{9,8},{10,11... | collective-permute-start | bytes 786440 | tf_op jit(solution)/shard_map/ppermute | solution.py:34
  28.2 4.4 %collective-permute-start.9 = (bf16[128,1024]{1,0:T(8,128)(2,1)S(1)}, bf16[128,1024]{1,0:T(8,128)(2,1)S(1)}, u32[]{:S(2)}, u32[]{:S(2)}) collective-permute-start(bf16[128,1024]{1,0:T(8,128)(2,1)S(1)} %get-tuple-element.65), channel_id=1, source_target_pairs={{0,1},{1,0},{2,3},{3,2},{4,5},{5,4},{6,7},{7,6},{8,9},{9,8},{10,11... | collective-permute-start | bytes 786440 | tf_op jit(solution)/shard_map/ppermute | solution.py:34
  28.7 9.2 %collective-permute-start.12 = (bf16[128,1024]{1,0:T(8,128)(2,1)S(1)}, bf16[128,1024]{1,0:T(8,128)(2,1)S(1)}, u32[]{:S(2)}, u32[]{:S(2)}) collective-permute-start(bf16[128,1024]{1,0:T(8,128)(2,1)S(1)} %convert_add_fusion.4), channel_id=1, source_target_pairs={{0,2},{1,3},{2,0},{3,1},{4,6},{5,7},{6,4},{7,5},{8,10},{9,11},{10,... | collective-permute-start | bytes 786440 | tf_op jit(solution)/shard_map/ppermute | solution.py:34
  31.5 6.5 %collective-permute-start.11 = (bf16[128,1024]{1,0:T(8,128)(2,1)S(1)}, bf16[128,1024]{1,0:T(8,128)(2,1)S(1)}, u32[]{:S(2)}, u32[]{:S(2)}) collective-permute-start(bf16[128,1024]{1,0:T(8,128)(2,1)S(1)} %get-tuple-element.69), channel_id=1, source_target_pairs={{0,1},{1,0},{2,3},{3,2},{4,5},{5,4},{6,7},{7,6},{8,9},{9,8},{10,11... | collective-permute-start | bytes 786440 | tf_op jit(solution)/shard_map/ppermute | solution.py:34
  32.6 10.1 %collective-permute-start.10 = (bf16[128,1024]{1,0:T(8,128)(2,1)S(1)}, bf16[128,1024]{1,0:T(8,128)(2,1)S(1)}, u32[]{:S(2)}, u32[]{:S(2)}) collective-permute-start(bf16[128,1024]{1,0:T(8,128)(2,1)S(1)} %add_convert_fusion.2), channel_id=1, source_target_pairs={{0,2},{1,3},{2,0},{3,1},{4,6},{5,7},{6,4},{7,5},{8,10},{9,11},{10,... | collective-permute-start | bytes 786440 | tf_op jit(solution)/shard_map/ppermute | solution.py:34
  33.1 9.7 %collective-permute-start.8 = (bf16[128,1024]{1,0:T(8,128)(2,1)S(1)}, bf16[128,1024]{1,0:T(8,128)(2,1)S(1)}, u32[]{:S(2)}, u32[]{:S(2)}) collective-permute-start(bf16[128,1024]{1,0:T(8,128)(2,1)S(1)} %get-tuple-element.62), channel_id=1, source_target_pairs={{0,1},{1,0},{2,3},{3,2},{4,5},{5,4},{6,7},{7,6},{8,9},{9,8},{10,11... | collective-permute-start | bytes 786440 | tf_op jit(solution)/shard_map/ppermute | solution.py:34
  38.1 12.0 %collective-permute-start.13 = (bf16[128,1024]{1,0:T(8,128)(2,1)S(1)}, bf16[128,1024]{1,0:T(8,128)(2,1)S(1)}, u32[]{:S(2)}, u32[]{:S(2)}) collective-permute-start(bf16[128,1024]{1,0:T(8,128)(2,1)S(1)} %add_convert_fusion.1), channel_id=1, source_target_pairs={{0,6},{1,7},{2,4},{3,5},{4,2},{5,3},{6,0},{7,1},{8,14},{9,15},{10,... | collective-permute-start | bytes 786440 | tf_op jit(solution)/shard_map/ppermute | solution.py:34
  50.5 11.1 %collective-permute-start.15 = (bf16[128,1024]{1,0:T(8,128)(2,1)S(1)}, bf16[128,1024]{1,0:T(8,128)(2,1)S(1)}, u32[]{:S(2)}, u32[]{:S(2)}) collective-permute-start(bf16[128,1024]{1,0:T(8,128)(2,1)S(1)} %multiply_convert_fusion.refs_0_), channel_id=1, source_target_pairs={{0,6},{1,7},{2,4},{3,5},{4,2},{5,3},{6,0},{7,1},{8,14},{9,15},{10,... | collective-permute-start | bytes 786440 | tf_op jit(solution)/shard_map/ppermute | solution.py:34
  52.4 13.2 %collective-permute-start.17 = (bf16[128,1024]{1,0:T(8,128)(2,1)S(1)}, bf16[128,1024]{1,0:T(8,128)(2,1)S(1)}, u32[]{:S(2)}, u32[]{:S(2)}) collective-permute-start(bf16[128,1024]{1,0:T(8,128)(2,1)S(1)} %multiply_convert_fusion.refs_0_), channel_id=1, source_target_pairs={{0,2},{1,3},{2,0},{3,1},{4,6},{5,7},{6,4},{7,5},{8,10},{9,11},{10,... | collective-permute-start | bytes 786440 | tf_op jit(solution)/shard_map/ppermute | solution.py:34
  55.2 10.5 %collective-permute-start.14 = (bf16[128,1024]{1,0:T(8,128)(2,1)S(1)}, bf16[128,1024]{1,0:T(8,128)(2,1)S(1)}, u32[]{:S(2)}, u32[]{:S(2)}) collective-permute-start(bf16[128,1024]{1,0:T(8,128)(2,1)S(1)} %multiply_convert_fusion.refs_0_), channel_id=1, source_target_pairs={{0,1},{1,0},{2,3},{3,2},{4,5},{5,4},{6,7},{7,6},{8,9},{9,8},{10,11... | collective-permute-start | bytes 786440 | tf_op jit(solution)/shard_map/ppermute | solution.py:34
  61.6 9.2 %collective-permute-start.16 = (bf16[128,1024]{1,0:T(8,128)(2,1)S(1)}, bf16[128,1024]{1,0:T(8,128)(2,1)S(1)}, u32[]{:S(2)}, u32[]{:S(2)}) collective-permute-start(bf16[128,1024]{1,0:T(8,128)(2,1)S(1)} %collective-permute-done.15.refs_0_), channel_id=1, source_target_pairs={{0,2},{1,3},{2,0},{3,1},{4,6},{5,7},{6,4},{7,5},{8,10},{9,11},{10,... | collective-permute-start | bytes 786440 | tf_op jit(solution)/shard_map/ppermute | solution.py:34
  63.4 4.8 %collective-permute-start.19 = (bf16[128,1024]{1,0:T(8,128)(2,1)S(1)}, bf16[128,1024]{1,0:T(8,128)(2,1)S(1)}, u32[]{:S(2)}, u32[]{:S(2)}) collective-permute-start(bf16[128,1024]{1,0:T(8,128)(2,1)S(1)} %collective-permute-done.15.refs_0_), channel_id=1, source_target_pairs={{0,1},{1,0},{2,3},{3,2},{4,5},{5,4},{6,7},{7,6},{8,9},{9,8},{10,11... | collective-permute-start | bytes 786440 | tf_op jit(solution)/shard_map/ppermute | solution.py:34
  65.6 1.5 %collective-permute-start.18 = (bf16[128,1024]{1,0:T(8,128)(2,1)S(1)}, bf16[128,1024]{1,0:T(8,128)(2,1)S(1)}, u32[]{:S(2)}, u32[]{:S(2)}) collective-permute-start(bf16[128,1024]{1,0:T(8,128)(2,1)S(1)} %collective-permute-done.17.refs_0_), channel_id=1, source_target_pairs={{0,1},{1,0},{2,3},{3,2},{4,5},{5,4},{6,7},{7,6},{8,9},{9,8},{10,11... | collective-permute-start | bytes 786440 | tf_op jit(solution)/shard_map/ppermute | solution.py:34
  70.8 1.5 %collective-permute-start.20 = (bf16[128,1024]{1,0:T(8,128)(2,1)S(1)}, bf16[128,1024]{1,0:T(8,128)(2,1)S(1)}, u32[]{:S(2)}, u32[]{:S(2)}) collective-permute-start(bf16[128,1024]{1,0:T(8,128)(2,1)S(1)} %collective-permute-done.16.own_rows), channel_id=1, source_target_pairs={{0,1},{1,0},{2,3},{3,2},{4,5},{5,4},{6,7},{7,6},{8,9},{9,8},{10,11... | collective-permute-start | bytes 786440 | tf_op jit(solution)/shard_map/ppermute | solution.py:34
  74.2 1.7 %collective-permute-start.21 = (bf16[128,1024]{1,0:T(8,128)(2,1)S(1)}, bf16[128,1024]{1,0:T(8,128)(2,1)S(1)}, u32[]{:S(2)}, u32[]{:S(2)}) collective-permute-start(bf16[128,1024]{1,0:T(8,128)(2,1)S(1)} %get-tuple-element.78), channel_id=1, source_target_pairs={{0,1},{1,0},{2,3},{3,2},{4,5},{5,4},{6,7},{7,6},{8,9},{9,8},{10,11... | collective-permute-start | bytes 786440 | tf_op jit(solution)/shard_map/ppermute | solution.py:34
  75.4 3.1 %collective-permute-start.25 = (bf16[128,1024]{1,0:T(8,128)(2,1)S(1)}, bf16[128,1024]{1,0:T(8,128)(2,1)S(1)}, u32[]{:S(2)}, u32[]{:S(2)}) collective-permute-start(bf16[128,1024]{1,0:T(8,128)(2,1)S(1)} %get-tuple-element.94), channel_id=1, source_target_pairs={{0,1},{1,0},{2,3},{3,2},{4,5},{5,4},{6,7},{7,6},{8,9},{9,8},{10,11... | collective-permute-start | bytes 786440 | tf_op jit(solution)/shard_map/ppermute | solution.py:34
  76.0 9.2 %collective-permute-start.23 = (bf16[128,1024]{1,0:T(8,128)(2,1)S(1)}, bf16[128,1024]{1,0:T(8,128)(2,1)S(1)}, u32[]{:S(2)}, u32[]{:S(2)}) collective-permute-start(bf16[128,1024]{1,0:T(8,128)(2,1)S(1)} %convert_add_fusion.2), channel_id=1, source_target_pairs={{0,2},{1,3},{2,0},{3,1},{4,6},{5,7},{6,4},{7,5},{8,10},{9,11},{10,... | collective-permute-start | bytes 786440 | tf_op jit(solution)/shard_map/ppermute | solution.py:34
  77.4 7.8 %collective-permute-start.22 = (bf16[128,1024]{1,0:T(8,128)(2,1)S(1)}, bf16[128,1024]{1,0:T(8,128)(2,1)S(1)}, u32[]{:S(2)}, u32[]{:S(2)}) collective-permute-start(bf16[128,1024]{1,0:T(8,128)(2,1)S(1)} %get-tuple-element.85), channel_id=1, source_target_pairs={{0,1},{1,0},{2,3},{3,2},{4,5},{5,4},{6,7},{7,6},{8,9},{9,8},{10,11... | collective-permute-start | bytes 786440 | tf_op jit(solution)/shard_map/ppermute | solution.py:34
  78.6 14.6 %collective-permute-start.26 = (bf16[128,1024]{1,0:T(8,128)(2,1)S(1)}, bf16[128,1024]{1,0:T(8,128)(2,1)S(1)}, u32[]{:S(2)}, u32[]{:S(2)}) collective-permute-start(bf16[128,1024]{1,0:T(8,128)(2,1)S(1)} %add_convert_fusion), channel_id=1, source_target_pairs={{0,2},{1,3},{2,0},{3,1},{4,6},{5,7},{6,4},{7,5},{8,10},{9,11},{10,... | collective-permute-start | bytes 786440 | tf_op jit(solution)/shard_map/ppermute | solution.py:34
  85.3 10.7 %collective-permute-start.27 = (bf16[128,1024]{1,0:T(8,128)(2,1)S(1)}, bf16[128,1024]{1,0:T(8,128)(2,1)S(1)}, u32[]{:S(2)}, u32[]{:S(2)}) collective-permute-start(bf16[128,1024]{1,0:T(8,128)(2,1)S(1)} %convert_add_fusion.1), channel_id=1, source_target_pairs={{0,6},{1,7},{2,4},{3,5},{4,2},{5,3},{6,0},{7,1},{8,14},{9,15},{10,... | collective-permute-start | bytes 786440 | tf_op jit(solution)/shard_map/ppermute | solution.py:34
  93.1 2.9 %collective-permute-start.24 = (bf16[128,1024]{1,0:T(8,128)(2,1)S(1)}, bf16[128,1024]{1,0:T(8,128)(2,1)S(1)}, u32[]{:S(2)}, u32[]{:S(2)}) collective-permute-start(bf16[128,1024]{1,0:T(8,128)(2,1)S(1)} %get-tuple-element.91), channel_id=1, source_target_pairs={{0,1},{1,0},{2,3},{3,2},{4,5},{5,4},{6,7},{7,6},{8,9},{9,8},{10,11... | collective-permute-start | bytes 786440 | tf_op jit(solution)/shard_map/ppermute | solution.py:34
